TPU v7x, 512 devices: a whole 4x8x8 slice. The times are simulated.
512 devices in a mesh: grp: 2 (over y_lo), slab: 64 (over y_hi, z, core), col: 4 (over x).
Axes of the slice: x: 4, y: 8 (y_hi: 4, y_lo: 2; y = y_hi * 2 + y_lo), z: 8, core: 2. Of those that a mesh axis runs over, the one named last changes fastest.
Arguments:
- heat_field: float32 [2, 32, 1024, 512], P('grp', None, 'slab', 'col'), may hold values from -6 to 6
- coeff: float32 [2, 32, 1024, 512], P('grp', None, 'slab', 'col'), may hold values from 0.2 to 1
- order: float32 [2, 2, 32, 1024, 512], P('grp', None, None, 'slab', 'col'), may hold values from 0.5 to 1
- block_owner: int32 [4, 64, 64, 1], P('col'), may hold values from 0 to 63; in each aligned block of 64 rows (0 to 63, 64 to 127, ..., all dimensions but the last counted through in order) at most 2 rows name the same one
- block_source: int32 [4, 64, 64], P('col'), may hold values from 0 to 255
- laser_cells: int32 [64, 4, 32], P('slab', 'col'), may hold values from 0 to 2047
Outputs:
- ending_warmth_pair: float32 [2, 32, 1024, 512], P('grp', None, 'slab', 'col')
- joined_solver_outputs: float32 [2, 2, 32, 1024, 512], P('grp', None, None, 'slab', 'col')
Inputs may be any that keep to these rules, and one draw needn't show every extreme that they name: `block_owner`: within the 64 units of one window device no owner slab is named more than 2 times; some window device names one owner exactly 2 times in every draw. `block_source`: several window units may read the same plate unit. `laser_cells`: A cell may repeat; each entry adds its heat.
All inputs are finite; a program needn't handle non-finite values.
Results may differ from a plain program's by a relative error of at most 0.0003.
Values sent between devices are 32-bit elements; how exact they have to be, the bound alone decides.
No kernel may reach another device: no remote copies, remote signals or barrier semaphores. Data moves between devices by JAX's collectives and lax.ppermute only.
A program may use at most 64 MiB of HBM per device.

v0:
```python
import jax
import jax.numpy as jnp
from jax import lax
from jax.sharding import PartitionSpec as P

PZ = 32
ZQ = 4
CX = 16
CY = 128


heat_dt = 0.07
phase_dt = 0.1
laser_power = 3.0
liquefying_threshold = 0.3
freezing_line_gradient = 0.5
solute_reject = 0.5
STENCIL_SHIFTS = ((0, 1, 1), (2, 1, 1), (1, 0, 1), (1, 2, 1), (1, 1, 0), (1, 1, 2))
PHASE_WEIGHTS = (1.0, 1.0, 1.3, 1.3, 0.7, 0.7)
SOLUTE_WEIGHTS = (0.8, 0.8, 0.8, 0.8, 0.8, 0.8)


def swapped(shard, axis, apart):
    return lax.ppermute(shard, axis, [(i, i ^ 1 << apart) for i in range(lax.axis_size(axis))])


def padded_2(shard, sides, width):
    for axis, dim in sides:
        size, length = (lax.axis_size(axis), shard.shape[dim])
        up = [(i, (i + 1) % size) for i in range(size - 1)]
        down = [(j, i) for i, j in up]
        last = lax.slice_in_dim(shard, length - width, length, axis=dim)
        first = lax.slice_in_dim(shard, 0, width, axis=dim)
        before = lax.ppermute(last, axis, up)
        after = lax.ppermute(first, axis, down)
        shard = jnp.concatenate([before, shard, after], axis=dim)
    return shard


def harmonic(center, beside):
    return 2.0 * center * beside / (center + beside)


def conduction(temp_pad, cond_pad):
    vertical_cell_count = temp_pad.shape[0] - 2
    row_count = temp_pad.shape[1] - 2
    col_count = temp_pad.shape[2] - 2
    center = temp_pad[1:-1, 1:-1, 1:-1]
    cond_mid = cond_pad[1:-1, 1:-1, 1:-1]
    summed = jnp.zeros_like(center)
    for along_z, along_x, along_y in STENCIL_SHIFTS:
        neighbour = temp_pad[
            along_z : along_z + vertical_cell_count,
            along_x : along_x + row_count,
            along_y : along_y + col_count,
        ]
        cond_next = cond_pad[
            along_z : along_z + vertical_cell_count,
            along_x : along_x + row_count,
            along_y : along_y + col_count,
        ]
        summed = summed + harmonic(cond_mid, cond_next) * (neighbour - center)
    return summed


def anisotropic(field_pad, weights):
    vertical_cell_count = field_pad.shape[0] - 2
    row_count = field_pad.shape[1] - 2
    col_count = field_pad.shape[2] - 2
    center = field_pad[1:-1, 1:-1, 1:-1]
    summed = jnp.zeros_like(center)
    for (along_z, along_x, along_y), weight in zip(STENCIL_SHIFTS, weights):
        neighbour = field_pad[
            along_z : along_z + vertical_cell_count,
            along_x : along_x + row_count,
            along_y : along_y + col_count,
        ]
        summed = summed + weight * (neighbour - center)
    return summed


def heat_step(temp_pad, cond_pad, temp, source, thermal_heat_capacity, loss):
    return temp + heat_dt * (
        (conduction(temp_pad, cond_pad) + source) / thermal_heat_capacity - loss * temp
    )


def order_variable_update(
    bordered_order_variable, bordered_concentration, patch_warmth, response_measure
):
    order_variable = bordered_order_variable[1:-1, 1:-1, 1:-1]
    dissolved_concentration = bordered_concentration[1:-1, 1:-1, 1:-1]
    forcing_term = 0.45 * jnp.tanh(
        response_measure
        * (liquefying_threshold - patch_warmth - freezing_line_gradient * dissolved_concentration)
    )
    updated_order_variable = order_variable + phase_dt * (
        anisotropic(bordered_order_variable, PHASE_WEIGHTS)
        + 4.0 * order_variable * (1.0 - order_variable) * (order_variable - 0.5 + forcing_term)
    )
    updated_concentration = (
        dissolved_concentration
        + phase_dt * anisotropic(bordered_concentration, SOLUTE_WEIGHTS)
        - solute_reject * (updated_order_variable - order_variable) * dissolved_concentration
    )
    return (updated_order_variable, updated_concentration)


def refine_table(half_cols):
    source = jnp.arange(half_cols)[:, None]
    target = jnp.arange(2 * half_cols)[None, :]
    parent = target // 2
    parity = target % 2
    beside = jnp.clip(parent - 1 + 2 * parity, 0, half_cols - 1)
    return 0.75 * (source == parent).astype(jnp.float32) + 0.25 * (source == beside).astype(
        jnp.float32
    )


def upsample_finer(coarse):
    table = refine_table(coarse.shape[-1])
    finer = jnp.dot(
        coarse, table, precision=lax.Precision.HIGHEST, preferred_element_type=jnp.float32
    )
    return jnp.broadcast_to(finer[..., None, :], finer.shape[:-1] + (2, finer.shape[-1]))


def coarsen(fine):
    split = fine.reshape(fine.shape[:-1] + (fine.shape[-1] // 2, 2))
    return 0.25 * jnp.sum(split, axis=(-3, -1))


def plate_cut(block):
    return (
        block.reshape(PZ // ZQ, ZQ, CX, 2, CY // 2)
        .transpose(0, 2, 3, 1, 4)
        .reshape(PZ // ZQ * CX * 2, ZQ, CY // 2)
    )


def plate_join(units):
    return units.reshape(PZ // ZQ, CX, 2, ZQ, CY // 2).transpose(0, 3, 1, 2, 4).reshape(PZ, CX, CY)


def window_cut(block):
    return (
        block.reshape(PZ // ZQ, ZQ, CX // 2, 2, CY)
        .transpose(0, 2, 1, 3, 4)
        .reshape(PZ // ZQ * (CX // 2), ZQ, 2, CY)
    )


def patch_assembly(units):
    return units.reshape(PZ // ZQ, CX // 2, ZQ, 2, CY).transpose(0, 2, 1, 3, 4).reshape(PZ, CX, CY)


def margin_thickness(field):
    return jnp.pad(field, ((1, 1), (0, 0), (0, 0)))


def per_device(heat_field, coeff, order, block_owner, block_source, laser_cells):
    slab_count = lax.axis_size("slab")
    my_slab = lax.axis_index("slab")
    patch_side_extent = lax.axis_index("grp") == 1
    local_heat = heat_field[0]
    pointwise_factor = coeff[0]
    slot_first = order[0, 0]
    slot_second = order[0, 1]
    units_wide = PZ // ZQ * (CX // 2)
    plate_count = PZ // ZQ * CX * 2
    capacity = max(2, 2 * units_wide // slab_count)
    owners = block_owner[0, :, :, 0]
    sources = block_source[0]
    hits = (owners[:, :, None] == jnp.arange(slab_count)[None, None, :]).astype(jnp.int32)
    ranks = jnp.sum(jnp.cumsum(hits, axis=1) * hits, axis=2) - 1
    slot_ids = jnp.arange(capacity)
    chosen = (owners == my_slab)[:, None, :] & (ranks[:, None, :] == slot_ids[None, :, None])
    plate_valid = jnp.any(chosen, axis=2)
    plate_pick = jnp.sum(jnp.where(chosen, sources[:, None, :], 0), axis=2)
    own_owner = owners[my_slab]
    own_rank = ranks[my_slab]
    wanted = (own_owner[None, None, :] == jnp.arange(slab_count)[:, None, None]) & (
        own_rank[None, None, :] == slot_ids[None, :, None]
    )
    window_valid = jnp.any(wanted, axis=2)
    window_pick = jnp.sum(jnp.where(wanted, jnp.arange(units_wide)[None, None, :], 0), axis=2)
    plate_units = plate_cut(local_heat)[plate_pick] * plate_valid[:, :, None, None].astype(
        jnp.float32
    )
    latent_fine = window_cut(local_heat)[window_pick] * window_valid[:, :, None, None, None].astype(
        jnp.float32
    )
    outbox = jnp.where(patch_side_extent, latent_fine, upsample_finer(plate_units)).reshape(
        slab_count, capacity, -1
    )
    moved = swapped(outbox, "grp", 0)
    inbox = lax.all_to_all(moved, "slab", split_axis=0, concat_axis=0, tiled=True)
    flat_rows = inbox.reshape(slab_count * capacity, -1)
    needed = flat_rows[own_owner * capacity + own_rank]
    patch_subdomains = needed.reshape(units_wide, ZQ, 2, CY)
    arriving = coarsen(inbox.reshape(slab_count, capacity, ZQ, 2, CY))
    patch_warmth = patch_assembly(patch_subdomains)
    arriving = arriving * plate_valid[:, :, None, None].astype(jnp.float32)
    plate_total = (
        jnp.zeros((plate_count, ZQ, CY // 2), jnp.float32)
        .at[plate_pick.reshape(-1)]
        .add(arriving.reshape(-1, ZQ, CY // 2))
    )
    latent_heat = plate_join(plate_total)
    deposit = (
        jnp.zeros((CX * CY,), jnp.float32).at[laser_cells[0, 0]].add(laser_power).reshape(CX, CY)
    )
    laser_field = jnp.concatenate([deposit[None], jnp.zeros((PZ - 1, CX, CY), jnp.float32)], 0)
    source = laser_field + latent_heat
    padded = padded_2(jnp.stack([local_heat, pointwise_factor]), (("slab", 2), ("col", 3)), 1)
    bordered_order_variable = padded_2(
        jnp.stack([slot_first, slot_second]), (("slab", 2), ("col", 3)), 1
    )
    cond_pad = margin_thickness(padded[1])
    first = heat_step(
        margin_thickness(padded[0]), cond_pad, local_heat, source, slot_first, slot_second
    )
    again = padded_2(first, (("slab", 1), ("col", 2)), 1)
    second_partial_update = heat_step(
        margin_thickness(again), cond_pad, first, source, slot_first, slot_second
    )
    updated_order_variable, updated_concentration = order_variable_update(
        margin_thickness(bordered_order_variable[0]),
        margin_thickness(bordered_order_variable[1]),
        patch_warmth,
        pointwise_factor,
    )
    ending_warmth_pair = jnp.where(patch_side_extent, patch_warmth, second_partial_update)[None]
    joined_solver_outputs = jnp.where(
        patch_side_extent,
        jnp.stack([updated_order_variable, updated_concentration]),
        jnp.stack([latent_heat, first]),
    )[None]
    return (ending_warmth_pair, joined_solver_outputs)


def solution(mesh):
    placed = (
        P("grp", None, "slab", "col"),
        P("grp", None, "slab", "col"),
        P("grp", None, None, "slab", "col"),
        P("col", None, None, None),
        P("col", None, None),
        P("slab", "col", None),
    )
    return jax.shard_map(
        per_device,
        mesh=mesh,
        in_specs=placed,
        out_specs=(P("grp", None, "slab", "col"), P("grp", None, None, "slab", "col")),
        check_vma=False,
    )
```

profile of v0, /device:TPU:58, one launch (start us, length us, event | category | flops | bytes accessed | tf_op | source)
XLA Modules:
  0.0 138.0 jit_solution(15808063341872967717)
XLA Ops:
  0.6 0.8 copy.96
  1.5 2.3 %select_reduce_fusion = s32[64,64]{0,1:T(8,128)S(1)} fusion(s32[64,64]{0,1:T(8,128)S(1)} %copy.96), kind=kOutput, calls=%fused_computation.5 | output fusion | flops 17821696 | bytes 32768 | tf_op jit(solution)/shard_map/jit(cumsum)/reduce_window_sum | solution.py:175
  3.8 0.8 broadcast_compare_fusion
  4.8 0.7 fusion.89
  5.7 1.3 reshape_squeeze.7
  7.0 0.3 copy.104
  8.1 0.7 gather_fusion.1
  9.2 0.4 fusion.67
  9.7 0.2 broadcast_in_dim.40
  9.9 0.6 broadcast_in_dim.41
  10.8 0.9 gather_fusion
  11.6 0.3 copy.99
  11.9 0.6 gather.12
  12.7 0.3 multiply_select_fusion
  13.0 3.3 %collective-permute-start = (f32[64,2,1024]{2,1,0:T(2,128)S(1)}, f32[64,2,1024]{2,1,0:T(2,128)}, u32[]{:S(2)}, u32[]{:S(2)}) collective-permute-start(f32[64,2,1024]{2,1,0:T(2,128)S(1)} %multiply_select_fusion), channel_id=1, source_target_pairs={{0,256},{256,0},{1,257},{257,1},{2,258},{258,2},{3,259},{259,3},{4... | collective-permute-start | bytes 1572872 | tf_op jit(solution)/shard_map/ppermute | solution.py:24
  16.4 11.7 %collective-permute-start.2 = (f32[2,32,1,128]{3,2,1,0:T(1,128)S(1)}, f32[2,32,1,128]{3,2,1,0:T(1,128)S(1)}, u32[]{:S(2)}, u32[]{:S(2)}) collective-permute-start(f32[2,32,1,128]{3,2,1,0:T(1,128)S(1)} %get-tuple-element.17), channel_id=1, source_target_pairs={{4,0},{8,4},{12,8},{16,12},{20,16},{24,20},{28,24},{32,28},{36,32}... | collective-permute-start | bytes 98312 | tf_op jit(solution)/shard_map/ppermute | solution.py:35
  28.1 1.9 %collective-permute-start.1 = (f32[2,32,1,128]{3,2,1,0:T(1,128)S(1)}, f32[2,32,1,128]{3,2,1,0:T(1,128)S(1)}, u32[]{:S(2)}, u32[]{:S(2)}) collective-permute-start(f32[2,32,1,128]{3,2,1,0:T(1,128)S(1)} %get-tuple-element.16), channel_id=1, source_target_pairs={{0,4},{4,8},{8,12},{12,16},{16,20},{20,24},{24,28},{28,32},{32,36}... | collective-permute-start | bytes 98312 | tf_op jit(solution)/shard_map/ppermute | solution.py:34
  30.1 6.7 %collective-permute-start.10 = (f32[2,32,1,128]{3,2,1,0:T(1,128)S(1)}, f32[2,32,1,128]{3,2,1,0:T(1,128)S(1)}, u32[]{:S(2)}, u32[]{:S(2)}) collective-permute-start(f32[2,32,1,128]{3,2,1,0:T(1,128)S(1)} %get-tuple-element.13), channel_id=1, source_target_pairs={{4,0},{8,4},{12,8},{16,12},{20,16},{24,20},{28,24},{32,28},{36,32}... | collective-permute-start | bytes 98312 | tf_op jit(solution)/shard_map/ppermute | solution.py:35
  36.8 1.9 %collective-permute-start.9 = (f32[2,32,1,128]{3,2,1,0:T(1,128)S(1)}, f32[2,32,1,128]{3,2,1,0:T(1,128)S(1)}, u32[]{:S(2)}, u32[]{:S(2)}) collective-permute-start(f32[2,32,1,128]{3,2,1,0:T(1,128)S(1)} %get-tuple-element.12), channel_id=1, source_target_pairs={{0,4},{4,8},{8,12},{12,16},{16,20},{20,24},{24,28},{28,32},{32,36}... | collective-permute-start | bytes 98312 | tf_op jit(solution)/shard_map/ppermute | solution.py:34
  38.7 0.7 fusion.86
  39.6 0.6 fusion.88
  40.2 0.5 fusion.87
  40.9 0.3 fusion.95
  41.1 0.9 copy.111
  42.0 2.4 %collective-permute-start.4 = (f32[2,32,18,1]{1,0,3,2:T(2,128)}, f32[2,32,18,1]{1,0,3,2:T(2,128)}, u32[]{:S(2)}, u32[]{:S(2)}) collective-permute-start(f32[2,32,18,1]{1,0,3,2:T(2,128)} %copy.111), channel_id=1, source_target_pairs={{1,0},{2,1},{3,2},{5,4},{6,5},{7,6},{9,8},{10,9},{11,10},{13,12},{... | collective-permute-start | bytes 13832 | tf_op jit(solution)/shard_map/ppermute | solution.py:35
  44.5 0.9 copy.110
  45.4 3.4 %collective-permute-start.3 = (f32[2,32,18,1]{1,0,3,2:T(2,128)}, f32[2,32,18,1]{1,0,3,2:T(2,128)}, u32[]{:S(2)}, u32[]{:S(2)}) collective-permute-start(f32[2,32,18,1]{1,0,3,2:T(2,128)} %copy.110), channel_id=1, source_target_pairs={{0,1},{1,2},{2,3},{4,5},{5,6},{6,7},{8,9},{9,10},{10,11},{12,13},{... | collective-permute-start | bytes 13832 | tf_op jit(solution)/shard_map/ppermute | solution.py:34
  48.9 9.8 %all-to-all-start = ((f32[64,2,1024]{2,1,0:T(2,128)}), f32[64,2,1024]{2,1,0:T(2,128)S(1)}, u32[]{:S(2)}, u32[]{:S(2)}) async-start(f32[64,2,1024]{2,1,0:T(2,128)} %collective-permute-done), calls=%async_computation | async-start | bytes 1048576 | tf_op jit(solution)/shard_map/all_to_all | solution.py:197
  58.8 1.1 fusion.94
  59.9 1.4 %copy.122 = f32[2,32,18,1]{1,0,3,2:T(2,128)S(1)} copy(f32[2,32,18,1]{3,2,1,0:T(8,128)} %get-tuple-element.9) | data formatting | bytes 9216 | tf_op jit(solution)/shard_map/slice | solution.py:33
  61.3 3.0 %collective-permute-start.12 = (f32[2,32,18,1]{1,0,3,2:T(2,128)S(1)}, f32[2,32,18,1]{1,0,3,2:T(2,128)S(1)}, u32[]{:S(2)}, u32[]{:S(2)}) collective-permute-start(f32[2,32,18,1]{1,0,3,2:T(2,128)S(1)} %copy.122), channel_id=1, source_target_pairs={{1,0},{2,1},{3,2},{5,4},{6,5},{7,6},{9,8},{10,9},{11,10},{13,12},{... | collective-permute-start | bytes 13832 | tf_op jit(solution)/shard_map/ppermute | solution.py:35
  64.4 0.3 copy.121
  64.7 2.9 %collective-permute-start.11 = (f32[2,32,18,1]{1,0,3,2:T(2,128)S(1)}, f32[2,32,18,1]{1,0,3,2:T(2,128)S(1)}, u32[]{:S(2)}, u32[]{:S(2)}) collective-permute-start(f32[2,32,18,1]{1,0,3,2:T(2,128)S(1)} %copy.121), channel_id=1, source_target_pairs={{0,1},{1,2},{2,3},{4,5},{5,6},{6,7},{8,9},{9,10},{10,11},{12,13},{... | collective-permute-start | bytes 13832 | tf_op jit(solution)/shard_map/ppermute | solution.py:34
  67.8 1.0 scatter_custom_fusion
  68.9 2.0 %copy.113 = f32[2,32,18,1]{3,2,1,0:T(8,128)} copy(f32[2,32,18,1]{1,0,3,2:T(2,128)} %collective-permute-done.4) | data formatting | bytes 9216 | tf_op jit(solution)/shard_map/ppermute | solution.py:35
  70.9 2.0 %copy.112 = f32[2,32,18,1]{3,2,1,0:T(8,128)} copy(f32[2,32,18,1]{1,0,3,2:T(2,128)} %collective-permute-done.3) | data formatting | bytes 9216 | tf_op jit(solution)/shard_map/ppermute | solution.py:34
  72.9 1.2 copy.124
  74.1 1.2 copy.123
  75.3 2.4 %pad_maximum_fusion = f32[2,32,18,130]{3,2,1,0:T(8,128)S(1)} fusion(f32[2,32,18,1]{3,2,1,0:T(8,128)} %copy.113, f32[2,32,1,128]{3,2,1,0:T(1,128)S(1)} %collective-permute-done.2, f32[2,32,16,128]{3,2,1,0:T(8,128)S(1)} %constant_dynamic-update-slice_fusion, f32[2,32,1,128]{3,2,1,0:T(1,128)S(1)} %collective-permute-done.1, f32[2,32,18,1]{3,2,1,0:T(8,128)} %copy.112), kind=kLoop, calls=%fused_computation.9 | loop fusion | flops 599040 | bytes 1198080 | tf_op jit(solution)/shard_map/concatenate | solution.py:36
  77.8 1.0 pad_maximum_fusion.1
  78.8 1.1 slice_bitcast_fusion.3
  80.0 0.4 reshape.342
  80.3 1.4 gather_fusion.2
  81.7 1.8 %copy.109 = f32[8,4,8,2,128]{4,3,2,1,0:T(2,128)} copy(f32[8,4,8,2,128]{4,2,3,1,0:T(8,128)} %bitcast.114) | data formatting | bytes 524288 | tf_op jit(solution)/shard_map/transpose | solution.py:154
  83.5 1.3 copy.115
  84.9 2.1 %reduce_sum.47 = f32[64,2,4,64]{0,3,2,1:T(8,128)S(1)} reduce(f32[64,2,4,2,64,2]{0,5,4,3,2,1:T(2,128)} %bitcast.108, f32[]{:T(128)} %constant.50.clone.1), dimensions={3,5}, to_apply=%region_7.8 | reduce | flops 98304 | bytes 655364 | tf_op jit(solution)/shard_map/reduce_sum | solution.py:130
  87.4 0.9 broadcast_in_dim.71
  88.3 15.1 %scatter_fusion = f32[256,4,64]{2,1,0:T(4,128)} fusion(f32[256,4,64]{2,1,0:T(4,128)} %broadcast_in_dim.71, s32[128]{0:T(128)S(1)} %copy-done.15, f32[128,4,64]{2,1,0:T(4,128)S(1)} %copy.118), kind=kCustom, calls=%fused_computation.4 | custom fusion | flops 32768 | bytes 393728 | tf_op jit(solution)/shard_map/scatter-add | solution.py:207
  103.3 1.1 copy.119
  104.5 0.8 copy.120
  105.3 2.0 %reshape.346 = f32[32,16,128]{2,1,0:T(8,128)} reshape(f32[8,4,16,2,64]{4,3,2,1,0:T(2,128)} %copy.120) | data formatting | bytes 524288 | tf_op jit(solution)/shard_map/reshape | solution.py:142
  107.4 2.1 %bitcast_add_fusion = f32[32,16,128]{2,1,0:T(8,128)S(1)} fusion(f32[1,32,16,128]{3,2,1,0:T(8,128)} %param.6, f32[32,18,130]{2,1,0:T(8,128)S(1)} %copy-done, f32[1,2,32,16,128]{4,3,2,1,0:T(8,128)} %param.8, f32[32,16,128]{2,1,0:T(8,128)} %reshape.346, f32[1,16,128]{2,1,0:T(8,128)S(1)} %bitcast.121, f32[32,18,130]{2,1,0:T(8,128)S(1)} %get-tuple-element.6), kind=kLoop, calls=%fused_computation.124 | loop fusion | flops 2818048 | bytes 5513216 | tf_op jit(solution)/shard_map/add | solution.py:83
  109.6 5.5 %collective-permute-start.6 = (f32[32,1,128]{2,1,0:T(1,128)S(1)}, f32[32,1,128]{2,1,0:T(1,128)S(1)}, u32[]{:S(2)}, u32[]{:S(2)}) collective-permute-start(f32[32,1,128]{2,1,0:T(1,128)S(1)} %get-tuple-element.21), channel_id=1, source_target_pairs={{4,0},{8,4},{12,8},{16,12},{20,16},{24,20},{28,24},{32,28},{36,32}... | collective-permute-start | bytes 49160 | tf_op jit(solution)/shard_map/ppermute | solution.py:35
  115.1 1.9 %collective-permute-start.5 = (f32[32,1,128]{2,1,0:T(1,128)S(1)}, f32[32,1,128]{2,1,0:T(1,128)S(1)}, u32[]{:S(2)}, u32[]{:S(2)}) collective-permute-start(f32[32,1,128]{2,1,0:T(1,128)S(1)} %get-tuple-element.20), channel_id=1, source_target_pairs={{0,4},{4,8},{8,12},{12,16},{16,20},{20,24},{24,28},{28,32},{32,36}... | collective-permute-start | bytes 49160 | tf_op jit(solution)/shard_map/ppermute | solution.py:34
  117.0 1.6 %fusion.35 = (f32[1,1,32,16,128]{4,3,2,1,0:T(8,128)S(1)}, f32[32,16,128]{2,1,0:T(8,128)}) fusion(f32[32,18,130]{2,1,0:T(8,128)S(1)} %get-tuple-element.5, f32[32,18,130]{2,1,0:T(8,128)S(1)} %get-tuple-element.4, f32[32,16,128]{2,1,0:T(8,128)S(1)} %bitcast.110, f32[1,32,16,128]{3,2,1,0:T(8,128)S(1)} %copy-done.11), kind=kLoop, calls=%fused_computation.67 | loop fusion | flops 3014656 | bytes 5242880 | tf_op jit(solution)/shard_map/stack | solution.py:236
  118.6 1.0 stack.28
  119.6 3.5 %collective-permute-done.5 = f32[32,1,128]{2,1,0:T(1,128)S(1)} collective-permute-done((f32[32,1,128]{2,1,0:T(1,128)S(1)}, f32[32,1,128]{2,1,0:T(1,128)S(1)}, u32[]{:S(2)}, u32[]{:S(2)}) %collective-permute-start.5) | collective-permute-done | bytes 16416 | tf_op jit(solution)/shard_map/ppermute | solution.py:34
  123.4 2.7 %collective-permute-start.8 = (f32[32,18,1]{2,1,0:T(8,128)S(1)}, f32[32,18,1]{2,1,0:T(8,128)S(1)}, u32[]{:S(2)}, u32[]{:S(2)}) collective-permute-start(f32[32,18,1]{2,1,0:T(8,128)S(1)} %get-tuple-element.19), channel_id=1, source_target_pairs={{1,0},{2,1},{3,2},{5,4},{6,5},{7,6},{9,8},{10,9},{11,10},{13,12},{... | collective-permute-start | bytes 6920 | tf_op jit(solution)/shard_map/ppermute | solution.py:35
  126.0 3.2 %collective-permute-start.7 = (f32[32,18,1]{2,1,0:T(8,128)S(1)}, f32[32,18,1]{2,1,0:T(8,128)S(1)}, u32[]{:S(2)}, u32[]{:S(2)}) collective-permute-start(f32[32,18,1]{2,1,0:T(8,128)S(1)} %get-tuple-element.18), channel_id=1, source_target_pairs={{0,1},{1,2},{2,3},{4,5},{5,6},{6,7},{8,9},{9,10},{10,11},{12,13},{... | collective-permute-start | bytes 6920 | tf_op jit(solution)/shard_map/ppermute | solution.py:34
  129.3 0.9 maximum_select_fusion
  130.1 2.9 %collective-permute-done.8 = f32[32,18,1]{2,1,0:T(8,128)S(1)} collective-permute-done((f32[32,18,1]{2,1,0:T(8,128)S(1)}, f32[32,18,1]{2,1,0:T(8,128)S(1)}, u32[]{:S(2)}, u32[]{:S(2)}) %collective-permute-start.8) | collective-permute-done | bytes 2336 | tf_op jit(solution)/shard_map/ppermute | solution.py:35
  133.0 2.7 %collective-permute-done.7 = f32[32,18,1]{2,1,0:T(8,128)S(1)} collective-permute-done((f32[32,18,1]{2,1,0:T(8,128)S(1)}, f32[32,18,1]{2,1,0:T(8,128)S(1)}, u32[]{:S(2)}, u32[]{:S(2)}) %collective-permute-start.7) | collective-permute-done | bytes 2336 | tf_op jit(solution)/shard_map/ppermute | solution.py:34
  135.7 0.5 select_maximum_fusion
  136.3 1.7 %select_bitcast_fusion = f32[1,32,16,128]{3,2,1,0:T(8,128)} fusion(f32[32,16,128]{2,1,0:T(8,128)S(1)} %bitcast.111, f32[32,16,128]{2,1,0:T(8,128)S(1)} %bitcast_add_fusion, f32[32,18,1]{2,1,0:T(8,128)S(1)} %collective-permute-done.8, f32[32,1,128]{2,1,0:T(1,128)S(1)} %collective-permute-done.6, f32[32,1,128]{2,1,0:T(1,128)S(1)} %collective-permute-done.5, ...), kind=kLoop, calls=%fused_computation.128 | loop fusion | flops 3407872 | bytes 5021697 | tf_op jit(solution)/shard_map/broadcast_in_dim | solution.py:233
  (93 shorter events, 3.8 us)
Async XLA Ops:
  3.7 3.8 %copy-start.14 = (s32[1,64,64]{2,1,0:T(8,128)S(1)}, s32[1,64,64]{2,1,0:T(8,128)}, u32[]{:S(2)}) copy-start(s32[1,64,64]{2,1,0:T(8,128)} %param.10) | copy-start | bytes 49156
  9.2 1.4 copy-start.4
  11.9 4.4 %copy-start.10 = (f32[1,32,16,128]{3,2,1,0:T(8,128)S(1)}, f32[1,32,16,128]{3,2,1,0:T(8,128)}, u32[]{:S(2)}) copy-start(f32[1,32,16,128]{3,2,1,0:T(8,128)} %param.7) | copy-start | bytes 786436
  12.5 17.5 %copy-start.2 = (f32[1,2,32,16,128]{4,3,2,1,0:T(8,128)S(1)}, f32[1,2,32,16,128]{4,3,2,1,0:T(8,128)}, u32[]{:S(2)}) copy-start(f32[1,2,32,16,128]{4,3,2,1,0:T(8,128)} %param.8) | copy-start | bytes 1572868
  13.0 27.2 %copy-start.16 = (s32[1,1,32]{2,1,0:T(1,128)S(1)}, s32[1,1,32]{2,1,0:T(1,128)}, u32[]{:S(2)}) copy-start(s32[1,1,32]{2,1,0:T(1,128)} %param.11) | copy-start | bytes 388
  13.0 35.9 %collective-permute-start = (f32[64,2,1024]{2,1,0:T(2,128)S(1)}, f32[64,2,1024]{2,1,0:T(2,128)}, u32[]{:S(2)}, u32[]{:S(2)}) collective-permute-start(f32[64,2,1024]{2,1,0:T(2,128)S(1)} %multiply_select_fusion), channel_id=1, source_target_pairs={{0,256},{256,0},{1,257},{257,1},{2,258},{258,2},{3,259},{259,3},{4... | collective-permute-start | bytes 1572872 | tf_op jit(solution)/shard_map/ppermute | solution.py:24
  16.4 24.3 %collective-permute-start.2 = (f32[2,32,1,128]{3,2,1,0:T(1,128)S(1)}, f32[2,32,1,128]{3,2,1,0:T(1,128)S(1)}, u32[]{:S(2)}, u32[]{:S(2)}) collective-permute-start(f32[2,32,1,128]{3,2,1,0:T(1,128)S(1)} %get-tuple-element.17), channel_id=1, source_target_pairs={{4,0},{8,4},{12,8},{16,12},{20,16},{24,20},{28,24},{32,28},{36,32}... | collective-permute-start | bytes 98312 | tf_op jit(solution)/shard_map/ppermute | solution.py:35
  28.1 12.6 %collective-permute-start.1 = (f32[2,32,1,128]{3,2,1,0:T(1,128)S(1)}, f32[2,32,1,128]{3,2,1,0:T(1,128)S(1)}, u32[]{:S(2)}, u32[]{:S(2)}) collective-permute-start(f32[2,32,1,128]{3,2,1,0:T(1,128)S(1)} %get-tuple-element.16), channel_id=1, source_target_pairs={{0,4},{4,8},{8,12},{12,16},{16,20},{20,24},{24,28},{28,32},{32,36}... | collective-permute-start | bytes 98312 | tf_op jit(solution)/shard_map/ppermute | solution.py:34
  30.1 18.7 %collective-permute-start.10 = (f32[2,32,1,128]{3,2,1,0:T(1,128)S(1)}, f32[2,32,1,128]{3,2,1,0:T(1,128)S(1)}, u32[]{:S(2)}, u32[]{:S(2)}) collective-permute-start(f32[2,32,1,128]{3,2,1,0:T(1,128)S(1)} %get-tuple-element.13), channel_id=1, source_target_pairs={{4,0},{8,4},{12,8},{16,12},{20,16},{24,20},{28,24},{32,28},{36,32}... | collective-permute-start | bytes 98312 | tf_op jit(solution)/shard_map/ppermute | solution.py:35
  36.8 12.0 %collective-permute-start.9 = (f32[2,32,1,128]{3,2,1,0:T(1,128)S(1)}, f32[2,32,1,128]{3,2,1,0:T(1,128)S(1)}, u32[]{:S(2)}, u32[]{:S(2)}) collective-permute-start(f32[2,32,1,128]{3,2,1,0:T(1,128)S(1)} %get-tuple-element.12), channel_id=1, source_target_pairs={{0,4},{4,8},{8,12},{12,16},{16,20},{20,24},{24,28},{28,32},{32,36}... | collective-permute-start | bytes 98312 | tf_op jit(solution)/shard_map/ppermute | solution.py:34
  42.0 26.8 %collective-permute-start.4 = (f32[2,32,18,1]{1,0,3,2:T(2,128)}, f32[2,32,18,1]{1,0,3,2:T(2,128)}, u32[]{:S(2)}, u32[]{:S(2)}) collective-permute-start(f32[2,32,18,1]{1,0,3,2:T(2,128)} %copy.111), channel_id=1, source_target_pairs={{1,0},{2,1},{3,2},{5,4},{6,5},{7,6},{9,8},{10,9},{11,10},{13,12},{... | collective-permute-start | bytes 13832 | tf_op jit(solution)/shard_map/ppermute | solution.py:35
  45.4 25.5 %collective-permute-start.3 = (f32[2,32,18,1]{1,0,3,2:T(2,128)}, f32[2,32,18,1]{1,0,3,2:T(2,128)}, u32[]{:S(2)}, u32[]{:S(2)}) collective-permute-start(f32[2,32,18,1]{1,0,3,2:T(2,128)} %copy.110), channel_id=1, source_target_pairs={{0,1},{1,2},{2,3},{4,5},{5,6},{6,7},{8,9},{9,10},{10,11},{12,13},{... | collective-permute-start | bytes 13832 | tf_op jit(solution)/shard_map/ppermute | solution.py:34
  48.9 31.0 %all-to-all-start = ((f32[64,2,1024]{2,1,0:T(2,128)}), f32[64,2,1024]{2,1,0:T(2,128)S(1)}, u32[]{:S(2)}, u32[]{:S(2)}) async-start(f32[64,2,1024]{2,1,0:T(2,128)} %collective-permute-done), calls=%async_computation | async-start | bytes 1048576 | tf_op jit(solution)/shard_map/all_to_all | solution.py:197
  61.3 11.5 %collective-permute-start.12 = (f32[2,32,18,1]{1,0,3,2:T(2,128)S(1)}, f32[2,32,18,1]{1,0,3,2:T(2,128)S(1)}, u32[]{:S(2)}, u32[]{:S(2)}) collective-permute-start(f32[2,32,18,1]{1,0,3,2:T(2,128)S(1)} %copy.122), channel_id=1, source_target_pairs={{1,0},{2,1},{3,2},{5,4},{6,5},{7,6},{9,8},{10,9},{11,10},{13,12},{... | collective-permute-start | bytes 13832 | tf_op jit(solution)/shard_map/ppermute | solution.py:35
  64.7 9.4 %collective-permute-start.11 = (f32[2,32,18,1]{1,0,3,2:T(2,128)S(1)}, f32[2,32,18,1]{1,0,3,2:T(2,128)S(1)}, u32[]{:S(2)}, u32[]{:S(2)}) collective-permute-start(f32[2,32,18,1]{1,0,3,2:T(2,128)S(1)} %copy.121), channel_id=1, source_target_pairs={{0,1},{1,2},{2,3},{4,5},{5,6},{6,7},{8,9},{9,10},{10,11},{12,13},{... | collective-permute-start | bytes 13832 | tf_op jit(solution)/shard_map/ppermute | solution.py:34
  75.3 2.5 %copy-start.5 = (f32[2,32,18,1]{3,2,1,0:T(8,128)S(1)}, f32[2,32,18,1]{3,2,1,0:T(8,128)}, u32[]{:S(2)}) copy-start(f32[2,32,18,1]{3,2,1,0:T(8,128)} %copy.124) | copy-start | bytes 13828
  75.3 2.5 %copy-start.6 = (f32[2,32,18,1]{3,2,1,0:T(8,128)S(1)}, f32[2,32,18,1]{3,2,1,0:T(8,128)}, u32[]{:S(2)}) copy-start(f32[2,32,18,1]{3,2,1,0:T(8,128)} %copy.123) | copy-start | bytes 13828
  84.8 3.4 %copy-start.15 = (s32[128]{0:T(128)S(1)}, s32[128]{0:T(128)}, u32[]{:S(2)}) copy-start(s32[128]{0:T(128)} %fusion.88) | copy-start | bytes 1540
  103.3 4.0 %copy-start = (f32[32,18,130]{2,1,0:T(8,128)S(1)}, f32[32,18,130]{2,1,0:T(8,128)}, u32[]{:S(2)}) copy-start(f32[32,18,130]{2,1,0:T(8,128)} %get-tuple-element.7) | copy-start | bytes 898564
  107.4 9.6 %copy-start.7 = (f32[8,4,8,2,128]{4,3,2,1,0:T(2,128)S(1)}, f32[8,4,8,2,128]{4,3,2,1,0:T(2,128)}, u32[]{:S(2)}) copy-start(f32[8,4,8,2,128]{4,3,2,1,0:T(2,128)} %copy.109) | copy-start | bytes 786436
  107.4 9.6 %copy-start.11 = (f32[1,32,16,128]{3,2,1,0:T(8,128)S(1)}, f32[1,32,16,128]{3,2,1,0:T(8,128)}, u32[]{:S(2)}) copy-start(f32[1,32,16,128]{3,2,1,0:T(8,128)} %param.7) | copy-start | bytes 786436
  109.6 10.0 %collective-permute-start.6 = (f32[32,1,128]{2,1,0:T(1,128)S(1)}, f32[32,1,128]{2,1,0:T(1,128)S(1)}, u32[]{:S(2)}, u32[]{:S(2)}) collective-permute-start(f32[32,1,128]{2,1,0:T(1,128)S(1)} %get-tuple-element.21), channel_id=1, source_target_pairs={{4,0},{8,4},{12,8},{16,12},{20,16},{24,20},{28,24},{32,28},{36,32}... | collective-permute-start | bytes 49160 | tf_op jit(solution)/shard_map/ppermute | solution.py:35
  115.1 8.1 %collective-permute-start.5 = (f32[32,1,128]{2,1,0:T(1,128)S(1)}, f32[32,1,128]{2,1,0:T(1,128)S(1)}, u32[]{:S(2)}, u32[]{:S(2)}) collective-permute-start(f32[32,1,128]{2,1,0:T(1,128)S(1)} %get-tuple-element.20), channel_id=1, source_target_pairs={{0,4},{4,8},{8,12},{12,16},{16,20},{20,24},{24,28},{28,32},{32,36}... | collective-permute-start | bytes 49160 | tf_op jit(solution)/shard_map/ppermute | solution.py:34
  117.0 1.6 %copy-start.1 = (f32[8,4,16,2,64]{4,3,2,1,0:T(2,128)S(1)}, f32[8,4,16,2,64]{4,3,2,1,0:T(2,128)}, u32[]{:S(2)}) copy-start(f32[8,4,16,2,64]{4,3,2,1,0:T(2,128)} %copy.120) | copy-start | bytes 786436
  119.6 9.6 %copy-start.12 = (f32[32,16,128]{2,1,0:T(8,128)S(1)}, f32[32,16,128]{2,1,0:T(8,128)}, u32[]{:S(2)}) copy-start(f32[32,16,128]{2,1,0:T(8,128)} %get-tuple-element.3) | copy-start | bytes 786436
  119.6 9.6 %copy-start.13 = (f32[1,1,32,16,128]{4,3,2,1,0:T(8,128)S(1)}, f32[1,1,32,16,128]{4,3,2,1,0:T(8,128)}, u32[]{:S(2)}) copy-start(f32[1,1,32,16,128]{4,3,2,1,0:T(8,128)} %stack.28) | copy-start | bytes 786436
  123.4 9.7 %collective-permute-start.8 = (f32[32,18,1]{2,1,0:T(8,128)S(1)}, f32[32,18,1]{2,1,0:T(8,128)S(1)}, u32[]{:S(2)}, u32[]{:S(2)}) collective-permute-start(f32[32,18,1]{2,1,0:T(8,128)S(1)} %get-tuple-element.19), channel_id=1, source_target_pairs={{1,0},{2,1},{3,2},{5,4},{6,5},{7,6},{9,8},{10,9},{11,10},{13,12},{... | collective-permute-start | bytes 6920 | tf_op jit(solution)/shard_map/ppermute | solution.py:35
  126.0 9.7 %collective-permute-start.7 = (f32[32,18,1]{2,1,0:T(8,128)S(1)}, f32[32,18,1]{2,1,0:T(8,128)S(1)}, u32[]{:S(2)}, u32[]{:S(2)}) collective-permute-start(f32[32,18,1]{2,1,0:T(8,128)S(1)} %get-tuple-element.18), channel_id=1, source_target_pairs={{0,1},{1,2},{2,3},{4,5},{5,6},{6,7},{8,9},{9,10},{10,11},{12,13},{... | collective-permute-start | bytes 6920 | tf_op jit(solution)/shard_map/ppermute | solution.py:34
  129.2 7.0 %copy-start.3 = (f32[1,2,32,16,128]{4,3,2,1,0:T(8,128)S(1)}, f32[1,2,32,16,128]{4,3,2,1,0:T(8,128)}, u32[]{:S(2)}) copy-start(f32[1,2,32,16,128]{4,3,2,1,0:T(8,128)} %param.8) | copy-start | bytes 1572868
  129.3 7.0 %copy-start.8 = (f32[8,4,8,2,128]{4,3,2,1,0:T(2,128)S(1)}, f32[8,4,8,2,128]{4,3,2,1,0:T(2,128)}, u32[]{:S(2)}) copy-start(f32[8,4,8,2,128]{4,3,2,1,0:T(2,128)} %copy.109) | copy-start | bytes 786436
  129.3 7.0 %copy-start.9 = (f32[32,16,128]{2,1,0:T(8,128)S(1)}, f32[32,16,128]{2,1,0:T(8,128)}, u32[]{:S(2)}) copy-start(f32[32,16,128]{2,1,0:T(8,128)} %reshape.346) | copy-start | bytes 786436
where the time goes:
time: 140 us; the launch traced here: 138 us
  starting transfers between devices  60.2 us (43%)
  other arithmetic  34.7 us (25%)
  local copies, waits for them, and re-layouts  32.3 us (23%)
  waiting for transfers between devices  9.12 us (7%)
    ppermute x6, starting transfers between devices, padded_2(): after = lax.ppermute(first, axis, down)  32 us
    ppermute x6, starting transfers between devices, padded_2(): before = lax.ppermute(last, axis, up)  15.2 us
    scatter-add x1, other arithmetic, per_device(): plate_total = jnp.zeros((plate_count, ZQ, CY // 2), jnp.float32).at[plate...  15.1 us
    all_to_all x1, starting transfers between devices, per_device(): lax.all_to_all(moved, 'slab', split_axis=0, concat_axis=0, tiled=True)  9.81 us
    ppermute x6, waiting for transfers between devices, padded_2(): before = lax.ppermute(last, axis, up)  6.21 us
    concatenate x6, other arithmetic, padded_2(): shard = jnp.concatenate([before, shard, after], axis=dim)  4.22 us
    ppermute x1, starting transfers between devices, swapped(): lax.ppermute(shard, axis, [(i, i ^ 1 << apart) for i in range(lax.axis_si...  3.26 us
    ppermute x2, local copies, waits for them, and re-layouts, padded_2(): before = lax.ppermute(last, axis, up)  3.24 us
  transfers between devices with their start and end apart: 14, of which 3 were waited for; matrix products, arithmetic and copies ran while one was open for 17% of the time, Pallas kernels for 0%

commit v1 on v0

v1 whole, which is shorter than its diff:
```python
import functools

import jax
import jax.numpy as jnp
from jax import lax
from jax.experimental import pallas as pl
from jax.experimental.pallas import tpu as pltpu
from jax.sharding import PartitionSpec as P

PZ = 32
ZQ = 4
CX = 16
CY = 128
HALF = CY // 2

heat_dt = 0.07
phase_dt = 0.1
laser_power = 3.0
liquefying_threshold = 0.3
freezing_line_gradient = 0.5
solute_reject = 0.5
PHASE_WEIGHTS = (1.0, 1.3, 0.7)
SOLUTE_WEIGHTS = (0.8, 0.8, 0.8)

F32 = jnp.float32
BF16 = jnp.bfloat16
BIG = 1 << 20


def iota(shape, dim):
    return lax.broadcasted_iota(jnp.int32, shape, dim)


def ones_where(mask):
    return jnp.where(mask, 1.0, 0.0).astype(BF16)


def two_parts(x):
    high = x.astype(BF16)
    return high, (x - high.astype(F32)).astype(BF16)


def dot(a, b, dims=((1,), (0,))):
    return lax.dot_general(a, b, (dims, ((), ())), preferred_element_type=F32)


def pick_left(table, x, dims=((1,), (0,))):
    width = x.shape[1]
    both = dot(table, jnp.concatenate(two_parts(x), axis=1), dims)
    return both[:, :width] + both[:, width:]


def pick_right(x, table, dims=((1,), (0,))):
    high, low = two_parts(x)
    return dot(high, table, dims) + dot(low, table, dims)


def plate_table(owners, sources, slab):
    count = owners.shape[0] // 2
    rows = []
    for parity in (0, 1):
        own = owners[pl.ds(parity, count, stride=2), :]
        src = sources[pl.ds(parity, count, stride=2), :]
        key = iota(own.shape, 1) * 256 + src
        mine = own == slab
        first = jnp.min(jnp.where(mine, key, BIG).astype(F32), axis=1, keepdims=True)
        last = jnp.max(jnp.where(mine, key, -1).astype(F32), axis=1, keepdims=True)
        first, last = first.astype(jnp.int32), last.astype(jnp.int32)
        for value, valid in ((first, first < BIG), (last, last > first)):
            unit = value & 255
            place = jnp.where(valid, (unit & 1) * 128 + (unit >> 1), -1)
            rows.append(ones_where(iota((count, 256), 1) == place))
    return jnp.concatenate(rows, axis=0)


def window_table(owners, slab):
    count = owners.shape[0] // 2
    own = owners[pl.ds(slab, 1), :]
    units = own.shape[1]
    unit = iota((count, units), 1)
    rows = []
    for parity in (0, 1):
        mine = jnp.broadcast_to(own, (count, units)) == iota((count, units), 0) * 2 + parity
        first = jnp.min(jnp.where(mine, unit, BIG).astype(F32), axis=1, keepdims=True)
        last = jnp.max(jnp.where(mine, unit, -1).astype(F32), axis=1, keepdims=True)
        first, last = first.astype(jnp.int32), last.astype(jnp.int32)
        rows.append(ones_where(unit == first))
        rows.append(ones_where((unit == last) & (last > first)))
    spread = ones_where((iota((units, 2 * units), 1) >> 1) == iota((units, 2 * units), 0))
    return dot(jnp.concatenate(rows, axis=0), spread).astype(BF16)


def pack_kernel(ids, owners, sources, heat, out):
    grp, slab = ids[0], ids[1]
    count = owners.shape[0] // 2
    lane = iota((CY, CY), 1)

    def store(result, pair):
        for block in range(4):
            out[:, block * 2 + pair, :] = result[block * count : (block + 1) * count]

    @pl.when(grp == 0)
    def _():
        table = plate_table(owners, sources, slab)
        for pair in (0, 1):
            even = heat[:, 2 * pair].reshape(CY, CY)
            odd = heat[:, 2 * pair + 1].reshape(CY, CY)
            left = jnp.where(lane < HALF, even, pltpu.roll(odd, HALF, 1))
            right = jnp.where(lane < HALF, pltpu.roll(even, HALF, 1), odd)
            store(pick_left(table, jnp.concatenate([left, right], axis=0)), pair)

    @pl.when(grp == 1)
    def _():
        table = window_table(owners, slab)
        row = iota((2 * CY, CY), 0)
        col = iota((2 * CY, CY), 1)
        mean = jnp.where((row >> 1) == col, 0.25, 0.0).astype(BF16)
        for pair in (0, 1):
            even = heat[:, 2 * pair].reshape(CY, CY)
            odd = heat[:, 2 * pair + 1].reshape(CY, CY)
            means = pick_right(jnp.concatenate([even, odd], axis=1), mean)
            store(pick_left(table, means), pair)


def edge_columns(x, first_row):
    row, lane = iota((8, CY), 0), iota((8, CY), 1)
    pick = ((row == first_row) & (lane == 0)) | ((row == first_row + 1) & (lane == CY - 1))
    high, low = two_parts(x)
    dims = ((1,), (1,))
    return dot(ones_where(pick), high, dims) + dot(ones_where(pick), low, dims)


def send_edges(x, parity, near, far, part):
    top, bottom = x[:, 0, :], x[:, CX - 1, :]
    near[part] = jnp.where(parity == 0, bottom, top)
    far[part] = jnp.where(parity == 0, top, bottom)


def edges_kernel(ids, heat, coeff, order, near, far, sides):
    grp, parity = ids[0], ids[1] & 1

    def send(fields):
        total = jnp.zeros((8, PZ * CX), F32)
        for part, field in enumerate(fields):
            send_edges(field, parity, near, far, part)
            total = total + edge_columns(field[...].reshape(PZ * CX, CY), 2 * part)
        sides[...] = total

    @pl.when(grp == 0)
    def _():
        send((heat, coeff))

    @pl.when(grp == 1)
    def _():
        send((order.at[0], order.at[1]))


def receive_sides(ids, sides, part):
    col, cols = ids[2], sides.shape[0]
    left = sides[pl.ds(jnp.maximum(col - 1, 0), 1), 2 * part + 1, :]
    right = sides[pl.ds(jnp.minimum(col + 1, cols - 1), 1), 2 * part, :]
    left = jnp.where(col > 0, left, 0.0)
    right = jnp.where(col < cols - 1, right, 0.0)
    size = left.shape[1]
    row = iota((8, size), 0)
    left = jnp.broadcast_to(left, (8, size))
    right = jnp.broadcast_to(right, (8, size))
    both = jnp.where(row == 0, left, jnp.where(row == 1, right, 0.0))
    row, lane = iota((8, CY), 0), iota((8, CY), 1)
    place = ones_where(((row == 0) & (lane == 0)) | ((row == 1) & (lane == CY - 1)))
    return pick_right(both, place, ((0,), (0,)))


def receive_rows(ids, near, far, part, above, below, slabs):
    slab = ids[1]
    parity = slab & 1
    near_row = jnp.where(parity == 0, near[1, part], near[0, part])
    far_row = jnp.where(parity == 0, far[0, part], far[1, part])
    above[...] = jnp.where(slab == 0, 0.0, jnp.where(parity == 0, far_row, near_row))
    below[...] = jnp.where(slab == slabs - 1, 0.0, jnp.where(parity == 0, near_row, far_row))


def beside(v, above, below, sides):
    row, lane = iota((CX, CY), 0), iota((CX, CY), 1)
    up = jnp.where(row == 0, jnp.broadcast_to(above, (CX, CY)), pltpu.roll(v, 1, 0))
    down = jnp.where(row == CX - 1, jnp.broadcast_to(below, (CX, CY)), pltpu.roll(v, CX - 1, 0))
    left = jnp.where(lane == 0, sides, pltpu.roll(v, 1, 1))
    right = jnp.where(lane == CY - 1, sides, pltpu.roll(v, CY - 1, 1))
    return up, down, left, right


def harmonic(center, beside_it):
    return 2.0 * center * beside_it / (center + beside_it)


def heat_planes(temp, cond, order, source, result, temp_halo, cond_halo):
    temp_above, temp_below, temp_sides = temp_halo
    cond_above, cond_below, cond_sides = cond_halo

    def plane(z, from_above):
        v, k = temp[z], cond[z]
        one = pl.ds(z, 1)
        vs = beside(v, temp_above[one, :], temp_below[one, :], temp_sides[z])
        ks = beside(k, cond_above[one, :], cond_below[one, :], cond_sides[z])
        later = jnp.minimum(z + 1, PZ - 1)
        to_below = harmonic(k, cond[later]) * (temp[later] - v)
        total = to_below - from_above
        for v_next, k_next in zip(vs, ks):
            total = total + harmonic(k, k_next) * (v_next - v)
        result[z] = v + heat_dt * ((total + source(z)) / order[0, z] - order[1, z] * v)
        return to_below

    lax.fori_loop(0, PZ, plane, jnp.zeros((CX, CY), F32), unroll=4)


def phase_planes(phi, sol, response, warmth, new_phi, new_sol, phi_halo, sol_halo):
    phi_above, phi_below, phi_sides = phi_halo
    sol_above, sol_below, sol_sides = sol_halo

    def spread(field, z, halo, weights):
        above, below, sides = halo
        f = field[z]
        one = pl.ds(z, 1)
        up, down, left, right = beside(f, above[one, :], below[one, :], sides[z])
        before = jnp.where(z > 0, field[jnp.maximum(z - 1, 0)], 0.0)
        after = jnp.where(z < PZ - 1, field[jnp.minimum(z + 1, PZ - 1)], 0.0)
        wz, wx, wy = weights
        total = (wz * ((before - f) + (after - f)) + wx * ((up - f) + (down - f))) + wy * (
            (left - f) + (right - f)
        )
        return f, total

    def plane(z, carry):
        p, spread_p = spread(phi, z, phi_halo, PHASE_WEIGHTS)
        s, spread_s = spread(sol, z, sol_halo, SOLUTE_WEIGHTS)
        drive = 0.45 * jnp.tanh(
            response[z] * (liquefying_threshold - warmth[z] - freezing_line_gradient * s)
        )
        p_new = p + phase_dt * (spread_p + 4.0 * p * (1.0 - p) * (p - 0.5 + drive))
        new_phi[z] = p_new
        new_sol[z] = s + phase_dt * spread_s - solute_reject * (p_new - p) * s
        return carry

    lax.fori_loop(0, PZ, plane, 0, unroll=4)


def first_kernel(
    slabs,
    ids,
    laser,
    owners,
    sources,
    inbox,
    near,
    far,
    sides,
    heat,
    coeff,
    order,
    warmth,
    joined,
    near_out,
    far_out,
    sides_out,
    above_a,
    below_a,
    sides_a,
    above_b,
    below_b,
    sides_b,
    deposit,
):
    grp, slab = ids[0], ids[1]
    parity = slab & 1
    count = owners.shape[0] // 2
    for part, (above, below, side) in enumerate(
        ((above_a, below_a, sides_a), (above_b, below_b, sides_b))
    ):
        receive_rows(ids, near, far, part, above, below, slabs)
        side[...] = receive_sides(ids, sides, part).reshape(PZ, CX, CY)
    halo_a = (above_a, below_a, sides_a)
    halo_b = (above_b, below_b, sides_b)

    def arrived(pair):
        rows = []
        for core in (0, 1):
            for slot in (0, 1):
                at = 2 * slot + pair
                rows.append(
                    jnp.where(parity == 0, inbox[core, :, at, :], inbox[core, :, 4 + at, :])
                )
        return jnp.concatenate(rows, axis=0)

    lane = iota((CY, CY), 1)

    @pl.when(grp == 0)
    def _():
        table = plate_table(owners, sources, slab)
        for pair in (0, 1):
            units = pick_left(table, arrived(pair), ((0,), (0,)))
            left, right = units[:CY], units[CY:]
            even = jnp.where(lane < HALF, left, pltpu.roll(right, HALF, 1))
            odd = jnp.where(lane < HALF, pltpu.roll(left, HALF, 1), right)
            for i, layer in ((2 * pair, even), (2 * pair + 1, odd)):
                layer = layer.reshape(PZ // ZQ, CX, CY)
                for q in range(PZ // ZQ):
                    joined[0, 0, ZQ * q + i] = layer[q]
        cell = iota((CX, CY), 0) * CY + iota((CX, CY), 1)

        def add(n, total):
            return total + jnp.where(cell == laser[n], laser_power, 0.0)

        deposit[...] = lax.fori_loop(
            0, laser.shape[0], add, jnp.zeros((CX, CY), F32), unroll=True
        )

        def source(z):
            return joined[0, 0, z] + jnp.where(z == 0, deposit[...], 0.0)

        first = joined.at[0, 1]
        heat_planes(heat, coeff, order, source, first, halo_a, halo_b)
        send_edges(first, parity, near_out, far_out, 0)
        sides_out[...] = edge_columns(first[...].reshape(PZ * CX, CY), 0)

    @pl.when(grp == 1)
    def _():
        table = window_table(owners, slab)
        row = iota((CY, 2 * CY), 0)
        col = iota((CY, 2 * CY), 1)
        target = col & (CY - 1)
        parent = target >> 1
        next_to = jnp.clip(parent - 1 + 2 * (target & 1), 0, HALF - 1)
        at = row - (col >> 7) * HALF
        fine = (jnp.where(at == parent, 0.75, 0.0) + jnp.where(at == next_to, 0.25, 0.0)).astype(
            BF16
        )
        for pair in (0, 1):
            refined = pick_right(arrived(pair), fine)
            placed = pick_left(table, refined, ((0,), (0,)))
            for i in (0, 1):
                layer = placed[:, i * CY : (i + 1) * CY].reshape(PZ // ZQ, CX, CY)
                for q in range(PZ // ZQ):
                    warmth[0, ZQ * q + 2 * pair + i] = layer[q]
        phase_planes(
            order.at[0],
            order.at[1],
            coeff,
            warmth.at[0],
            joined.at[0, 0],
            joined.at[0, 1],
            halo_a,
            halo_b,
        )


def second_kernel(
    slabs,
    ids,
    laser,
    near_k,
    far_k,
    sides_k,
    near,
    far,
    sides,
    coeff,
    order,
    warmth,
    joined,
    result,
    above_a,
    below_a,
    sides_a,
    above_b,
    below_b,
    sides_b,
    deposit,
):
    grp = ids[0]

    @pl.when(grp == 0)
    def _():
        receive_rows(ids, near, far, 0, above_a, below_a, slabs)
        sides_a[...] = receive_sides(ids, sides, 0).reshape(PZ, CX, CY)
        receive_rows(ids, near_k, far_k, 1, above_b, below_b, slabs)
        sides_b[...] = receive_sides(ids, sides_k, 1).reshape(PZ, CX, CY)
        cell = iota((CX, CY), 0) * CY + iota((CX, CY), 1)

        def add(n, total):
            return total + jnp.where(cell == laser[n], laser_power, 0.0)

        deposit[...] = lax.fori_loop(
            0, laser.shape[0], add, jnp.zeros((CX, CY), F32), unroll=True
        )

        def source(z):
            return joined[0, 0, z] + jnp.where(z == 0, deposit[...], 0.0)

        heat_planes(
            joined.at[0, 1],
            coeff,
            order,
            source,
            result.at[0],
            (above_a, below_a, sides_a),
            (above_b, below_b, sides_b),
        )

    @pl.when(grp == 1)
    def _():
        result[...] = warmth[...]


SMEM = pl.BlockSpec(memory_space=pltpu.SMEM)
VMEM = pl.BlockSpec(memory_space=pltpu.VMEM)
PARAMS = pltpu.CompilerParams(vmem_limit_bytes=24 << 20)


def call(kernel, specs, outs, scratch=()):
    shapes = [jax.ShapeDtypeStruct(shape, F32) for shape in outs]
    single = len(shapes) == 1
    return pl.pallas_call(
        kernel,
        out_shape=shapes[0] if single else shapes,
        in_specs=list(specs),
        out_specs=VMEM if single else [VMEM] * len(shapes),
        scratch_shapes=list(scratch),
        compiler_params=PARAMS,
    )


def halo_scratch():
    one = [
        pltpu.VMEM((PZ, CY), F32),
        pltpu.VMEM((PZ, CY), F32),
        pltpu.VMEM((PZ, CX, CY), F32),
    ]
    return one + one + [pltpu.VMEM((CX, CY), F32)]


def per_device(heat_field, coeff, order, block_owner, block_source, laser_cells):
    slabs = lax.axis_size("slab")
    chips = slabs // 2
    grp = lax.axis_index("grp")
    ids = jnp.stack([grp, lax.axis_index("slab"), lax.axis_index("col")]).astype(jnp.int32)
    near_pairs = [[2 * i, 2 * i + 1] for i in range(chips)]
    far_pairs = [[2 * i + 1, (2 * i + 2) % slabs] for i in range(chips)]
    same_core = [[2 * i + k for i in range(chips)] for k in range(2)]
    heat, conduct, orders = heat_field[0], coeff[0], order[0]
    owners, sources, laser = block_owner[0, :, :, 0], block_source[0], laser_cells[0, 0]

    outbox = call(pack_kernel, [SMEM, VMEM, VMEM, VMEM], [(chips, 8, CY)])(
        ids, owners, sources, heat.reshape(PZ // ZQ, ZQ, CX, CY)
    )
    crossed = lax.all_gather(outbox, "grp")
    crossed = lax.dynamic_index_in_dim(crossed, 1 - grp, 0, keepdims=False)
    moved = lax.all_to_all(
        crossed, "slab", split_axis=0, concat_axis=0, tiled=True, axis_index_groups=same_core
    )
    inbox = lax.all_gather(moved, "slab", axis_index_groups=near_pairs)

    rows, columns = (2, PZ, CY), (8, PZ * CX)
    near, far, sides = call(edges_kernel, [SMEM, VMEM, VMEM, VMEM], [rows, rows, columns])(
        ids, heat, conduct, orders
    )

    def exchanged(near, far, sides):
        def pairs(x, groups):
            return lax.all_gather(x, "slab", axis_index_groups=groups)

        return pairs(near, near_pairs), pairs(far, far_pairs), lax.all_gather(sides, "col")

    near, far, sides = exchanged(near, far, sides)
    row, field = (1, PZ, CY), (PZ, CX, CY)
    warmth, joined, near_1, far_1, sides_1 = call(
        functools.partial(first_kernel, slabs),
        [SMEM, SMEM] + [VMEM] * 9,
        [(1,) + field, (1, 2) + field, row, row, columns],
        halo_scratch(),
    )(ids, laser, owners, sources, inbox, near, far, sides, heat, conduct, orders)
    near_1, far_1, sides_1 = exchanged(near_1, far_1, sides_1)
    warmth = call(
        functools.partial(second_kernel, slabs),
        [SMEM, SMEM] + [VMEM] * 10,
        [(1,) + field],
        halo_scratch(),
    )(ids, laser, near, far, sides, near_1, far_1, sides_1, conduct, orders, warmth, joined)
    return warmth, joined


def solution(mesh):
    placed = (
        P("grp", None, "slab", "col"),
        P("grp", None, "slab", "col"),
        P("grp", None, None, "slab", "col"),
        P("col", None, None, None),
        P("col", None, None),
        P("slab", "col", None),
    )
    return jax.shard_map(
        per_device,
        mesh=mesh,
        in_specs=placed,
        out_specs=(P("grp", None, "slab", "col"), P("grp", None, None, "slab", "col")),
        check_vma=False,
    )
```

time: 140 us -> 81.6 us (0.58)
  the two profiles are of different devices: /device:TPU:58 before, /device:TPU:32 now
where the time goes in v1:
time: 81.6 us; the launch traced here: 81.1 us
  blocking collectives  52.2 us (64%)
  starting transfers between devices  15.9 us (19%)
  Pallas kernels  7.56 us (9%)
  local copies, waits for them, and re-layouts  4.75 us (6%)
    all_gather x2, blocking collectives, exchanged(): lax.all_gather(sides, 'col')  24 us
    all_gather x4, blocking collectives, pairs(): return lax.all_gather(x, 'slab', axis_index_groups=groups)  19.9 us
    all_to_all x1, starting transfers between devices, per_device(): lax.all_to_all(crossed, 'slab', split_axis=0, concat_axis=0, tiled=True,...  15.9 us
    all_gather x1, blocking collectives, per_device(): crossed = lax.all_gather(outbox, 'grp')  6.04 us
    unnamed x18, local copies, waits for them, and re-layouts  4.09 us
    pallas_call x1, Pallas kernels, per_device(): call(functools.partial(first_kernel, slabs), [SMEM, SMEM] + [VMEM] * 9, [...  3.28 us
    pallas_call x1, Pallas kernels, per_device(): call(functools.partial(second_kernel, slabs), [SMEM, SMEM] + [VMEM] * 10,...  2.51 us
    all_gather x1, blocking collectives, per_device(): inbox = lax.all_gather(moved, 'slab', axis_index_groups=near_pairs)  2.11 us
  transfers between devices with their start and end apart: 1, of which 0 were waited for; matrix products, arithmetic and copies ran while one was open for 0% of the time, Pallas kernels for 1%

profile of v1, /device:TPU:32, one launch (start us, length us, event | category | flops | bytes accessed | tf_op | source)
XLA Modules:
  0.0 81.1 jit_solution(2381953105609336852)
XLA Ops:
  0.6 0.0 copy-start.5
  0.6 0.1 pad_add_fusion.ids
  0.7 0.7 copy-done.5
  1.4 0.0 copy-start.1
  1.4 0.9 %copy-done.1 = f32[1,32,16,128]{3,2,1,0:T(8,128)S(1)} copy-done((f32[1,32,16,128]{3,2,1,0:T(8,128)S(1)}, f32[1,32,16,128]{3,2,1,0:T(8,128)}, u32[]{:S(2)}) %copy-start.1) | copy-done | bytes 262168
  2.3 0.0 copy-start.6
  2.3 0.8 copy-done.6
  3.1 0.0 copy-start.3
  3.1 0.9 %shard_map.78 = f32[32,8,128]{2,1,0:T(8,128)S(1)} custom-call(s32[3]{0:T(128)S(1)} %pad_add_fusion.ids, s32[64,64]{1,0:T(8,128)S(1)} %bitcast.39, s32[64,64]{1,0:T(8,128)S(1)} %bitcast.41, f32[8,4,16,128]{3,2,1,0:T(8,128)S(1)} %bitcast.23), custom_call_target="tpu_custom_call" | custom-call | tf_op jit(solution)/shard_map/pallas_call | solution.py:452
  4.1 0.0 copy-start
  4.1 6.0 %all-gather.3 = f32[64,8,128]{2,1,0:T(8,128)S(1)} all-gather(f32[32,8,128]{2,1,0:T(8,128)S(1)} %shard_map.78), channel_id=5, replica_groups=mesh['grp'=2,'slab'=64,'col'=4] {'grp'}, dimensions={0}, use_global_device_ids=true | all-gather | bytes 393216 | tf_op jit(solution)/shard_map/all_gather | solution.py:455
  10.1 0.0 copy-start.2
  10.1 0.7 dynamic-slice_bitcast_fusion
  10.8 15.9 %all-to-all-start = ((f32[32,8,128]{2,1,0:T(8,128)}), f32[32,8,128]{2,1,0:T(8,128)S(1)}, u32[]{:S(2)}, u32[]{:S(2)}) async-start(f32[32,8,128]{2,1,0:T(8,128)} %dynamic-slice_bitcast_fusion), calls=%async_computation | async-start | bytes 262144 | tf_op jit(solution)/shard_map/all_to_all | solution.py:457
  26.6 0.0 copy-done.3
  26.6 0.0 copy-done
  26.7 0.0 copy-done.2
  26.7 0.8 %shard_map.77 = (f32[2,32,128]{2,1,0:T(8,128)S(1)}, f32[2,32,128]{2,1,0:T(8,128)S(1)}, f32[8,512]{1,0:T(8,128)S(1)}) custom-call(s32[3]{0:T(128)S(1)} %pad_add_fusion.ids, f32[32,16,128]{2,1,0:T(8,128)S(1)} %bitcast.24, f32[32,16,128]{2,1,0:T(8,128)S(1)} %bitcast.26, f32[2,32,16,128]{3,2,1,0:T(8,128)S(1)} %bitcast.20), custom_call_target="tpu_custom_call" | custom-call | tf_op jit(solution)/shard_map/pallas_call | solution.py:463
  27.5 1.9 %all-gather = f32[4,32,128]{2,1,0:T(8,128)S(1)} all-gather(f32[2,32,128]{2,1,0:T(8,128)S(1)} %get-tuple-element.10), channel_id=2, replica_groups={{0,4},{8,12},{16,20},{24,28},{32,36},{40,44},{48,52},{56,60},{64,68},{7..., dimensions={0}, use_global_device_ids=true | all-gather | bytes 98304 | tf_op jit(solution)/shard_map/all_gather | solution.py:469
  29.4 8.2 %all-gather.1 = f32[4,32,128]{2,1,0:T(8,128)S(1)} all-gather(f32[2,32,128]{2,1,0:T(8,128)S(1)} %get-tuple-element.11), channel_id=3, replica_groups={{4,8},{12,16},{20,24},{28,32},{36,40},{44,48},{52,56},{60,64},{68,72},{..., dimensions={0}, use_global_device_ids=true | all-gather | bytes 98304 | tf_op jit(solution)/shard_map/all_gather | solution.py:469
  37.6 12.2 %all-gather.2 = f32[32,512]{1,0:T(8,128)S(1)} all-gather(f32[8,512]{1,0:T(8,128)S(1)} %get-tuple-element.12), channel_id=4, replica_groups=mesh['grp'=2,'slab'=64,'col'=4] {'col'}, dimensions={0}, use_global_device_ids=true | all-gather | bytes 81920 | tf_op jit(solution)/shard_map/all_gather | solution.py:471
  49.8 0.0 copy-start.7
  49.8 0.0 all-to-all-done
  49.8 2.1 %all-gather.4 = f32[64,8,128]{2,1,0:T(8,128)S(1)} all-gather(f32[32,8,128]{2,1,0:T(8,128)S(1)} %all-to-all-done), channel_id=6, replica_groups={{0,4},{8,12},{16,20},{24,28},{32,36},{40,44},{48,52},{56,60},{64,68},{7..., dimensions={0}, use_global_device_ids=true | all-gather | bytes 393216 | tf_op jit(solution)/shard_map/all_gather | solution.py:460
  51.9 0.0 copy-start.8
  51.9 0.0 copy-done.7
  51.9 0.7 copy-done.8
  52.6 3.3 %shard_map.79 = (f32[1,32,16,128]{3,2,1,0:T(8,128)S(1)}, f32[1,2,32,16,128]{4,3,2,1,0:T(8,128)}, f32[1,32,128]{2,1,0:T(8,128)S(1)}, f32[1,32,128]{2,1,0:T(8,128)S(1)}, f32[8,512]{1,0:T(8,128)S(1)}) custom-call(s32[3]{0:T(128)S(1)} %pad_add_fusion.ids, s32[32]{0:T(128)S(1)} %bitcast.43, s32[64,64]{1,0:T(8,128)S(1)} %bitcast.40, s32[64,64]{1,0:T(8,128)S(1)} %bitcast.42, ...), custom_call_target="tpu_custom_call" | custom-call | tf_op jit(solution)/shard_map/pallas_call | solution.py:475
  55.8 1.8 %all-gather.5 = f32[2,32,128]{2,1,0:T(8,128)S(1)} all-gather(f32[1,32,128]{2,1,0:T(8,128)S(1)} %get-tuple-element.13), channel_id=7, replica_groups={{0,4},{8,12},{16,20},{24,28},{32,36},{40,44},{48,52},{56,60},{64,68},{7..., dimensions={0}, use_global_device_ids=true | all-gather | bytes 49152 | tf_op jit(solution)/shard_map/all_gather | solution.py:469
  57.7 8.0 %all-gather.6 = f32[2,32,128]{2,1,0:T(8,128)S(1)} all-gather(f32[1,32,128]{2,1,0:T(8,128)S(1)} %get-tuple-element.14), channel_id=8, replica_groups={{4,8},{12,16},{20,24},{28,32},{36,40},{44,48},{52,56},{60,64},{68,72},{..., dimensions={0}, use_global_device_ids=true | all-gather | bytes 49152 | tf_op jit(solution)/shard_map/all_gather | solution.py:469
  65.7 11.9 %all-gather.7 = f32[32,512]{1,0:T(8,128)S(1)} all-gather(f32[8,512]{1,0:T(8,128)S(1)} %get-tuple-element.15), channel_id=9, replica_groups=mesh['grp'=2,'slab'=64,'col'=4] {'col'}, dimensions={0}, use_global_device_ids=true | all-gather | bytes 81920 | tf_op jit(solution)/shard_map/all_gather | solution.py:471
  77.6 0.0 copy-start.4
  77.6 1.0 %copy-done.4 = f32[1,2,32,16,128]{4,3,2,1,0:T(8,128)S(1)} copy-done((f32[1,2,32,16,128]{4,3,2,1,0:T(8,128)S(1)}, f32[1,2,32,16,128]{4,3,2,1,0:T(8,128)}, u32[]{:S(2)}) %copy-start.4) | copy-done | bytes 524312
  78.6 2.5 %shard_map.80 = f32[1,32,16,128]{3,2,1,0:T(8,128)} custom-call(s32[3]{0:T(128)S(1)} %pad_add_fusion.ids, s32[32]{0:T(128)S(1)} %bitcast.44, f32[2,2,32,128]{3,2,1,0:T(8,128)S(1)} %bitcast.33, f32[2,2,32,128]{3,2,1,0:T(8,128)S(1)} %bitcast.35, f32[4,8,512]{2,1,0:T(8,128)S(1)} %bitcast.31, f32[2,1,32,128]{3,2,1,0:T(8,128)S(1)} %bitcast.37, ...), custom_call_target="tpu_custom_call" | custom-call | tf_op jit(solution)/shard_map/pallas_call | solution.py:482
Async XLA Ops:
  0.6 0.8 copy-start.5
  1.4 0.9 %copy-start.1 = (f32[1,32,16,128]{3,2,1,0:T(8,128)S(1)}, f32[1,32,16,128]{3,2,1,0:T(8,128)}, u32[]{:S(2)}) copy-start(f32[1,32,16,128]{3,2,1,0:T(8,128)} %param.6) | copy-start | bytes 786436
  2.3 0.8 copy-start.6
  3.1 23.5 %copy-start.3 = (f32[1,32,16,128]{3,2,1,0:T(8,128)S(1)}, f32[1,32,16,128]{3,2,1,0:T(8,128)}, u32[]{:S(2)}) copy-start(f32[1,32,16,128]{3,2,1,0:T(8,128)} %param.7) | copy-start | bytes 786436
  4.1 22.6 %copy-start = (f32[1,2,32,16,128]{4,3,2,1,0:T(8,128)S(1)}, f32[1,2,32,16,128]{4,3,2,1,0:T(8,128)}, u32[]{:S(2)}) copy-start(f32[1,2,32,16,128]{4,3,2,1,0:T(8,128)} %param.8) | copy-start | bytes 1572868
  10.1 16.6 %copy-start.2 = (f32[1,32,16,128]{3,2,1,0:T(8,128)S(1)}, f32[1,32,16,128]{3,2,1,0:T(8,128)}, u32[]{:S(2)}) copy-start(f32[1,32,16,128]{3,2,1,0:T(8,128)} %param.6) | copy-start | bytes 786436
  10.8 39.0 %all-to-all-start = ((f32[32,8,128]{2,1,0:T(8,128)}), f32[32,8,128]{2,1,0:T(8,128)S(1)}, u32[]{:S(2)}, u32[]{:S(2)}) async-start(f32[32,8,128]{2,1,0:T(8,128)} %dynamic-slice_bitcast_fusion), calls=%async_computation | async-start | bytes 262144 | tf_op jit(solution)/shard_map/all_to_all | solution.py:457
  49.8 2.1 %copy-start.7 = (s32[1,64,64]{2,1,0:T(8,128)S(1)}, s32[1,64,64]{2,1,0:T(8,128)}, u32[]{:S(2)}) copy-start(s32[1,64,64]{2,1,0:T(8,128)} %param.10) | copy-start | bytes 49156
  51.9 0.7 copy-start.8
  77.6 1.0 %copy-start.4 = (f32[1,2,32,16,128]{4,3,2,1,0:T(8,128)S(1)}, f32[1,2,32,16,128]{4,3,2,1,0:T(8,128)}, u32[]{:S(2)}) copy-start(f32[1,2,32,16,128]{4,3,2,1,0:T(8,128)} %get-tuple-element.9.joined) | copy-start | bytes 1572868

commit v2 on v1

--- a/solution.py
+++ b/solution.py
@@ -1,5 +1,3 @@
-import functools
-
 import jax
 import jax.numpy as jnp
 from jax import lax
@@ -90,8 +88,9 @@
     return dot(jnp.concatenate(rows, axis=0), spread).astype(BF16)
 
 
-def pack_kernel(ids, owners, sources, heat, out):
+def pack_kernel(ids, owners, sources, heats, out):
     grp, slab = ids[0], ids[1]
+    heat = heats.at[1 - grp]
     count = owners.shape[0] // 2
     lane = iota((CY, CY), 1)
 
@@ -99,7 +98,7 @@
         for block in range(4):
             out[:, block * 2 + pair, :] = result[block * count : (block + 1) * count]
 
-    @pl.when(grp == 0)
+    @pl.when(grp == 1)
     def _():
         table = plate_table(owners, sources, slab)
         for pair in (0, 1):
@@ -109,7 +108,7 @@
             right = jnp.where(lane < HALF, pltpu.roll(even, HALF, 1), odd)
             store(pick_left(table, jnp.concatenate([left, right], axis=0)), pair)
 
-    @pl.when(grp == 1)
+    @pl.when(grp == 0)
     def _():
         table = window_table(owners, slab)
         row = iota((2 * CY, CY), 0)
@@ -122,45 +121,40 @@
             store(pick_left(table, means), pair)
 
 
-def edge_columns(x, first_row):
-    row, lane = iota((8, CY), 0), iota((8, CY), 1)
-    pick = ((row == first_row) & (lane == 0)) | ((row == first_row + 1) & (lane == CY - 1))
+def edge_columns(x, right):
+    pick = ones_where(iota((8, CY), 1) == jnp.where(right, CY - 1, 0))
     high, low = two_parts(x)
     dims = ((1,), (1,))
-    return dot(ones_where(pick), high, dims) + dot(ones_where(pick), low, dims)
-
-
-def send_edges(x, parity, near, far, part):
-    top, bottom = x[:, 0, :], x[:, CX - 1, :]
-    near[part] = jnp.where(parity == 0, bottom, top)
-    far[part] = jnp.where(parity == 0, top, bottom)
-
-
-def edges_kernel(ids, heat, coeff, order, near, far, sides):
-    grp, parity = ids[0], ids[1] & 1
-
-    def send(fields):
-        total = jnp.zeros((8, PZ * CX), F32)
-        for part, field in enumerate(fields):
-            send_edges(field, parity, near, far, part)
-            total = total + edge_columns(field[...].reshape(PZ * CX, CY), 2 * part)
-        sides[...] = total
+    return (dot(pick, high, dims) + dot(pick, low, dims))[:1]
+
+
+def send_edges(ids, fields, near, far, side_a, side_b):
+    even_slab, even_col = ids[1] & 1 == 0, ids[2] & 1 == 0
+    for part, x in enumerate(fields):
+        top, bottom = x[:, 0, :], x[:, CX - 1, :]
+        near[part] = jnp.where(even_slab, bottom, top)
+        far[part] = jnp.where(even_slab, top, bottom)
+        flat = x[...].reshape(PZ * CX, CY)
+        side_a[part : part + 1] = edge_columns(flat, even_col)
+        side_b[part : part + 1] = edge_columns(flat, jnp.logical_not(even_col))
+
+
+def edges_kernel(ids, heat, coeff, order, near, far, side_a, side_b):
+    grp = ids[0]
 
     @pl.when(grp == 0)
     def _():
-        send((heat, coeff))
+        send_edges(ids, (heat, coeff), near, far, side_a, side_b)
 
     @pl.when(grp == 1)
     def _():
-        send((order.at[0], order.at[1]))
-
-
-def receive_sides(ids, sides, part):
-    col, cols = ids[2], sides.shape[0]
-    left = sides[pl.ds(jnp.maximum(col - 1, 0), 1), 2 * part + 1, :]
-    right = sides[pl.ds(jnp.minimum(col + 1, cols - 1), 1), 2 * part, :]
-    left = jnp.where(col > 0, left, 0.0)
-    right = jnp.where(col < cols - 1, right, 0.0)
+        send_edges(ids, (order.at[0], order.at[1]), near, far, side_a, side_b)
+
+
+def receive_sides(ids, side_a, side_b, part):
+    even = ids[2] & 1 == 0
+    in_a, in_b = side_a[part : part + 1], side_b[part : part + 1]
+    left, right = jnp.where(even, in_b, in_a), jnp.where(even, in_a, in_b)
     size = left.shape[1]
     row = iota((8, size), 0)
     left = jnp.broadcast_to(left, (8, size))
@@ -171,13 +165,12 @@
     return pick_right(both, place, ((0,), (0,)))
 
 
-def receive_rows(ids, near, far, part, above, below, slabs):
-    slab = ids[1]
-    parity = slab & 1
-    near_row = jnp.where(parity == 0, near[1, part], near[0, part])
-    far_row = jnp.where(parity == 0, far[0, part], far[1, part])
-    above[...] = jnp.where(slab == 0, 0.0, jnp.where(parity == 0, far_row, near_row))
-    below[...] = jnp.where(slab == slabs - 1, 0.0, jnp.where(parity == 0, near_row, far_row))
+def receive_rows(ids, near, far, part, above, below):
+    even = ids[1] & 1 == 0
+    near_row = jnp.where(even, near[1, part], near[0, part])
+    far_row = far[part]
+    above[...] = jnp.where(even, far_row, near_row)
+    below[...] = jnp.where(even, near_row, far_row)
 
 
 def beside(v, above, below, sides):
@@ -245,7 +238,6 @@
 
 
 def first_kernel(
-    slabs,
     ids,
     laser,
     owners,
@@ -253,7 +245,8 @@
     inbox,
     near,
     far,
-    sides,
+    side_a,
+    side_b,
     heat,
     coeff,
     order,
@@ -261,7 +254,8 @@
     joined,
     near_out,
     far_out,
-    sides_out,
+    side_a_out,
+    side_b_out,
     above_a,
     below_a,
     sides_a,
@@ -276,8 +270,8 @@
     for part, (above, below, side) in enumerate(
         ((above_a, below_a, sides_a), (above_b, below_b, sides_b))
     ):
-        receive_rows(ids, near, far, part, above, below, slabs)
-        side[...] = receive_sides(ids, sides, part).reshape(PZ, CX, CY)
+        receive_rows(ids, near, far, part, above, below)
+        side[...] = receive_sides(ids, side_a, side_b, part).reshape(PZ, CX, CY)
     halo_a = (above_a, below_a, sides_a)
     halo_b = (above_b, below_b, sides_b)
 
@@ -319,8 +313,7 @@
 
         first = joined.at[0, 1]
         heat_planes(heat, coeff, order, source, first, halo_a, halo_b)
-        send_edges(first, parity, near_out, far_out, 0)
-        sides_out[...] = edge_columns(first[...].reshape(PZ * CX, CY), 0)
+        send_edges(ids, (first,), near_out, far_out, side_a_out, side_b_out)
 
     @pl.when(grp == 1)
     def _():
@@ -354,15 +347,16 @@
 
 
 def second_kernel(
-    slabs,
     ids,
     laser,
     near_k,
     far_k,
-    sides_k,
+    side_a_k,
+    side_b_k,
     near,
     far,
-    sides,
+    side_a,
+    side_b,
     coeff,
     order,
     warmth,
@@ -380,10 +374,10 @@
 
     @pl.when(grp == 0)
     def _():
-        receive_rows(ids, near, far, 0, above_a, below_a, slabs)
-        sides_a[...] = receive_sides(ids, sides, 0).reshape(PZ, CX, CY)
-        receive_rows(ids, near_k, far_k, 1, above_b, below_b, slabs)
-        sides_b[...] = receive_sides(ids, sides_k, 1).reshape(PZ, CX, CY)
+        receive_rows(ids, near, far, 0, above_a, below_a)
+        sides_a[...] = receive_sides(ids, side_a, side_b, 0).reshape(PZ, CX, CY)
+        receive_rows(ids, near_k, far_k, 1, above_b, below_b)
+        sides_b[...] = receive_sides(ids, side_a_k, side_b_k, 1).reshape(PZ, CX, CY)
         cell = iota((CX, CY), 0) * CY + iota((CX, CY), 1)
 
         def add(n, total):
@@ -438,53 +432,57 @@
     return one + one + [pltpu.VMEM((CX, CY), F32)]
 
 
+def swaps(starts):
+    return [pair for i in starts for pair in ((i, i + 1), (i + 1, i))]
+
+
 def per_device(heat_field, coeff, order, block_owner, block_source, laser_cells):
-    slabs = lax.axis_size("slab")
+    slabs, cols = lax.axis_size("slab"), lax.axis_size("col")
     chips = slabs // 2
     grp = lax.axis_index("grp")
     ids = jnp.stack([grp, lax.axis_index("slab"), lax.axis_index("col")]).astype(jnp.int32)
     near_pairs = [[2 * i, 2 * i + 1] for i in range(chips)]
-    far_pairs = [[2 * i + 1, (2 * i + 2) % slabs] for i in range(chips)]
     same_core = [[2 * i + k for i in range(chips)] for k in range(2)]
+    far_swap = swaps(range(1, slabs - 1, 2))
+    side_a_swap, side_b_swap = swaps(range(0, cols - 1, 2)), swaps(range(1, cols - 1, 2))
     heat, conduct, orders = heat_field[0], coeff[0], order[0]
     owners, sources, laser = block_owner[0, :, :, 0], block_source[0], laser_cells[0, 0]
 
+    heats = lax.all_gather(heat.reshape(PZ // ZQ, ZQ, CX, CY), "grp")
     outbox = call(pack_kernel, [SMEM, VMEM, VMEM, VMEM], [(chips, 8, CY)])(
-        ids, owners, sources, heat.reshape(PZ // ZQ, ZQ, CX, CY)
+        ids, owners, sources, heats
     )
-    crossed = lax.all_gather(outbox, "grp")
-    crossed = lax.dynamic_index_in_dim(crossed, 1 - grp, 0, keepdims=False)
     moved = lax.all_to_all(
-        crossed, "slab", split_axis=0, concat_axis=0, tiled=True, axis_index_groups=same_core
+        outbox, "slab", split_axis=0, concat_axis=0, tiled=True, axis_index_groups=same_core
     )
     inbox = lax.all_gather(moved, "slab", axis_index_groups=near_pairs)
 
-    rows, columns = (2, PZ, CY), (8, PZ * CX)
-    near, far, sides = call(edges_kernel, [SMEM, VMEM, VMEM, VMEM], [rows, rows, columns])(
+    def exchanged(near, far, side_a, side_b):
+        far = lax.ppermute(far, "slab", far_swap)
+        side_a = lax.ppermute(side_a, "col", side_a_swap)
+        side_b = lax.ppermute(side_b, "col", side_b_swap)
+        near = lax.all_gather(near, "slab", axis_index_groups=near_pairs)
+        return near, far, side_a, side_b
+
+    rows, column = (2, PZ, CY), (2, PZ * CX)
+    edges = call(edges_kernel, [SMEM, VMEM, VMEM, VMEM], [rows, rows, column, column])(
         ids, heat, conduct, orders
     )
-
-    def exchanged(near, far, sides):
-        def pairs(x, groups):
-            return lax.all_gather(x, "slab", axis_index_groups=groups)
-
-        return pairs(near, near_pairs), pairs(far, far_pairs), lax.all_gather(sides, "col")
-
-    near, far, sides = exchanged(near, far, sides)
-    row, field = (1, PZ, CY), (PZ, CX, CY)
-    warmth, joined, near_1, far_1, sides_1 = call(
-        functools.partial(first_kernel, slabs),
-        [SMEM, SMEM] + [VMEM] * 9,
-        [(1,) + field, (1, 2) + field, row, row, columns],
+    edges = exchanged(*edges)
+    row, column, field = (1, PZ, CY), (1, PZ * CX), (PZ, CX, CY)
+    warmth, joined, *edges_1 = call(
+        first_kernel,
+        [SMEM, SMEM] + [VMEM] * 10,
+        [(1,) + field, (1, 2) + field, row, row, column, column],
         halo_scratch(),
-    )(ids, laser, owners, sources, inbox, near, far, sides, heat, conduct, orders)
-    near_1, far_1, sides_1 = exchanged(near_1, far_1, sides_1)
+    )(ids, laser, owners, sources, inbox, *edges, heat, conduct, orders)
+    edges_1 = exchanged(*edges_1)
     warmth = call(
-        functools.partial(second_kernel, slabs),
-        [SMEM, SMEM] + [VMEM] * 10,
+        second_kernel,
+        [SMEM, SMEM] + [VMEM] * 12,
         [(1,) + field],
         halo_scratch(),
-    )(ids, laser, near, far, sides, near_1, far_1, sides_1, conduct, orders, warmth, joined)
+    )(ids, laser, *edges, *edges_1, conduct, orders, warmth, joined)
     return warmth, joined
 
 

time: 81.6 us -> 64.2 us (0.79)
  the two profiles are of different devices: /device:TPU:32 before, /device:TPU:34 now
where the time goes in v2:
time: 64.2 us; the launch traced here: 63.8 us
  starting transfers between devices  32.6 us (51%)
  blocking collectives  15.8 us (25%)
  Pallas kernels  8.62 us (13%)
  waiting for transfers between devices  4.19 us (7%)
  local copies, waits for them, and re-layouts  1.72 us (3%)
  between operations  0.75 us (1%)
    all_to_all x1, starting transfers between devices, per_device(): lax.all_to_all(outbox, 'slab', split_axis=0, concat_axis=0, tiled=True, a...  16.1 us
    all_gather x1, blocking collectives, per_device(): heats = lax.all_gather(heat.reshape(PZ // ZQ, ZQ, CX, CY), 'grp')  9.07 us
    ppermute x2, starting transfers between devices, exchanged(): far = lax.ppermute(far, 'slab', far_swap)  6.2 us
    ppermute x2, starting transfers between devices, exchanged(): side_b = lax.ppermute(side_b, 'col', side_b_swap)  6.03 us
    all_gather x2, blocking collectives, exchanged(): near = lax.all_gather(near, 'slab', axis_index_groups=near_pairs)  4.8 us
    ppermute x2, starting transfers between devices, exchanged(): side_a = lax.ppermute(side_a, 'col', side_a_swap)  4.31 us
    pallas_call x1, Pallas kernels, per_device(): call(first_kernel, [SMEM, SMEM] + [VMEM] * 10, [(1,) + field, (1, 2) + fi...  3.35 us
    pallas_call x1, Pallas kernels, per_device(): call(second_kernel, [SMEM, SMEM] + [VMEM] * 12, [(1,) + field], halo_scra...  2.5 us
  transfers between devices with their start and end apart: 7, of which 2 were waited for; matrix products, arithmetic and copies ran while one was open for 0% of the time, Pallas kernels for 2%

profile of v2, /device:TPU:34, one launch (start us, length us, event | category | flops | bytes accessed | tf_op | source)
XLA Modules:
  0.0 63.8 jit_solution(8898176321912895709)
XLA Ops:
  0.6 0.0 copy-start.4
  0.6 0.0 copy-start.5
  0.7 0.0 copy-start.2
  0.7 9.1 %all_gather.23.heats = f32[2,8,4,16,128]{4,3,2,1,0:T(8,128)S(1)} all-gather(f32[1,8,4,16,128]{4,3,2,1,0:T(8,128)} %bitcast.16), channel_id=1, replica_groups=mesh['grp'=2,'slab'=64,'col'=4] {'grp'}, dimensions={0}, use_global_device_ids=true | all-gather | bytes 786432 | tf_op jit(solution)/shard_map/all_gather | solution.py:451
  9.7 0.0 copy-start
  9.7 0.1 pad_add_fusion.ids
  9.8 0.0 copy-done.4
  9.8 0.0 copy-done.5
  9.8 1.8 %shard_map.78 = f32[32,8,128]{2,1,0:T(8,128)} custom-call(s32[3]{0:T(128)S(1)} %pad_add_fusion.ids, s32[64,64]{1,0:T(8,128)S(1)} %bitcast.26, s32[64,64]{1,0:T(8,128)S(1)} %bitcast.28, f32[2,8,4,16,128]{4,3,2,1,0:T(8,128)S(1)} %all_gather.23.heats), custom_call_target="tpu_custom_call" | custom-call | tf_op jit(solution)/shard_map/pallas_call | solution.py:452
  11.6 0.0 copy-start.1
  11.6 16.1 %all-to-all-start = ((f32[32,8,128]{2,1,0:T(8,128)}), f32[32,8,128]{2,1,0:T(8,128)S(1)}, u32[]{:S(2)}, u32[]{:S(2)}) async-start(f32[32,8,128]{2,1,0:T(8,128)} %shard_map.78), calls=%async_computation | async-start | bytes 262144 | tf_op jit(solution)/shard_map/all_to_all | solution.py:455
  27.7 0.0 copy-done.2
  27.7 0.0 copy-done
  27.7 0.0 copy-done.1
  27.7 1.0 %shard_map.77 = (f32[2,32,128]{2,1,0:T(8,128)S(1)}, f32[2,32,128]{2,1,0:T(8,128)S(1)}, f32[2,512]{1,0:T(2,128)S(1)}, f32[2,512]{1,0:T(2,128)S(1)}) custom-call(s32[3]{0:T(128)S(1)} %pad_add_fusion.ids, f32[32,16,128]{2,1,0:T(8,128)S(1)} %bitcast.17, f32[32,16,128]{2,1,0:T(8,128)S(1)} %bitcast.19, f32[2,32,16,128]{3,2,1,0:T(8,128)S(1)} %bitcast.13), custom_call_target="tpu_custom_call" | custom-call | tf_op jit(solution)/shard_map/pallas_call | solution.py:468
  28.7 2.4 %collective-permute-start.1 = (f32[2,512]{1,0:T(2,128)S(1)}, f32[2,512]{1,0:T(2,128)S(1)}, u32[]{:S(2)}, u32[]{:S(2)}) collective-permute-start(f32[2,512]{1,0:T(2,128)S(1)} %get-tuple-element.14), channel_id=1, source_target_pairs={{0,1},{1,0},{2,3},{3,2},{4,5},{5,4},{6,7},{7,6},{8,9},{9,8},{10,11... | collective-permute-start | bytes 12296 | tf_op jit(solution)/shard_map/ppermute | solution.py:462
  31.1 4.1 %collective-permute-start.2 = (f32[2,512]{1,0:T(2,128)S(1)}, f32[2,512]{1,0:T(2,128)S(1)}, u32[]{:S(2)}, u32[]{:S(2)}) collective-permute-start(f32[2,512]{1,0:T(2,128)S(1)} %get-tuple-element.15), channel_id=1, source_target_pairs={{1,2},{2,1},{5,6},{6,5},{9,10},{10,9},{13,14},{14,13},{17,18},{18,... | collective-permute-start | bytes 12296 | tf_op jit(solution)/shard_map/ppermute | solution.py:463
  35.2 2.0 %collective-permute-start = (f32[2,32,128]{2,1,0:T(8,128)S(1)}, f32[2,32,128]{2,1,0:T(8,128)S(1)}, u32[]{:S(2)}, u32[]{:S(2)}) collective-permute-start(f32[2,32,128]{2,1,0:T(8,128)S(1)} %get-tuple-element.13), channel_id=1, source_target_pairs={{4,8},{8,4},{12,16},{16,12},{20,24},{24,20},{28,32},{32,28},{36,40... | collective-permute-start | bytes 98312 | tf_op jit(solution)/shard_map/ppermute | solution.py:461
  37.2 3.0 %all-gather = f32[4,32,128]{2,1,0:T(8,128)S(1)} all-gather(f32[2,32,128]{2,1,0:T(8,128)S(1)} %get-tuple-element.12), channel_id=2, replica_groups={{0,4},{8,12},{16,20},{24,28},{32,36},{40,44},{48,52},{56,60},{64,68},{7..., dimensions={0}, use_global_device_ids=true | all-gather | bytes 98304 | tf_op jit(solution)/shard_map/all_gather | solution.py:464
  40.2 0.0 all-to-all-done
  40.2 2.0 %all-gather.1 = f32[64,8,128]{2,1,0:T(8,128)S(1)} all-gather(f32[32,8,128]{2,1,0:T(8,128)S(1)} %all-to-all-done), channel_id=3, replica_groups={{0,4},{8,12},{16,20},{24,28},{32,36},{40,44},{48,52},{56,60},{64,68},{7..., dimensions={0}, use_global_device_ids=true | all-gather | bytes 393216 | tf_op jit(solution)/shard_map/all_gather | solution.py:458
  42.2 0.0 collective-permute-done.1.side_a.side_a_k
  42.2 0.0 collective-permute-done.2.side_b.side_b_k
  42.2 2.5 %collective-permute-done.far.far_k = f32[2,32,128]{2,1,0:T(8,128)S(1)} collective-permute-done((f32[2,32,128]{2,1,0:T(8,128)S(1)}, f32[2,32,128]{2,1,0:T(8,128)S(1)}, u32[]{:S(2)}, u32[]{:S(2)}) %collective-permute-start) | collective-permute-done | bytes 32800 | tf_op jit(solution)/shard_map/ppermute | solution.py:461
  44.7 0.0 copy-start.6
  44.7 0.7 %copy-done.6 = s32[1,1,32]{2,1,0:T(1,128)S(1)} copy-done((s32[1,1,32]{2,1,0:T(1,128)S(1)}, s32[1,1,32]{2,1,0:T(1,128)}, u32[]{:S(2)}) %copy-start.6) | copy-done | bytes 152
  45.3 3.3 %shard_map.79 = (f32[1,32,16,128]{3,2,1,0:T(8,128)S(1)}, f32[1,2,32,16,128]{4,3,2,1,0:T(8,128)}, f32[1,32,128]{2,1,0:T(8,128)S(1)}, f32[1,32,128]{2,1,0:T(8,128)...) custom-call(s32[3]{0:T(128)S(1)} %pad_add_fusion.ids, s32[32]{0:T(128)S(1)} %bitcast.30, s32[64,64]{1,0:T(8,128)S(1)} %bitcast.27, ...), custom_call_target="tpu_custom_call" | custom-call | tf_op jit(solution)/shard_map/pallas_call | solution.py:473
  48.7 4.2 %collective-permute-start.3 = (f32[1,32,128]{2,1,0:T(8,128)S(1)}, f32[1,32,128]{2,1,0:T(8,128)S(1)}, u32[]{:S(2)}, u32[]{:S(2)}) collective-permute-start(f32[1,32,128]{2,1,0:T(8,128)S(1)} %get-tuple-element.17), channel_id=1, source_target_pairs={{4,8},{8,4},{12,16},{16,12},{20,24},{24,20},{28,32},{32,28},{36,40... | collective-permute-start | bytes 49160 | tf_op jit(solution)/shard_map/ppermute | solution.py:461
  52.8 1.9 %collective-permute-start.4 = (f32[1,512]{1,0:T(1,128)S(1)}, f32[1,512]{1,0:T(1,128)S(1)}, u32[]{:S(2)}, u32[]{:S(2)}) collective-permute-start(f32[1,512]{1,0:T(1,128)S(1)} %get-tuple-element.18), channel_id=1, source_target_pairs={{0,1},{1,0},{2,3},{3,2},{4,5},{5,4},{6,7},{7,6},{8,9},{9,8},{10,11... | collective-permute-start | bytes 6152 | tf_op jit(solution)/shard_map/ppermute | solution.py:462
  54.8 1.9 %collective-permute-start.5 = (f32[1,512]{1,0:T(1,128)S(1)}, f32[1,512]{1,0:T(1,128)S(1)}, u32[]{:S(2)}, u32[]{:S(2)}) collective-permute-start(f32[1,512]{1,0:T(1,128)S(1)} %get-tuple-element.19), channel_id=1, source_target_pairs={{1,2},{2,1},{5,6},{6,5},{9,10},{10,9},{13,14},{14,13},{17,18},{18,... | collective-permute-start | bytes 6152 | tf_op jit(solution)/shard_map/ppermute | solution.py:463
  56.7 1.8 %all-gather.2 = f32[2,32,128]{2,1,0:T(8,128)S(1)} all-gather(f32[1,32,128]{2,1,0:T(8,128)S(1)} %get-tuple-element.16), channel_id=4, replica_groups={{0,4},{8,12},{16,20},{24,28},{32,36},{40,44},{48,52},{56,60},{64,68},{7..., dimensions={0}, use_global_device_ids=true | all-gather | bytes 49152 | tf_op jit(solution)/shard_map/all_gather | solution.py:464
  58.5 0.0 collective-permute-done.4.side_a
  58.5 1.7 %collective-permute-done.5.side_b = f32[1,512]{1,0:T(1,128)S(1)} collective-permute-done((f32[1,512]{1,0:T(1,128)S(1)}, f32[1,512]{1,0:T(1,128)S(1)}, u32[]{:S(2)}, u32[]{:S(2)}) %collective-permute-start.5) | collective-permute-done | bytes 2080 | tf_op jit(solution)/shard_map/ppermute | solution.py:463
  60.3 0.0 collective-permute-done.3.far
  60.3 0.0 copy-start.3
  60.3 1.0 %copy-done.3 = f32[1,2,32,16,128]{4,3,2,1,0:T(8,128)S(1)} copy-done((f32[1,2,32,16,128]{4,3,2,1,0:T(8,128)S(1)}, f32[1,2,32,16,128]{4,3,2,1,0:T(8,128)}, u32[]{:S(2)}) %copy-start.3) | copy-done | bytes 524312
  61.3 2.5 %shard_map.80 = f32[1,32,16,128]{3,2,1,0:T(8,128)} custom-call(s32[3]{0:T(128)S(1)} %pad_add_fusion.ids, s32[32]{0:T(128)S(1)} %bitcast.31, f32[2,2,32,128]{3,2,1,0:T(8,128)S(1)} %bitcast.24, f32[2,32,128]{2,1,0:T(8,128)S(1)} %collective-permute-done.far.far_k, f32[2,512]{1,0:T(2,128)S(1)} %collective-permute-done.1.side_a.side_a_k, ...), custom_call_target="tpu_custom_call" | custom-call | tf_op jit(solution)/shard_map/pallas_call | solution.py:480
Async XLA Ops:
  0.6 9.2 %copy-start.4 = (s32[1,64,64,1]{2,3,1,0:T(1,128)S(1)}, s32[1,64,64,1]{2,3,1,0:T(1,128)}, u32[]{:S(2)}) copy-start(s32[1,64,64,1]{2,3,1,0:T(1,128)} %param.9) | copy-start | bytes 49156
  0.6 9.2 %copy-start.5 = (s32[1,64,64]{2,1,0:T(8,128)S(1)}, s32[1,64,64]{2,1,0:T(8,128)}, u32[]{:S(2)}) copy-start(s32[1,64,64]{2,1,0:T(8,128)} %param.10) | copy-start | bytes 49156
  0.7 27.0 %copy-start.2 = (f32[1,32,16,128]{3,2,1,0:T(8,128)S(1)}, f32[1,32,16,128]{3,2,1,0:T(8,128)}, u32[]{:S(2)}) copy-start(f32[1,32,16,128]{3,2,1,0:T(8,128)} %param.7) | copy-start | bytes 786436
  9.7 18.0 %copy-start = (f32[1,2,32,16,128]{4,3,2,1,0:T(8,128)S(1)}, f32[1,2,32,16,128]{4,3,2,1,0:T(8,128)}, u32[]{:S(2)}) copy-start(f32[1,2,32,16,128]{4,3,2,1,0:T(8,128)} %param.8) | copy-start | bytes 1572868
  11.6 16.1 %copy-start.1 = (f32[1,32,16,128]{3,2,1,0:T(8,128)S(1)}, f32[1,32,16,128]{3,2,1,0:T(8,128)}, u32[]{:S(2)}) copy-start(f32[1,32,16,128]{3,2,1,0:T(8,128)} %param.6) | copy-start | bytes 786436
  11.6 28.6 %all-to-all-start = ((f32[32,8,128]{2,1,0:T(8,128)}), f32[32,8,128]{2,1,0:T(8,128)S(1)}, u32[]{:S(2)}, u32[]{:S(2)}) async-start(f32[32,8,128]{2,1,0:T(8,128)} %shard_map.78), calls=%async_computation | async-start | bytes 262144 | tf_op jit(solution)/shard_map/all_to_all | solution.py:455
  28.7 13.5 %collective-permute-start.1 = (f32[2,512]{1,0:T(2,128)S(1)}, f32[2,512]{1,0:T(2,128)S(1)}, u32[]{:S(2)}, u32[]{:S(2)}) collective-permute-start(f32[2,512]{1,0:T(2,128)S(1)} %get-tuple-element.14), channel_id=1, source_target_pairs={{0,1},{1,0},{2,3},{3,2},{4,5},{5,4},{6,7},{7,6},{8,9},{9,8},{10,11... | collective-permute-start | bytes 12296 | tf_op jit(solution)/shard_map/ppermute | solution.py:462
  31.1 11.1 %collective-permute-start.2 = (f32[2,512]{1,0:T(2,128)S(1)}, f32[2,512]{1,0:T(2,128)S(1)}, u32[]{:S(2)}, u32[]{:S(2)}) collective-permute-start(f32[2,512]{1,0:T(2,128)S(1)} %get-tuple-element.15), channel_id=1, source_target_pairs={{1,2},{2,1},{5,6},{6,5},{9,10},{10,9},{13,14},{14,13},{17,18},{18,... | collective-permute-start | bytes 12296 | tf_op jit(solution)/shard_map/ppermute | solution.py:463
  35.2 9.5 %collective-permute-start = (f32[2,32,128]{2,1,0:T(8,128)S(1)}, f32[2,32,128]{2,1,0:T(8,128)S(1)}, u32[]{:S(2)}, u32[]{:S(2)}) collective-permute-start(f32[2,32,128]{2,1,0:T(8,128)S(1)} %get-tuple-element.13), channel_id=1, source_target_pairs={{4,8},{8,4},{12,16},{16,12},{20,24},{24,20},{28,32},{32,28},{36,40... | collective-permute-start | bytes 98312 | tf_op jit(solution)/shard_map/ppermute | solution.py:461
  44.7 0.7 %copy-start.6 = (s32[1,1,32]{2,1,0:T(1,128)S(1)}, s32[1,1,32]{2,1,0:T(1,128)}, u32[]{:S(2)}) copy-start(s32[1,1,32]{2,1,0:T(1,128)} %param.11) | copy-start | bytes 388
  48.7 11.6 %collective-permute-start.3 = (f32[1,32,128]{2,1,0:T(8,128)S(1)}, f32[1,32,128]{2,1,0:T(8,128)S(1)}, u32[]{:S(2)}, u32[]{:S(2)}) collective-permute-start(f32[1,32,128]{2,1,0:T(8,128)S(1)} %get-tuple-element.17), channel_id=1, source_target_pairs={{4,8},{8,4},{12,16},{16,12},{20,24},{24,20},{28,32},{32,28},{36,40... | collective-permute-start | bytes 49160 | tf_op jit(solution)/shard_map/ppermute | solution.py:461
  52.8 5.7 %collective-permute-start.4 = (f32[1,512]{1,0:T(1,128)S(1)}, f32[1,512]{1,0:T(1,128)S(1)}, u32[]{:S(2)}, u32[]{:S(2)}) collective-permute-start(f32[1,512]{1,0:T(1,128)S(1)} %get-tuple-element.18), channel_id=1, source_target_pairs={{0,1},{1,0},{2,3},{3,2},{4,5},{5,4},{6,7},{7,6},{8,9},{9,8},{10,11... | collective-permute-start | bytes 6152 | tf_op jit(solution)/shard_map/ppermute | solution.py:462
  54.8 5.5 %collective-permute-start.5 = (f32[1,512]{1,0:T(1,128)S(1)}, f32[1,512]{1,0:T(1,128)S(1)}, u32[]{:S(2)}, u32[]{:S(2)}) collective-permute-start(f32[1,512]{1,0:T(1,128)S(1)} %get-tuple-element.19), channel_id=1, source_target_pairs={{1,2},{2,1},{5,6},{6,5},{9,10},{10,9},{13,14},{14,13},{17,18},{18,... | collective-permute-start | bytes 6152 | tf_op jit(solution)/shard_map/ppermute | solution.py:463
  60.3 1.0 %copy-start.3 = (f32[1,2,32,16,128]{4,3,2,1,0:T(8,128)S(1)}, f32[1,2,32,16,128]{4,3,2,1,0:T(8,128)}, u32[]{:S(2)}) copy-start(f32[1,2,32,16,128]{4,3,2,1,0:T(8,128)} %get-tuple-element.11.joined) | copy-start | bytes 1572868

commit v3 on v2

--- a/solution.py
+++ b/solution.py
@@ -88,9 +88,41 @@
     return dot(jnp.concatenate(rows, axis=0), spread).astype(BF16)
 
 
-def pack_kernel(ids, owners, sources, heats, out):
+def laser_heat(cells):
+    count = cells.shape[1]
+    rows = ones_where(iota((CX, count), 0) == jnp.broadcast_to(cells >> 7, (CX, count)))
+    lanes = ones_where(iota((CY, count), 0) == jnp.broadcast_to(cells & 127, (CY, count)))
+    return laser_power * dot(rows, lanes, ((1,), (1,)))
+
+
+def pack_kernel(
+    ids,
+    owners_in,
+    sources_in,
+    heat_in,
+    laser_in,
+    out,
+    deposit,
+    owners,
+    sources,
+    heat,
+    laser,
+    sems,
+):
+    copies = [
+        pltpu.make_async_copy(source, target, sems.at[n])
+        for n, (source, target) in enumerate(
+            (
+                (owners_in, owners),
+                (sources_in, sources),
+                (heat_in, heat),
+                (laser_in, laser),
+            )
+        )
+    ]
+    for copy in copies:
+        copy.start()
     grp, slab = ids[0], ids[1]
-    heat = heats.at[1 - grp]
     count = owners.shape[0] // 2
     lane = iota((CY, CY), 1)
 
@@ -98,9 +130,14 @@
         for block in range(4):
             out[:, block * 2 + pair, :] = result[block * count : (block + 1) * count]
 
-    @pl.when(grp == 1)
+    for n in (0, 1, 3):
+        copies[n].wait()
+
+    @pl.when(grp == 0)
     def _():
         table = plate_table(owners, sources, slab)
+        deposit[...] = laser_heat(laser[...])
+        copies[2].wait()
         for pair in (0, 1):
             even = heat[:, 2 * pair].reshape(CY, CY)
             odd = heat[:, 2 * pair + 1].reshape(CY, CY)
@@ -108,9 +145,10 @@
             right = jnp.where(lane < HALF, pltpu.roll(even, HALF, 1), odd)
             store(pick_left(table, jnp.concatenate([left, right], axis=0)), pair)
 
-    @pl.when(grp == 0)
+    @pl.when(grp == 1)
     def _():
         table = window_table(owners, slab)
+        copies[2].wait()
         row = iota((2 * CY, CY), 0)
         col = iota((2 * CY, CY), 1)
         mean = jnp.where((row >> 1) == col, 0.25, 0.0).astype(BF16)
@@ -165,9 +203,14 @@
     return pick_right(both, place, ((0,), (0,)))
 
 
+def near_rows(inbox, chips, part):
+    start = chips + part * PZ // 8
+    return [inbox[core, start : start + PZ // 8].reshape(PZ, CY) for core in (0, 1)]
+
+
 def receive_rows(ids, near, far, part, above, below):
     even = ids[1] & 1 == 0
-    near_row = jnp.where(even, near[1, part], near[0, part])
+    near_row = jnp.where(even, near[1], near[0])
     far_row = far[part]
     above[...] = jnp.where(even, far_row, near_row)
     below[...] = jnp.where(even, near_row, far_row)
@@ -186,7 +229,9 @@
     return 2.0 * center * beside_it / (center + beside_it)
 
 
-def heat_planes(temp, cond, order, source, result, temp_halo, cond_halo):
+def heat_planes(
+    temp, cond, order, source, result, temp_halo, cond_halo, begin=0, end=PZ
+):
     temp_above, temp_below, temp_sides = temp_halo
     cond_above, cond_below, cond_sides = cond_halo
 
@@ -203,7 +248,12 @@
         result[z] = v + heat_dt * ((total + source(z)) / order[0, z] - order[1, z] * v)
         return to_below
 
-    lax.fori_loop(0, PZ, plane, jnp.zeros((CX, CY), F32), unroll=4)
+    if begin == 0:
+        carry = jnp.zeros((CX, CY), F32)
+    else:
+        before = begin - 1
+        carry = harmonic(cond[before], cond[begin]) * (temp[begin] - temp[before])
+    lax.fori_loop(begin, end, plane, carry, unroll=4)
 
 
 def phase_planes(phi, sol, response, warmth, new_phi, new_sol, phi_halo, sol_halo):
@@ -239,19 +289,18 @@
 
 def first_kernel(
     ids,
-    laser,
+    deposit,
     owners,
     sources,
     inbox,
-    near,
     far,
     side_a,
     side_b,
     heat,
     coeff,
     order,
+    joined,
     warmth,
-    joined,
     near_out,
     far_out,
     side_a_out,
@@ -262,15 +311,14 @@
     above_b,
     below_b,
     sides_b,
-    deposit,
 ):
     grp, slab = ids[0], ids[1]
     parity = slab & 1
-    count = owners.shape[0] // 2
+    chips = owners.shape[0] // 2
     for part, (above, below, side) in enumerate(
         ((above_a, below_a, sides_a), (above_b, below_b, sides_b))
     ):
-        receive_rows(ids, near, far, part, above, below)
+        receive_rows(ids, near_rows(inbox, chips, part), far, part, above, below)
         side[...] = receive_sides(ids, side_a, side_b, part).reshape(PZ, CX, CY)
     halo_a = (above_a, below_a, sides_a)
     halo_b = (above_b, below_b, sides_b)
@@ -281,7 +329,9 @@
             for slot in (0, 1):
                 at = 2 * slot + pair
                 rows.append(
-                    jnp.where(parity == 0, inbox[core, :, at, :], inbox[core, :, 4 + at, :])
+                    jnp.where(
+                        parity == 0, inbox[core, :chips, at, :], inbox[core, :chips, 4 + at, :]
+                    )
                 )
         return jnp.concatenate(rows, axis=0)
 
@@ -298,20 +348,12 @@
             for i, layer in ((2 * pair, even), (2 * pair + 1, odd)):
                 layer = layer.reshape(PZ // ZQ, CX, CY)
                 for q in range(PZ // ZQ):
-                    joined[0, 0, ZQ * q + i] = layer[q]
-        cell = iota((CX, CY), 0) * CY + iota((CX, CY), 1)
-
-        def add(n, total):
-            return total + jnp.where(cell == laser[n], laser_power, 0.0)
-
-        deposit[...] = lax.fori_loop(
-            0, laser.shape[0], add, jnp.zeros((CX, CY), F32), unroll=True
-        )
+                    joined[0, ZQ * q + i] = layer[q]
 
         def source(z):
-            return joined[0, 0, z] + jnp.where(z == 0, deposit[...], 0.0)
-
-        first = joined.at[0, 1]
+            return joined[0, z] + jnp.where(z == 0, deposit[...], 0.0)
+
+        first = joined.at[1]
         heat_planes(heat, coeff, order, source, first, halo_a, halo_b)
         send_edges(ids, (first,), near_out, far_out, side_a_out, side_b_out)
 
@@ -333,14 +375,14 @@
             for i in (0, 1):
                 layer = placed[:, i * CY : (i + 1) * CY].reshape(PZ // ZQ, CX, CY)
                 for q in range(PZ // ZQ):
-                    warmth[0, ZQ * q + 2 * pair + i] = layer[q]
+                    warmth[ZQ * q + 2 * pair + i] = layer[q]
         phase_planes(
             order.at[0],
             order.at[1],
             coeff,
-            warmth.at[0],
-            joined.at[0, 0],
-            joined.at[0, 1],
+            warmth,
+            joined.at[0],
+            joined.at[1],
             halo_a,
             halo_b,
         )
@@ -348,8 +390,8 @@
 
 def second_kernel(
     ids,
-    laser,
-    near_k,
+    deposit,
+    inbox,
     far_k,
     side_a_k,
     side_b_k,
@@ -359,67 +401,83 @@
     side_b,
     coeff,
     order,
+    joined,
     warmth,
-    joined,
-    result,
+    result_out,
+    joined_out,
     above_a,
     below_a,
     sides_a,
     above_b,
     below_b,
     sides_b,
-    deposit,
+    result,
+    sems,
 ):
     grp = ids[0]
+    joined_copy = pltpu.make_async_copy(joined, joined_out.at[0], sems.at[0])
+    joined_copy.start()
+    parts = RESULT_PARTS
+    size = PZ // parts
 
     @pl.when(grp == 0)
     def _():
-        receive_rows(ids, near, far, 0, above_a, below_a)
+        receive_rows(ids, [near[0, 0], near[1, 0]], far, 0, above_a, below_a)
         sides_a[...] = receive_sides(ids, side_a, side_b, 0).reshape(PZ, CX, CY)
-        receive_rows(ids, near_k, far_k, 1, above_b, below_b)
+        chips = inbox.shape[1] - 2 * PZ // 8
+        receive_rows(ids, near_rows(inbox, chips, 1), far_k, 1, above_b, below_b)
         sides_b[...] = receive_sides(ids, side_a_k, side_b_k, 1).reshape(PZ, CX, CY)
-        cell = iota((CX, CY), 0) * CY + iota((CX, CY), 1)
-
-        def add(n, total):
-            return total + jnp.where(cell == laser[n], laser_power, 0.0)
-
-        deposit[...] = lax.fori_loop(
-            0, laser.shape[0], add, jnp.zeros((CX, CY), F32), unroll=True
-        )
 
         def source(z):
-            return joined[0, 0, z] + jnp.where(z == 0, deposit[...], 0.0)
-
-        heat_planes(
-            joined.at[0, 1],
-            coeff,
-            order,
-            source,
-            result.at[0],
-            (above_a, below_a, sides_a),
-            (above_b, below_b, sides_b),
-        )
+            return joined[0, z] + jnp.where(z == 0, deposit[...], 0.0)
+
+        copies = []
+        for n in range(parts):
+            heat_planes(
+                joined.at[1],
+                coeff,
+                order,
+                source,
+                result,
+                (above_a, below_a, sides_a),
+                (above_b, below_b, sides_b),
+                n * size,
+                (n + 1) * size,
+            )
+            planes = pl.ds(n * size, size)
+            copy = pltpu.make_async_copy(
+                result.at[planes], result_out.at[0, planes], sems.at[1 + n]
+            )
+            copy.start()
+            copies.append(copy)
+        for copy in copies:
+            copy.wait()
 
     @pl.when(grp == 1)
     def _():
-        result[...] = warmth[...]
-
-
+        copy = pltpu.make_async_copy(warmth, result_out.at[0], sems.at[1])
+        copy.start()
+        copy.wait()
+
+    joined_copy.wait()
+
+
+RESULT_PARTS = 4
+HBM = pl.BlockSpec(memory_space=pltpu.HBM)
 SMEM = pl.BlockSpec(memory_space=pltpu.SMEM)
 VMEM = pl.BlockSpec(memory_space=pltpu.VMEM)
-PARAMS = pltpu.CompilerParams(vmem_limit_bytes=24 << 20)
-
-
-def call(kernel, specs, outs, scratch=()):
+
+
+def call(kernel, specs, outs, scratch=(), out_space=VMEM, limit=24 << 20):
     shapes = [jax.ShapeDtypeStruct(shape, F32) for shape in outs]
     single = len(shapes) == 1
     return pl.pallas_call(
         kernel,
         out_shape=shapes[0] if single else shapes,
         in_specs=list(specs),
-        out_specs=VMEM if single else [VMEM] * len(shapes),
+        out_specs=out_space if single else [out_space] * len(shapes),
         scratch_shapes=list(scratch),
-        compiler_params=PARAMS,
+        compiler_params=pltpu.CompilerParams(vmem_limit_bytes=limit),
     )
 
 
@@ -429,7 +487,7 @@
         pltpu.VMEM((PZ, CY), F32),
         pltpu.VMEM((PZ, CX, CY), F32),
     ]
-    return one + one + [pltpu.VMEM((CX, CY), F32)]
+    return one + one
 
 
 def swaps(starts):
@@ -446,44 +504,58 @@
     far_swap = swaps(range(1, slabs - 1, 2))
     side_a_swap, side_b_swap = swaps(range(0, cols - 1, 2)), swaps(range(1, cols - 1, 2))
     heat, conduct, orders = heat_field[0], coeff[0], order[0]
-    owners, sources, laser = block_owner[0, :, :, 0], block_source[0], laser_cells[0, 0]
-
-    heats = lax.all_gather(heat.reshape(PZ // ZQ, ZQ, CX, CY), "grp")
-    outbox = call(pack_kernel, [SMEM, VMEM, VMEM, VMEM], [(chips, 8, CY)])(
-        ids, owners, sources, heats
+    owners, sources, laser = block_owner[0, :, :, 0], block_source[0], laser_cells[0]
+
+    slab_table = pltpu.VMEM(owners.shape, jnp.int32)
+    outbox, deposit = call(
+        pack_kernel,
+        [SMEM] + [HBM] * 4,
+        [(chips, 8, CY), (CX, CY)],
+        [
+            slab_table,
+            slab_table,
+            pltpu.VMEM((PZ // ZQ, ZQ, CX, CY), F32),
+            pltpu.VMEM(laser.shape, jnp.int32),
+            pltpu.SemaphoreType.DMA((4,)),
+        ],
+        limit=60 << 20,
+    )(ids, owners, sources, heat.reshape(PZ // ZQ, ZQ, CX, CY), laser)
+    crossed = lax.all_gather(outbox, "grp")
+    crossed = lax.dynamic_index_in_dim(crossed, 1 - grp, 0, keepdims=False)
+    moved = lax.all_to_all(
+        crossed, "slab", split_axis=0, concat_axis=0, tiled=True, axis_index_groups=same_core
     )
-    moved = lax.all_to_all(
-        outbox, "slab", split_axis=0, concat_axis=0, tiled=True, axis_index_groups=same_core
-    )
-    inbox = lax.all_gather(moved, "slab", axis_index_groups=near_pairs)
-
-    def exchanged(near, far, side_a, side_b):
+
+    def exchanged(far, side_a, side_b):
         far = lax.ppermute(far, "slab", far_swap)
         side_a = lax.ppermute(side_a, "col", side_a_swap)
         side_b = lax.ppermute(side_b, "col", side_b_swap)
-        near = lax.all_gather(near, "slab", axis_index_groups=near_pairs)
-        return near, far, side_a, side_b
-
-    rows, column = (2, PZ, CY), (2, PZ * CX)
-    edges = call(edges_kernel, [SMEM, VMEM, VMEM, VMEM], [rows, rows, column, column])(
-        ids, heat, conduct, orders
+        return far, side_a, side_b
+
+    rows, column = (2, PZ, CY), (12, PZ * CX)
+    near, *edges = call(
+        edges_kernel, [SMEM] + [VMEM] * 3, [rows, rows, column, column]
+    )(ids, heat, conduct, orders)
+    edges = exchanged(*edges)
+    inbox = lax.all_gather(
+        jnp.concatenate([moved, near.reshape(-1, 8, CY)]), "slab", axis_index_groups=near_pairs
     )
-    edges = exchanged(*edges)
     row, column, field = (1, PZ, CY), (1, PZ * CX), (PZ, CX, CY)
-    warmth, joined, *edges_1 = call(
+    joined, warmth, near_1, *edges_1 = call(
         first_kernel,
-        [SMEM, SMEM] + [VMEM] * 10,
-        [(1,) + field, (1, 2) + field, row, row, column, column],
+        [SMEM] + [VMEM] * 10,
+        [(2,) + field, field, row, row, column, column],
         halo_scratch(),
-    )(ids, laser, owners, sources, inbox, *edges, heat, conduct, orders)
+    )(ids, deposit, owners, sources, inbox, *edges, heat, conduct, orders)
     edges_1 = exchanged(*edges_1)
-    warmth = call(
+    near_1 = lax.all_gather(near_1, "slab", axis_index_groups=near_pairs)
+    return call(
         second_kernel,
-        [SMEM, SMEM] + [VMEM] * 12,
-        [(1,) + field],
-        halo_scratch(),
-    )(ids, laser, *edges, *edges_1, conduct, orders, warmth, joined)
-    return warmth, joined
+        [SMEM] + [VMEM] * 13,
+        [(1,) + field, (1, 2) + field],
+        halo_scratch() + [pltpu.VMEM(field, F32), pltpu.SemaphoreType.DMA((1 + RESULT_PARTS,))],
+        HBM,
+    )(ids, deposit, inbox, *edges, near_1, *edges_1, conduct, orders, joined, warmth)
 
 
 def solution(mesh):

time: 64.2 us -> 59.5 us (0.927)
  blocking collectives: 15.8 us -> 10.3 us
  starting transfers between devices: 32.6 us -> 36.2 us
  waiting for transfers between devices: 4.19 us -> 0.99 us
    all_gather x4 -> x3, blocking collectives: 15.8 us -> 10.3 us  [the longest x1 6.26 us: per_device(): crossed = lax.all_gather(outbox, 'grp')]
    ppermute x2, starting transfers between devices: 6.2 us -> 9.25 us  [exchanged(): far = lax.ppermute(far, 'slab', far_swap)]
    ppermute x2, waiting for transfers between devices: 2.46 us -> 0.01 us  [exchanged(): far = lax.ppermute(far, 'slab', far_swap)]
    unnamed x14, local copies, waits for them, and re-layouts: 1.72 us -> 0.67 us
    ppermute x2, waiting for transfers between devices: 1.72 us -> 0.97 us  [exchanged(): side_b = lax.ppermute(side_b, 'col', side_b_swap)]
    ppermute x2, starting transfers between devices: 6.03 us -> 6.72 us  [exchanged(): side_b = lax.ppermute(side_b, 'col', side_b_swap)]
    squeeze x0 -> x1, local copies, waits for them, and re-layouts: none -> 0.66 us  [per_device(): crossed = lax.dynamic_index_in_dim(crossed, 1 - grp, 0, keepdims=False)]
  transfers between devices with their start and end apart: 7 -> 7, of which waited for: 2 -> 1; matrix products, arithmetic and copies ran while one was open for 0% -> 0% of each run, Pallas kernels for 2% -> 2%
where the time goes in v3:
time: 59.5 us; the launch traced here: 59 us
  starting transfers between devices  36.2 us (61%)
  blocking collectives  10.3 us (17%)
  Pallas kernels  8.78 us (15%)
  local copies, waits for them, and re-layouts  1.34 us (2%)
  waiting for transfers between devices  0.99 us (2%)
  between operations  0.81 us (1%)
  other arithmetic  0.68 us (1%)
    all_to_all x1, starting transfers between devices, per_device(): lax.all_to_all(crossed, 'slab', split_axis=0, concat_axis=0, tiled=True,...  15.8 us
    ppermute x2, starting transfers between devices, exchanged(): far = lax.ppermute(far, 'slab', far_swap)  9.25 us
    ppermute x2, starting transfers between devices, exchanged(): side_b = lax.ppermute(side_b, 'col', side_b_swap)  6.72 us
    all_gather x1, blocking collectives, per_device(): crossed = lax.all_gather(outbox, 'grp')  6.26 us
    ppermute x2, starting transfers between devices, exchanged(): side_a = lax.ppermute(side_a, 'col', side_a_swap)  4.36 us
    pallas_call x1, Pallas kernels, per_device(): call(pack_kernel, [SMEM] + [HBM] * 4, [(chips, 8, CY), (CX, CY)], [slab_t...  2.78 us
    pallas_call x1, Pallas kernels, per_device(): call(first_kernel, [SMEM] + [VMEM] * 10, [(2,) + field, field, row, row,...  2.54 us
    pallas_call x1, Pallas kernels, per_device(): call(second_kernel, [SMEM] + [VMEM] * 13, [(1,) + field, (1, 2) + field],...  2.5 us
  transfers between devices with their start and end apart: 7, of which 1 were waited for; matrix products, arithmetic and copies ran while one was open for 0% of the time, Pallas kernels for 2%

profile of v3, /device:TPU:34, one launch (start us, length us, event | category | flops | bytes accessed | tf_op | source)
XLA Modules:
  0.0 59.0 jit_solution(16542698885645166127)
XLA Ops:
  0.6 0.7 %pad_add_fusion.ids = s32[3]{0:T(128)} fusion(s32[1]{0:T(128)} %bitcast.2, s32[1]{0:T(128)} %bitcast.1, s32[1]{0:T(128)} %bitcast), kind=kLoop, calls=%fused_computation.2 | loop fusion | flops 6 | bytes 24 | tf_op jit(solution)/shard_map/stack | solution.py:501
  1.3 0.0 copy-start.2
  1.3 2.8 %shard_map.77 = (f32[32,8,128]{2,1,0:T(8,128)}, f32[16,128]{1,0:T(8,128)}) custom-call(s32[3]{0:T(128)} %pad_add_fusion.ids, s32[64,64]{1,0:T(8,128)} %bitcast.28, s32[64,64]{1,0:T(8,128)} %bitcast.30, f32[8,4,16,128]{3,2,1,0:T(8,128)} %bitcast.21, s32[1,32]{1,0:T(1,128)} %bitcast.34), custom_call_target="tpu_custom_call" | custom-call | tf_op jit(solution)/shard_map/pallas_call | solution.py:510
  4.1 0.0 copy-start
  4.1 6.3 %all-gather = f32[64,8,128]{2,1,0:T(8,128)S(1)} all-gather(f32[32,8,128]{2,1,0:T(8,128)} %get-tuple-element.15), channel_id=2, replica_groups=mesh['grp'=2,'slab'=64,'col'=4] {'grp'}, dimensions={0}, use_global_device_ids=true | all-gather | bytes 393216 | tf_op jit(solution)/shard_map/all_gather | solution.py:523
  10.4 0.0 copy-start.1
  10.4 0.7 %dynamic-slice_bitcast_fusion = f32[32,8,128]{2,1,0:T(8,128)} fusion(f32[2,32,8,128]{3,2,1,0:T(8,128)S(1)} %bitcast.33, s32[]{:T(128)S(6)} %select_n.4), kind=kLoop, calls=%fused_computation.1 | loop fusion | bytes 262148 | tf_op jit(solution)/shard_map/jit(dynamic_index_in_dim)/squeeze | solution.py:524
  11.0 15.8 %all-to-all-start = ((f32[32,8,128]{2,1,0:T(8,128)}), f32[32,8,128]{2,1,0:T(8,128)S(1)}, u32[]{:S(2)}, u32[]{:S(2)}) async-start(f32[32,8,128]{2,1,0:T(8,128)} %dynamic-slice_bitcast_fusion), calls=%async_computation | async-start | bytes 262144 | tf_op jit(solution)/shard_map/all_to_all | solution.py:525
  26.9 0.0 copy-start.6
  26.9 0.0 copy-done.2
  26.9 0.0 copy-done
  26.9 0.0 copy-done.1
  26.9 0.6 %copy-done.6 = s32[3]{0:T(128)S(1)} copy-done((s32[3]{0:T(128)S(1)}, s32[3]{0:T(128)}, u32[]{:S(2)}) %copy-start.6) | copy-done | bytes 36
  27.6 1.0 %shard_map.78 = (f32[2,32,128]{2,1,0:T(8,128)S(1)}, f32[2,32,128]{2,1,0:T(8,128)S(1)}, f32[12,512]{1,0:T(8,128)S(1)}, f32[12,512]{1,0:T(8,128)S(1)}) custom-call(s32[3]{0:T(128)S(1)} %copy-done.6, f32[32,16,128]{2,1,0:T(8,128)S(1)} %bitcast.22, f32[32,16,128]{2,1,0:T(8,128)S(1)} %bitcast.24, f32[2,32,16,128]{3,2,1,0:T(8,128)S(1)} %bitcast.16), custom_call_target="tpu_custom_call" | custom-call | tf_op jit(solution)/shard_map/pallas_call | solution.py:536
  28.5 2.6 %collective-permute-start = (f32[2,32,128]{2,1,0:T(8,128)S(1)}, f32[2,32,128]{2,1,0:T(8,128)S(1)}, u32[]{:S(2)}, u32[]{:S(2)}) collective-permute-start(f32[2,32,128]{2,1,0:T(8,128)S(1)} %get-tuple-element.17), channel_id=1, source_target_pairs={{4,8},{8,4},{12,16},{16,12},{20,24},{24,20},{28,32},{32,28},{36,40... | collective-permute-start | bytes 98312 | tf_op jit(solution)/shard_map/ppermute | solution.py:530
  31.1 2.4 %collective-permute-start.1 = (f32[12,512]{1,0:T(8,128)S(1)}, f32[12,512]{1,0:T(8,128)S(1)}, u32[]{:S(2)}, u32[]{:S(2)}) collective-permute-start(f32[12,512]{1,0:T(8,128)S(1)} %get-tuple-element.18), channel_id=1, source_target_pairs={{0,1},{1,0},{2,3},{3,2},{4,5},{5,4},{6,7},{7,6},{8,9},{9,8},{10,11... | collective-permute-start | bytes 73736 | tf_op jit(solution)/shard_map/ppermute | solution.py:531
  33.6 4.1 %collective-permute-start.2 = (f32[12,512]{1,0:T(8,128)S(1)}, f32[12,512]{1,0:T(8,128)S(1)}, u32[]{:S(2)}, u32[]{:S(2)}) collective-permute-start(f32[12,512]{1,0:T(8,128)S(1)} %get-tuple-element.19), channel_id=1, source_target_pairs={{1,2},{2,1},{5,6},{6,5},{9,10},{10,9},{13,14},{14,13},{17,18},{18,... | collective-permute-start | bytes 73736 | tf_op jit(solution)/shard_map/ppermute | solution.py:532
  37.6 0.0 all-to-all-done
  37.7 0.0 copy-start.3
  37.7 0.0 copy-start.4
  37.7 0.0 copy-start.5
  37.7 2.2 %all-gather.1 = f32[80,8,128]{2,1,0:T(8,128)S(1)} all-gather(f32[40,8,128]{2,1,0:T(8,128)S(1)} %pad_maximum_fusion), channel_id=3, replica_groups={{0,4},{8,12},{16,20},{24,28},{32,36},{40,44},{48,52},{56,60},{64,68},{7..., dimensions={0}, use_global_device_ids=true | all-gather | bytes 491520 | tf_op jit(solution)/shard_map/all_gather | solution.py:540
  39.9 0.0 collective-permute-done.1.side_a.side_a_k
  39.9 0.0 collective-permute-done.2.side_b.side_b_k
  39.9 0.0 collective-permute-done.far.far_k
  39.9 0.0 copy-done.3
  39.9 0.0 copy-done.4
  39.9 0.0 copy-done.5
  39.9 2.5 %shard_map.79 = (f32[2,32,16,128]{3,2,1,0:T(8,128)S(1)}, f32[32,16,128]{2,1,0:T(8,128)S(1)}, f32[1,32,128]{2,1,0:T(8,128)S(1)}, f32[1,32,128]{2,1,0:T(8,128)S(1)...) custom-call(s32[3]{0:T(128)S(1)} %copy-done.6, f32[16,128]{1,0:T(8,128)S(1)} %copy-done.5, s32[64,64]{1,0:T(8,128)S(1)} %bitcast.29, ...), custom_call_target="tpu_custom_call" | custom-call | tf_op jit(solution)/shard_map/pallas_call | solution.py:544
  42.5 6.7 %collective-permute-start.3 = (f32[1,32,128]{2,1,0:T(8,128)S(1)}, f32[1,32,128]{2,1,0:T(8,128)S(1)}, u32[]{:S(2)}, u32[]{:S(2)}) collective-permute-start(f32[1,32,128]{2,1,0:T(8,128)S(1)} %get-tuple-element.21), channel_id=1, source_target_pairs={{4,8},{8,4},{12,16},{16,12},{20,24},{24,20},{28,32},{32,28},{36,40... | collective-permute-start | bytes 49160 | tf_op jit(solution)/shard_map/ppermute | solution.py:530
  49.1 1.9 %collective-permute-start.4 = (f32[1,512]{1,0:T(1,128)S(1)}, f32[1,512]{1,0:T(1,128)S(1)}, u32[]{:S(2)}, u32[]{:S(2)}) collective-permute-start(f32[1,512]{1,0:T(1,128)S(1)} %get-tuple-element.22), channel_id=1, source_target_pairs={{0,1},{1,0},{2,3},{3,2},{4,5},{5,4},{6,7},{7,6},{8,9},{9,8},{10,11... | collective-permute-start | bytes 6152 | tf_op jit(solution)/shard_map/ppermute | solution.py:531
  51.1 2.7 %collective-permute-start.5 = (f32[1,512]{1,0:T(1,128)S(1)}, f32[1,512]{1,0:T(1,128)S(1)}, u32[]{:S(2)}, u32[]{:S(2)}) collective-permute-start(f32[1,512]{1,0:T(1,128)S(1)} %get-tuple-element.23), channel_id=1, source_target_pairs={{1,2},{2,1},{5,6},{6,5},{9,10},{10,9},{13,14},{14,13},{17,18},{18,... | collective-permute-start | bytes 6152 | tf_op jit(solution)/shard_map/ppermute | solution.py:532
  53.7 1.8 %all-gather.2 = f32[2,32,128]{2,1,0:T(8,128)S(1)} all-gather(f32[1,32,128]{2,1,0:T(8,128)S(1)} %get-tuple-element.20), channel_id=4, replica_groups={{0,4},{8,12},{16,20},{24,28},{32,36},{40,44},{48,52},{56,60},{64,68},{7..., dimensions={0}, use_global_device_ids=true | all-gather | bytes 49152 | tf_op jit(solution)/shard_map/all_gather | solution.py:551
  55.6 0.0 collective-permute-done.4.side_a
  55.6 1.0 %collective-permute-done.5.side_b = f32[1,512]{1,0:T(1,128)S(1)} collective-permute-done((f32[1,512]{1,0:T(1,128)S(1)}, f32[1,512]{1,0:T(1,128)S(1)}, u32[]{:S(2)}, u32[]{:S(2)}) %collective-permute-start.5) | collective-permute-done | bytes 2080 | tf_op jit(solution)/shard_map/ppermute | solution.py:532
  56.5 0.0 collective-permute-done.3.far
  56.5 2.5 %shard_map.80 = (f32[1,32,16,128]{3,2,1,0:T(8,128)}, f32[1,2,32,16,128]{4,3,2,1,0:T(8,128)}) custom-call(s32[3]{0:T(128)S(1)} %copy-done.6, f32[16,128]{1,0:T(8,128)S(1)} %copy-done.5, f32[2,40,8,128]{3,2,1,0:T(8,128)S(1)} %bitcast.20, f32[2,32,128]{2,1,0:T(8,128)S(1)} %collective-permute-done.far.far_k, ...), custom_call_target="tpu_custom_call" | custom-call | tf_op jit(solution)/shard_map/pallas_call | solution.py:552
  (1 shorter events, 0.0 us)
Async XLA Ops:
  1.3 25.6 %copy-start.2 = (f32[1,32,16,128]{3,2,1,0:T(8,128)S(1)}, f32[1,32,16,128]{3,2,1,0:T(8,128)}, u32[]{:S(2)}) copy-start(f32[1,32,16,128]{3,2,1,0:T(8,128)} %param.7) | copy-start | bytes 786436
  4.1 22.8 %copy-start = (f32[1,2,32,16,128]{4,3,2,1,0:T(8,128)S(1)}, f32[1,2,32,16,128]{4,3,2,1,0:T(8,128)}, u32[]{:S(2)}) copy-start(f32[1,2,32,16,128]{4,3,2,1,0:T(8,128)} %param.8) | copy-start | bytes 1572868
  10.4 16.6 %copy-start.1 = (f32[1,32,16,128]{3,2,1,0:T(8,128)S(1)}, f32[1,32,16,128]{3,2,1,0:T(8,128)}, u32[]{:S(2)}) copy-start(f32[1,32,16,128]{3,2,1,0:T(8,128)} %param.6) | copy-start | bytes 786436
  11.0 26.6 %all-to-all-start = ((f32[32,8,128]{2,1,0:T(8,128)}), f32[32,8,128]{2,1,0:T(8,128)S(1)}, u32[]{:S(2)}, u32[]{:S(2)}) async-start(f32[32,8,128]{2,1,0:T(8,128)} %dynamic-slice_bitcast_fusion), calls=%async_computation | async-start | bytes 262144 | tf_op jit(solution)/shard_map/all_to_all | solution.py:525
  26.9 0.7 %copy-start.6 = (s32[3]{0:T(128)S(1)}, s32[3]{0:T(128)}, u32[]{:S(2)}) copy-start(s32[3]{0:T(128)} %pad_add_fusion.ids) | copy-start | bytes 40
  28.5 11.4 %collective-permute-start = (f32[2,32,128]{2,1,0:T(8,128)S(1)}, f32[2,32,128]{2,1,0:T(8,128)S(1)}, u32[]{:S(2)}, u32[]{:S(2)}) collective-permute-start(f32[2,32,128]{2,1,0:T(8,128)S(1)} %get-tuple-element.17), channel_id=1, source_target_pairs={{4,8},{8,4},{12,16},{16,12},{20,24},{24,20},{28,32},{32,28},{36,40... | collective-permute-start | bytes 98312 | tf_op jit(solution)/shard_map/ppermute | solution.py:530
  31.1 8.8 %collective-permute-start.1 = (f32[12,512]{1,0:T(8,128)S(1)}, f32[12,512]{1,0:T(8,128)S(1)}, u32[]{:S(2)}, u32[]{:S(2)}) collective-permute-start(f32[12,512]{1,0:T(8,128)S(1)} %get-tuple-element.18), channel_id=1, source_target_pairs={{0,1},{1,0},{2,3},{3,2},{4,5},{5,4},{6,7},{7,6},{8,9},{9,8},{10,11... | collective-permute-start | bytes 73736 | tf_op jit(solution)/shard_map/ppermute | solution.py:531
  33.6 6.3 %collective-permute-start.2 = (f32[12,512]{1,0:T(8,128)S(1)}, f32[12,512]{1,0:T(8,128)S(1)}, u32[]{:S(2)}, u32[]{:S(2)}) collective-permute-start(f32[12,512]{1,0:T(8,128)S(1)} %get-tuple-element.19), channel_id=1, source_target_pairs={{1,2},{2,1},{5,6},{6,5},{9,10},{10,9},{13,14},{14,13},{17,18},{18,... | collective-permute-start | bytes 73736 | tf_op jit(solution)/shard_map/ppermute | solution.py:532
  37.7 2.2 %copy-start.3 = (s32[1,64,64,1]{2,3,1,0:T(1,128)S(1)}, s32[1,64,64,1]{2,3,1,0:T(1,128)}, u32[]{:S(2)}) copy-start(s32[1,64,64,1]{2,3,1,0:T(1,128)} %param.9) | copy-start | bytes 49156
  37.7 2.2 %copy-start.4 = (s32[1,64,64]{2,1,0:T(8,128)S(1)}, s32[1,64,64]{2,1,0:T(8,128)}, u32[]{:S(2)}) copy-start(s32[1,64,64]{2,1,0:T(8,128)} %param.10) | copy-start | bytes 49156
  37.7 2.2 %copy-start.5 = (f32[16,128]{1,0:T(8,128)S(1)}, f32[16,128]{1,0:T(8,128)}, u32[]{:S(2)}) copy-start(f32[16,128]{1,0:T(8,128)} %get-tuple-element.14.deposit) | copy-start | bytes 24580
  42.5 14.1 %collective-permute-start.3 = (f32[1,32,128]{2,1,0:T(8,128)S(1)}, f32[1,32,128]{2,1,0:T(8,128)S(1)}, u32[]{:S(2)}, u32[]{:S(2)}) collective-permute-start(f32[1,32,128]{2,1,0:T(8,128)S(1)} %get-tuple-element.21), channel_id=1, source_target_pairs={{4,8},{8,4},{12,16},{16,12},{20,24},{24,20},{28,32},{32,28},{36,40... | collective-permute-start | bytes 49160 | tf_op jit(solution)/shard_map/ppermute | solution.py:530
  49.1 6.4 %collective-permute-start.4 = (f32[1,512]{1,0:T(1,128)S(1)}, f32[1,512]{1,0:T(1,128)S(1)}, u32[]{:S(2)}, u32[]{:S(2)}) collective-permute-start(f32[1,512]{1,0:T(1,128)S(1)} %get-tuple-element.22), channel_id=1, source_target_pairs={{0,1},{1,0},{2,3},{3,2},{4,5},{5,4},{6,7},{7,6},{8,9},{9,8},{10,11... | collective-permute-start | bytes 6152 | tf_op jit(solution)/shard_map/ppermute | solution.py:531
  51.1 5.5 %collective-permute-start.5 = (f32[1,512]{1,0:T(1,128)S(1)}, f32[1,512]{1,0:T(1,128)S(1)}, u32[]{:S(2)}, u32[]{:S(2)}) collective-permute-start(f32[1,512]{1,0:T(1,128)S(1)} %get-tuple-element.23), channel_id=1, source_target_pairs={{1,2},{2,1},{5,6},{6,5},{9,10},{10,9},{13,14},{14,13},{17,18},{18,... | collective-permute-start | bytes 6152 | tf_op jit(solution)/shard_map/ppermute | solution.py:532

commit v4 on v3

--- a/solution.py
+++ b/solution.py
@@ -160,39 +160,55 @@
 
 
 def edge_columns(x, right):
-    pick = ones_where(iota((8, CY), 1) == jnp.where(right, CY - 1, 0))
+    side = jnp.where(right, iota((8, CY), 0), 1 - iota((8, CY), 0))
+    lane = iota((8, CY), 1)
+    pick = ones_where(((side == 0) & (lane == CY - 1)) | ((side == 1) & (lane == 0)))
     high, low = two_parts(x)
     dims = ((1,), (1,))
-    return (dot(pick, high, dims) + dot(pick, low, dims))[:1]
-
-
-def send_edges(ids, fields, near, far, side_a, side_b):
-    even_slab, even_col = ids[1] & 1 == 0, ids[2] & 1 == 0
-    for part, x in enumerate(fields):
-        top, bottom = x[:, 0, :], x[:, CX - 1, :]
-        near[part] = jnp.where(even_slab, bottom, top)
-        far[part] = jnp.where(even_slab, top, bottom)
-        flat = x[...].reshape(PZ * CX, CY)
-        side_a[part : part + 1] = edge_columns(flat, even_col)
-        side_b[part : part + 1] = edge_columns(flat, jnp.logical_not(even_col))
-
-
-def edges_kernel(ids, heat, coeff, order, near, far, side_a, side_b):
-    grp = ids[0]
+    return (dot(pick, high, dims) + dot(pick, low, dims))[:2]
+
+
+def send_columns(ids, x, side_a, side_b, part):
+    columns = edge_columns(x, ids[2] & 1 == 0)
+    side_a[part : part + 1, : x.shape[0]] = columns[:1]
+    side_b[part : part + 1, : x.shape[0]] = columns[1:]
+
+
+def edge_row(x, top):
+    return jnp.where(top, x[:, 0, :], x[:, CX - 1, :])
+
+
+def edges_kernel(ids, heat, coeff, order, near, side_a, side_b):
+    grp, top = ids[0], ids[1] & 1 == 1
+
+    def send(fields):
+        for part, x in enumerate(fields):
+            near[part] = edge_row(x, top)
+            send_columns(ids, x[...].reshape(PZ * CX, CY), side_a, side_b, part)
 
     @pl.when(grp == 0)
     def _():
-        send_edges(ids, (heat, coeff), near, far, side_a, side_b)
+        send((heat, coeff))
 
     @pl.when(grp == 1)
     def _():
-        send_edges(ids, (order.at[0], order.at[1]), near, far, side_a, side_b)
-
-
-def receive_sides(ids, side_a, side_b, part):
+        send((order.at[0], order.at[1]))
+
+
+def lines_of(ids, side_a, side_b, part):
     even = ids[2] & 1 == 0
     in_a, in_b = side_a[part : part + 1], side_b[part : part + 1]
-    left, right = jnp.where(even, in_b, in_a), jnp.where(even, in_a, in_b)
+    return jnp.where(even, in_b, in_a), jnp.where(even, in_a, in_b)
+
+
+def down(line, start=0, step=1):
+    shape = (PZ, line.shape[1])
+    at = iota(shape, 1) == iota(shape, 0) * step + start
+    return jnp.sum(jnp.where(at, jnp.broadcast_to(line, shape), 0.0), axis=1, keepdims=True)
+
+
+def receive_sides(ids, side_a, side_b, part):
+    left, right = lines_of(ids, side_a, side_b, part)
     size = left.shape[1]
     row = iota((8, size), 0)
     left = jnp.broadcast_to(left, (8, size))
@@ -203,17 +219,9 @@
     return pick_right(both, place, ((0,), (0,)))
 
 
-def near_rows(inbox, chips, part):
+def near_row(inbox, chips, parity, part):
     start = chips + part * PZ // 8
-    return [inbox[core, start : start + PZ // 8].reshape(PZ, CY) for core in (0, 1)]
-
-
-def receive_rows(ids, near, far, part, above, below):
-    even = ids[1] & 1 == 0
-    near_row = jnp.where(even, near[1], near[0])
-    far_row = far[part]
-    above[...] = jnp.where(even, far_row, near_row)
-    below[...] = jnp.where(even, near_row, far_row)
+    return inbox[1 - parity, pl.ds(start, PZ // 8)].reshape(PZ, CY)
 
 
 def beside(v, above, below, sides):
@@ -256,7 +264,9 @@
     lax.fori_loop(begin, end, plane, carry, unroll=4)
 
 
-def phase_planes(phi, sol, response, warmth, new_phi, new_sol, phi_halo, sol_halo):
+def phase_planes(
+    phi, sol, response, warmth, new_phi, new_sol, phi_halo, sol_halo, begin, end
+):
     phi_above, phi_below, phi_sides = phi_halo
     sol_above, sol_below, sol_sides = sol_halo
 
@@ -284,7 +294,7 @@
         new_sol[z] = s + phase_dt * spread_s - solute_reject * (p_new - p) * s
         return carry
 
-    lax.fori_loop(0, PZ, plane, 0, unroll=4)
+    lax.fori_loop(begin, end, plane, 0, unroll=4)
 
 
 def first_kernel(
@@ -293,7 +303,6 @@
     owners,
     sources,
     inbox,
-    far,
     side_a,
     side_b,
     heat,
@@ -314,14 +323,8 @@
 ):
     grp, slab = ids[0], ids[1]
     parity = slab & 1
+    far_top = parity == 0
     chips = owners.shape[0] // 2
-    for part, (above, below, side) in enumerate(
-        ((above_a, below_a, sides_a), (above_b, below_b, sides_b))
-    ):
-        receive_rows(ids, near_rows(inbox, chips, part), far, part, above, below)
-        side[...] = receive_sides(ids, side_a, side_b, part).reshape(PZ, CX, CY)
-    halo_a = (above_a, below_a, sides_a)
-    halo_b = (above_b, below_b, sides_b)
 
     def arrived(pair):
         rows = []
@@ -353,9 +356,32 @@
         def source(z):
             return joined[0, z] + jnp.where(z == 0, deposit[...], 0.0)
 
+        near_above = parity == 1
+        for part, (above, below, side) in enumerate(
+            ((above_a, below_a, sides_a), (above_b, below_b, sides_b))
+        ):
+            row = near_row(inbox, chips, parity, part)
+            above[...] = jnp.where(near_above, row, 0.0)
+            below[...] = jnp.where(near_above, 0.0, row)
+            side[...] = receive_sides(ids, side_a, side_b, part).reshape(PZ, CX, CY)
+        halo_a = (above_a, below_a, sides_a)
+        halo_b = (above_b, below_b, sides_b)
         first = joined.at[1]
         heat_planes(heat, coeff, order, source, first, halo_a, halo_b)
-        send_edges(ids, (first,), near_out, far_out, side_a_out, side_b_out)
+        near_out[0] = edge_row(first, near_above)
+        scale = heat_dt / edge_row(order.at[0], far_top)
+        for part, x in enumerate((heat, coeff, first)):
+            far_out[part * PZ : (part + 1) * PZ] = edge_row(x, far_top)
+        far_out[3 * PZ : 4 * PZ] = scale
+        at = iota((PZ * CX, CY), 0) == iota((PZ * CX, CY), 1) * CX + jnp.where(far_top, 0, CX - 1)
+        lines = lines_of(ids, side_a, side_b, 0) + lines_of(ids, side_a, side_b, 1)
+        rows = iota((8, PZ * CX), 0)
+        corners = jnp.zeros((8, PZ * CX), F32)
+        for n, line in enumerate(lines):
+            corners = jnp.where(rows == n, jnp.broadcast_to(line, corners.shape), corners)
+        far_out[4 * PZ :] = pick_right(corners, ones_where(at))
+        send_columns(ids, first[...].reshape(PZ * CX, CY), side_a_out, side_b_out, 0)
+        send_columns(ids, scale, side_a_out, side_b_out, 1)
 
     @pl.when(grp == 1)
     def _():
@@ -376,29 +402,21 @@
                 layer = placed[:, i * CY : (i + 1) * CY].reshape(PZ // ZQ, CX, CY)
                 for q in range(PZ // ZQ):
                     warmth[ZQ * q + 2 * pair + i] = layer[q]
-        phase_planes(
-            order.at[0],
-            order.at[1],
-            coeff,
-            warmth,
-            joined.at[0],
-            joined.at[1],
-            halo_a,
-            halo_b,
-        )
+        for part in (0, 1):
+            far_out[part * PZ : (part + 1) * PZ] = edge_row(order.at[part], far_top)
 
 
 def second_kernel(
     ids,
     deposit,
     inbox,
-    far_k,
     side_a_k,
     side_b_k,
     near,
     far,
     side_a,
     side_b,
+    heat,
     coeff,
     order,
     joined,
@@ -412,60 +430,109 @@
     below_b,
     sides_b,
     result,
+    both,
     sems,
 ):
-    grp = ids[0]
-    joined_copy = pltpu.make_async_copy(joined, joined_out.at[0], sems.at[0])
-    joined_copy.start()
+    grp, parity = ids[0], ids[1] & 1
+    even = parity == 0
+    chips = inbox.shape[1] - 2 * PZ // 8
     parts = RESULT_PARTS
     size = PZ // parts
+    halo_a = (above_a, below_a, sides_a)
+    halo_b = (above_b, below_b, sides_b)
+
+    def place(above, below, near_values, far_values):
+        above[...] = jnp.where(even, far_values, near_values)
+        below[...] = jnp.where(even, near_values, far_values)
+
+    def write(source, target, n):
+        copy = pltpu.make_async_copy(source, target, sems.at[n])
+        copy.start()
+        return copy
 
     @pl.when(grp == 0)
     def _():
-        receive_rows(ids, [near[0, 0], near[1, 0]], far, 0, above_a, below_a)
+        copies = [write(joined.at[0], joined_out.at[0, 0], 0)]
+        t_far, k_far, partial, scale_far = [far[n * PZ : (n + 1) * PZ] for n in range(4)]
+        t_here, k_here = edge_row(heat, even), edge_row(coeff, even)
+        scale = heat_dt / edge_row(order.at[0], even)
+        crossing = harmonic(k_here, k_far) * (t_far - t_here)
+        first = both.at[0]
+        first[...] = joined[1]
+        for top, row in ((True, 0), (False, CX - 1)):
+            add = jnp.where(even == top, scale * crossing, 0.0)
+            first[:, row, :] = first[:, row, :] + add
+        copies.append(write(first, joined_out.at[0, 1], 1))
+        place(above_a, below_a, near[1 - parity, 0], partial - scale_far * crossing)
+        place(above_b, below_b, near_row(inbox, chips, parity, 1), k_far)
         sides_a[...] = receive_sides(ids, side_a, side_b, 0).reshape(PZ, CX, CY)
-        chips = inbox.shape[1] - 2 * PZ // 8
-        receive_rows(ids, near_rows(inbox, chips, 1), far_k, 1, above_b, below_b)
         sides_b[...] = receive_sides(ids, side_a_k, side_b_k, 1).reshape(PZ, CX, CY)
+        row = jnp.where(even, 0, CX - 1)
+        lane = iota((PZ, CY), 1)
+        add = jnp.zeros((PZ, CY), F32)
+        temps, conds = lines_of(ids, side_a_k, side_b_k, 0), lines_of(ids, side_a_k, side_b_k, 1)
+        scales = lines_of(ids, side_a, side_b, 1)
+        for n, end in enumerate((0, CY - 1)):
+            t, k = down(temps[n], row, CX), down(conds[n], row, CX)
+            corner = 4 * PZ + n
+            t_next, k_next = down(far[corner : corner + 1]), down(far[corner + 2 : corner + 3])
+            shared = 2.0 * k * k_next / jnp.maximum(k + k_next, 1e-6)
+            change = down(scales[n][:, :CY]) * shared * (t_next - t)
+            add = add + jnp.where(lane == end, change, 0.0)
+        for top, row in ((True, 0), (False, CX - 1)):
+            sides_a[:, row, :] = sides_a[:, row, :] + jnp.where(even == top, add, 0.0)
 
         def source(z):
             return joined[0, z] + jnp.where(z == 0, deposit[...], 0.0)
 
-        copies = []
         for n in range(parts):
-            heat_planes(
-                joined.at[1],
-                coeff,
-                order,
-                source,
-                result,
-                (above_a, below_a, sides_a),
-                (above_b, below_b, sides_b),
-                n * size,
-                (n + 1) * size,
-            )
-            planes = pl.ds(n * size, size)
-            copy = pltpu.make_async_copy(
-                result.at[planes], result_out.at[0, planes], sems.at[1 + n]
-            )
-            copy.start()
-            copies.append(copy)
+            begin, end = n * size, (n + 1) * size
+            heat_planes(first, coeff, order, source, result, halo_a, halo_b, begin, end)
+            planes = pl.ds(begin, size)
+            copies.append(write(result.at[planes], result_out.at[0, planes], 2 + n))
         for copy in copies:
             copy.wait()
 
     @pl.when(grp == 1)
     def _():
-        copy = pltpu.make_async_copy(warmth, result_out.at[0], sems.at[1])
-        copy.start()
-        copy.wait()
-
-    joined_copy.wait()
+        copies = [write(warmth, result_out.at[0], 0)]
+        for part, (above, below, side) in enumerate((halo_a, halo_b)):
+            far_values = far[part * PZ : (part + 1) * PZ]
+            place(above, below, near_row(inbox, chips, parity, part), far_values)
+            side[...] = receive_sides(ids, side_a_k, side_b_k, part).reshape(PZ, CX, CY)
+        for n in range(parts):
+            begin, end = n * size, (n + 1) * size
+            phase_planes(
+                order.at[0],
+                order.at[1],
+                coeff,
+                warmth,
+                both.at[0],
+                both.at[1],
+                halo_a,
+                halo_b,
+                begin,
+                end,
+            )
+            planes = pl.ds(begin, size)
+            copies.append(write(both.at[:, planes], joined_out.at[0, :, planes], 2 + n))
+        for copy in copies:
+            copy.wait()
 
 
 RESULT_PARTS = 4
 HBM = pl.BlockSpec(memory_space=pltpu.HBM)
 SMEM = pl.BlockSpec(memory_space=pltpu.SMEM)
 VMEM = pl.BlockSpec(memory_space=pltpu.VMEM)
+
+
+def located(kernel, slabs, cols):
+    def body(number, *refs):
+        n = number[0]
+        ids = lax.div(n, slabs * cols), lax.rem(lax.div(n, cols), slabs), lax.rem(n, cols)
+        kernel(ids, *refs)
+
+    return body
 
 
 def call(kernel, specs, outs, scratch=(), out_space=VMEM, limit=24 << 20):
@@ -498,7 +565,11 @@
     slabs, cols = lax.axis_size("slab"), lax.axis_size("col")
     chips = slabs // 2
     grp = lax.axis_index("grp")
-    ids = jnp.stack([grp, lax.axis_index("slab"), lax.axis_index("col")]).astype(jnp.int32)
+    number = lax.axis_index(("grp", "slab", "col")).reshape(1)
+
+    def place(kernel, *specs, **options):
+        return call(located(kernel, slabs, cols), *specs, **options)
+
     near_pairs = [[2 * i, 2 * i + 1] for i in range(chips)]
     same_core = [[2 * i + k for i in range(chips)] for k in range(2)]
     far_swap = swaps(range(1, slabs - 1, 2))
@@ -507,7 +578,7 @@
     owners, sources, laser = block_owner[0, :, :, 0], block_source[0], laser_cells[0]
 
     slab_table = pltpu.VMEM(owners.shape, jnp.int32)
-    outbox, deposit = call(
+    outbox, deposit = place(
         pack_kernel,
         [SMEM] + [HBM] * 4,
         [(chips, 8, CY), (CX, CY)],
@@ -519,43 +590,59 @@
             pltpu.SemaphoreType.DMA((4,)),
         ],
         limit=60 << 20,
-    )(ids, owners, sources, heat.reshape(PZ // ZQ, ZQ, CX, CY), laser)
-    crossed = lax.all_gather(outbox, "grp")
+    )(number, owners, sources, heat.reshape(PZ // ZQ, ZQ, CX, CY), laser)
+    moved = lax.all_to_all(
+        outbox, "slab", split_axis=0, concat_axis=0, tiled=True, axis_index_groups=same_core
+    )
+    crossed = lax.all_gather(moved, "grp")
     crossed = lax.dynamic_index_in_dim(crossed, 1 - grp, 0, keepdims=False)
-    moved = lax.all_to_all(
-        crossed, "slab", split_axis=0, concat_axis=0, tiled=True, axis_index_groups=same_core
+
+    rows, column, field = (2, PZ, CY), (2, PZ * CX), (PZ, CX, CY)
+    near, side_a, side_b = place(edges_kernel, [SMEM] + [VMEM] * 3, [rows, column, column])(
+        number, heat, conduct, orders
     )
-
-    def exchanged(far, side_a, side_b):
-        far = lax.ppermute(far, "slab", far_swap)
-        side_a = lax.ppermute(side_a, "col", side_a_swap)
-        side_b = lax.ppermute(side_b, "col", side_b_swap)
-        return far, side_a, side_b
-
-    rows, column = (2, PZ, CY), (12, PZ * CX)
-    near, *edges = call(
-        edges_kernel, [SMEM] + [VMEM] * 3, [rows, rows, column, column]
-    )(ids, heat, conduct, orders)
-    edges = exchanged(*edges)
+    side_a = lax.ppermute(side_a, "col", side_a_swap)
+    side_b = lax.ppermute(side_b, "col", side_b_swap)
     inbox = lax.all_gather(
-        jnp.concatenate([moved, near.reshape(-1, 8, CY)]), "slab", axis_index_groups=near_pairs
+        jnp.concatenate([crossed, near.reshape(-1, 8, CY)]), "slab", axis_index_groups=near_pairs
     )
-    row, column, field = (1, PZ, CY), (1, PZ * CX), (PZ, CX, CY)
-    joined, warmth, near_1, *edges_1 = call(
+    joined, warmth, near_1, far_1, side_a_1, side_b_1 = place(
         first_kernel,
-        [SMEM] + [VMEM] * 10,
-        [(2,) + field, field, row, row, column, column],
+        [SMEM] + [VMEM] * 9,
+        [(2,) + field, field, (1, PZ, CY), (4 * PZ + 8, CY), column, column],
         halo_scratch(),
-    )(ids, deposit, owners, sources, inbox, *edges, heat, conduct, orders)
-    edges_1 = exchanged(*edges_1)
+    )(number, deposit, owners, sources, inbox, side_a, side_b, heat, conduct, orders)
+    far_1 = lax.ppermute(far_1, "slab", far_swap)
+    side_a_1 = lax.ppermute(side_a_1, "col", side_a_swap)
+    side_b_1 = lax.ppermute(side_b_1, "col", side_b_swap)
     near_1 = lax.all_gather(near_1, "slab", axis_index_groups=near_pairs)
-    return call(
+    return place(
         second_kernel,
         [SMEM] + [VMEM] * 13,
         [(1,) + field, (1, 2) + field],
-        halo_scratch() + [pltpu.VMEM(field, F32), pltpu.SemaphoreType.DMA((1 + RESULT_PARTS,))],
+        halo_scratch()
+        + [
+            pltpu.VMEM(field, F32),
+            pltpu.VMEM((2,) + field, F32),
+            pltpu.SemaphoreType.DMA((2 + RESULT_PARTS,)),
+        ],
         HBM,
-    )(ids, deposit, inbox, *edges, near_1, *edges_1, conduct, orders, joined, warmth)
+    )(
+        number,
+        deposit,
+        inbox,
+        side_a,
+        side_b,
+        near_1,
+        far_1,
+        side_a_1,
+        side_b_1,
+        heat,
+        conduct,
+        orders,
+        joined,
+        warmth,
+    )
 
 
 def solution(mesh):

time: 59.5 us -> 54.5 us (0.916)
  the two profiles are of different devices: /device:TPU:34 before, /device:TPU:3 now
where the time goes in v4:
time: 54.5 us; the launch traced here: 54.1 us
  starting transfers between devices  30.4 us (56%)
  blocking collectives  11.3 us (21%)
  Pallas kernels  6.21 us (11%)
  waiting for transfers between devices  3.35 us (6%)
  local copies, waits for them, and re-layouts  1.94 us (4%)
  between operations  0.82 us (2%)
    all_to_all x1, starting transfers between devices, per_device(): lax.all_to_all(outbox, 'slab', split_axis=0, concat_axis=0, tiled=True, a...  15.7 us
    all_gather x1, blocking collectives, per_device(): lax.all_gather(jnp.concatenate([crossed, near.reshape(-1, 8, CY)]), 'slab...  5.02 us
    all_gather x1, blocking collectives, per_device(): crossed = lax.all_gather(moved, 'grp')  4.48 us
    ppermute x1, starting transfers between devices, per_device(): side_b = lax.ppermute(side_b, 'col', side_b_swap)  3.78 us
    ppermute x1, starting transfers between devices, per_device(): side_b_1 = lax.ppermute(side_b_1, 'col', side_b_swap)  3.78 us
    all_to_all x1, waiting for transfers between devices, per_device(): lax.all_to_all(outbox, 'slab', split_axis=0, concat_axis=0, tiled=True, a...  3.34 us
    ppermute x1, starting transfers between devices, per_device(): far_1 = lax.ppermute(far_1, 'slab', far_swap)  2.86 us
    ppermute x1, starting transfers between devices, per_device(): side_a = lax.ppermute(side_a, 'col', side_a_swap)  2.17 us
  transfers between devices with their start and end apart: 6, of which 1 were waited for; matrix products, arithmetic and copies ran while one was open for 0% of the time, Pallas kernels for 0%

profile of v4, /device:TPU:3, one launch (start us, length us, event | category | flops | bytes accessed | tf_op | source)
XLA Modules:
  0.0 54.1 jit_solution(17209173282134484197)
XLA Ops:
  0.6 0.0 copy-start
  0.6 2.0 %shard_map.77 = (f32[32,8,128]{2,1,0:T(8,128)}, f32[16,128]{1,0:T(8,128)}) custom-call(s32[1]{0:T(128)} %bitcast.number, s32[64,64]{1,0:T(8,128)} %bitcast.27, s32[64,64]{1,0:T(8,128)} %bitcast.29, f32[8,4,16,128]{3,2,1,0:T(8,128)} %bitcast.17, s32[1,32]{1,0:T(1,128)} %bitcast.33), custom_call_target="tpu_custom_call" | custom-call | tf_op jit(solution)/shard_map/pallas_call | solution.py:581
  2.7 15.7 %all-to-all-start = ((f32[32,8,128]{2,1,0:T(8,128)}), f32[32,8,128]{2,1,0:T(8,128)S(1)}, u32[]{:S(2)}, u32[]{:S(2)}) async-start(f32[32,8,128]{2,1,0:T(8,128)} %get-tuple-element.14), calls=%async_computation | async-start | bytes 262144 | tf_op jit(solution)/shard_map/all_to_all | solution.py:594
  18.4 0.0 copy-done
  18.4 0.0 copy-start.1
  18.4 0.9 %copy-done.1 = f32[1,32,16,128]{3,2,1,0:T(8,128)S(1)} copy-done((f32[1,32,16,128]{3,2,1,0:T(8,128)S(1)}, f32[1,32,16,128]{3,2,1,0:T(8,128)}, u32[]{:S(2)}) %copy-start.1) | copy-done | bytes 262168
  19.4 0.0 copy-start.3
  19.4 0.9 %copy-done.3 = f32[1,32,16,128]{3,2,1,0:T(8,128)S(1)} copy-done((f32[1,32,16,128]{3,2,1,0:T(8,128)S(1)}, f32[1,32,16,128]{3,2,1,0:T(8,128)}, u32[]{:S(2)}) %copy-start.3) | copy-done | bytes 262168
  20.3 0.3 shard_map.78
  20.6 2.2 %collective-permute-start = (f32[2,512]{1,0:T(2,128)S(1)}, f32[2,512]{1,0:T(2,128)S(1)}, u32[]{:S(2)}, u32[]{:S(2)}) collective-permute-start(f32[2,512]{1,0:T(2,128)S(1)} %get-tuple-element.16), channel_id=1, source_target_pairs={{0,1},{1,0},{2,3},{3,2},{4,5},{5,4},{6,7},{7,6},{8,9},{9,8},{10,11... | collective-permute-start | bytes 12296 | tf_op jit(solution)/shard_map/ppermute | solution.py:604
  22.8 3.8 %collective-permute-start.1 = (f32[2,512]{1,0:T(2,128)S(1)}, f32[2,512]{1,0:T(2,128)S(1)}, u32[]{:S(2)}, u32[]{:S(2)}) collective-permute-start(f32[2,512]{1,0:T(2,128)S(1)} %get-tuple-element.17), channel_id=1, source_target_pairs={{1,2},{2,1},{5,6},{6,5},{9,10},{10,9},{13,14},{14,13},{17,18},{18,... | collective-permute-start | bytes 12296 | tf_op jit(solution)/shard_map/ppermute | solution.py:605
  26.6 3.3 %all-to-all-done = f32[32,8,128]{2,1,0:T(8,128)S(1)} async-done(((f32[32,8,128]{2,1,0:T(8,128)}), f32[32,8,128]{2,1,0:T(8,128)S(1)}, u32[]{:S(2)}, u32[]{:S(2)}) %all-to-all-start) | async-done | bytes 131104 | tf_op jit(solution)/shard_map/all_to_all | solution.py:594
  29.9 4.5 %all-gather = f32[64,8,128]{2,1,0:T(8,128)S(1)} all-gather(f32[32,8,128]{2,1,0:T(8,128)S(1)} %all-to-all-done), channel_id=2, replica_groups=mesh['grp'=2,'slab'=64,'col'=4] {'grp'}, dimensions={0}, use_global_device_ids=true | all-gather | bytes 393216 | tf_op jit(solution)/shard_map/all_gather | solution.py:597
  34.4 0.0 copy-start.4
  34.4 0.0 copy-start.2
  34.4 0.0 copy-start.5
  34.5 0.0 copy-start.6
  34.5 0.0 copy-start.7
  34.5 5.0 %all-gather.1 = f32[80,8,128]{2,1,0:T(8,128)S(1)} all-gather(f32[40,8,128]{2,1,0:T(8,128)S(1)} %pad_maximum_fusion), channel_id=3, replica_groups={{0,4},{8,12},{16,20},{24,28},{32,36},{40,44},{48,52},{56,60},{64,68},{7..., dimensions={0}, use_global_device_ids=true | all-gather | bytes 491520 | tf_op jit(solution)/shard_map/all_gather | solution.py:606
  39.5 0.0 collective-permute-done.refs_4_.refs_2_
  39.5 0.0 collective-permute-done.1.refs_5_.refs_3_
  39.5 0.0 copy-done.4
  39.5 0.0 copy-done.2
  39.5 0.0 copy-done.5
  39.5 0.0 copy-done.6
  39.5 0.0 copy-done.7
  39.5 1.8 %shard_map.79 = (f32[2,32,16,128]{3,2,1,0:T(8,128)S(1)}, f32[32,16,128]{2,1,0:T(8,128)S(1)}, f32[1,32,128]{2,1,0:T(8,128)S(1)}, f32[136,128]{1,0:T(8,128)S(1)}, ...) custom-call(s32[1]{0:T(128)} %bitcast.number, f32[16,128]{1,0:T(8,128)S(1)} %copy-done.7, s32[64,64]{1,0:T(8,128)S(1)} %bitcast.28, ...), custom_call_target="tpu_custom_call" | custom-call | tf_op jit(solution)/shard_map/pallas_call | solution.py:609
  41.3 2.9 %collective-permute-start.2 = (f32[136,128]{1,0:T(8,128)S(1)}, f32[136,128]{1,0:T(8,128)S(1)}, u32[]{:S(2)}, u32[]{:S(2)}) collective-permute-start(f32[136,128]{1,0:T(8,128)S(1)} %get-tuple-element.19), channel_id=1, source_target_pairs={{4,8},{8,4},{12,16},{16,12},{20,24},{24,20},{28,32},{32,28},{36,40... | collective-permute-start | bytes 208904 | tf_op jit(solution)/shard_map/ppermute | solution.py:615
  44.2 2.2 %collective-permute-start.3 = (f32[2,512]{1,0:T(2,128)S(1)}, f32[2,512]{1,0:T(2,128)S(1)}, u32[]{:S(2)}, u32[]{:S(2)}) collective-permute-start(f32[2,512]{1,0:T(2,128)S(1)} %get-tuple-element.20), channel_id=1, source_target_pairs={{0,1},{1,0},{2,3},{3,2},{4,5},{5,4},{6,7},{7,6},{8,9},{9,8},{10,11... | collective-permute-start | bytes 12296 | tf_op jit(solution)/shard_map/ppermute | solution.py:616
  46.4 3.8 %collective-permute-start.4 = (f32[2,512]{1,0:T(2,128)S(1)}, f32[2,512]{1,0:T(2,128)S(1)}, u32[]{:S(2)}, u32[]{:S(2)}) collective-permute-start(f32[2,512]{1,0:T(2,128)S(1)} %get-tuple-element.21), channel_id=1, source_target_pairs={{1,2},{2,1},{5,6},{6,5},{9,10},{10,9},{13,14},{14,13},{17,18},{18,... | collective-permute-start | bytes 12296 | tf_op jit(solution)/shard_map/ppermute | solution.py:617
  50.2 1.8 %all-gather.2 = f32[2,32,128]{2,1,0:T(8,128)S(1)} all-gather(f32[1,32,128]{2,1,0:T(8,128)S(1)} %get-tuple-element.18), channel_id=4, replica_groups={{0,4},{8,12},{16,20},{24,28},{32,36},{40,44},{48,52},{56,60},{64,68},{7..., dimensions={0}, use_global_device_ids=true | all-gather | bytes 49152 | tf_op jit(solution)/shard_map/all_gather | solution.py:618
  52.0 0.0 collective-permute-done.3.refs_6_
  52.0 0.0 collective-permute-done.4.refs_7_
  52.0 0.0 collective-permute-done.2.refs_5_
  52.0 2.1 %shard_map.80 = (f32[1,32,16,128]{3,2,1,0:T(8,128)}, f32[1,2,32,16,128]{4,3,2,1,0:T(8,128)}) custom-call(s32[1]{0:T(128)} %bitcast.number, f32[16,128]{1,0:T(8,128)S(1)} %copy-done.7, f32[2,40,8,128]{3,2,1,0:T(8,128)S(1)} %bitcast.22, f32[2,512]{1,0:T(2,128)S(1)} %collective-permute-done.refs_4_.refs_2_, ...), custom_call_target="tpu_custom_call" | custom-call | tf_op jit(solution)/shard_map/pallas_call | solution.py:619
  (2 shorter events, 0.0 us)
Async XLA Ops:
  0.6 17.8 %copy-start = (f32[1,2,32,16,128]{4,3,2,1,0:T(8,128)S(1)}, f32[1,2,32,16,128]{4,3,2,1,0:T(8,128)}, u32[]{:S(2)}) copy-start(f32[1,2,32,16,128]{4,3,2,1,0:T(8,128)} %param.8) | copy-start | bytes 1572868
  2.7 27.2 %all-to-all-start = ((f32[32,8,128]{2,1,0:T(8,128)}), f32[32,8,128]{2,1,0:T(8,128)S(1)}, u32[]{:S(2)}, u32[]{:S(2)}) async-start(f32[32,8,128]{2,1,0:T(8,128)} %get-tuple-element.14), calls=%async_computation | async-start | bytes 262144 | tf_op jit(solution)/shard_map/all_to_all | solution.py:594
  18.4 1.0 %copy-start.1 = (f32[1,32,16,128]{3,2,1,0:T(8,128)S(1)}, f32[1,32,16,128]{3,2,1,0:T(8,128)}, u32[]{:S(2)}) copy-start(f32[1,32,16,128]{3,2,1,0:T(8,128)} %param.6) | copy-start | bytes 786436
  19.4 0.9 %copy-start.3 = (f32[1,32,16,128]{3,2,1,0:T(8,128)S(1)}, f32[1,32,16,128]{3,2,1,0:T(8,128)}, u32[]{:S(2)}) copy-start(f32[1,32,16,128]{3,2,1,0:T(8,128)} %param.7) | copy-start | bytes 786436
  20.6 18.9 %collective-permute-start = (f32[2,512]{1,0:T(2,128)S(1)}, f32[2,512]{1,0:T(2,128)S(1)}, u32[]{:S(2)}, u32[]{:S(2)}) collective-permute-start(f32[2,512]{1,0:T(2,128)S(1)} %get-tuple-element.16), channel_id=1, source_target_pairs={{0,1},{1,0},{2,3},{3,2},{4,5},{5,4},{6,7},{7,6},{8,9},{9,8},{10,11... | collective-permute-start | bytes 12296 | tf_op jit(solution)/shard_map/ppermute | solution.py:604
  22.8 16.7 %collective-permute-start.1 = (f32[2,512]{1,0:T(2,128)S(1)}, f32[2,512]{1,0:T(2,128)S(1)}, u32[]{:S(2)}, u32[]{:S(2)}) collective-permute-start(f32[2,512]{1,0:T(2,128)S(1)} %get-tuple-element.17), channel_id=1, source_target_pairs={{1,2},{2,1},{5,6},{6,5},{9,10},{10,9},{13,14},{14,13},{17,18},{18,... | collective-permute-start | bytes 12296 | tf_op jit(solution)/shard_map/ppermute | solution.py:605
  34.4 5.1 %copy-start.4 = (f32[1,32,16,128]{3,2,1,0:T(8,128)S(1)}, f32[1,32,16,128]{3,2,1,0:T(8,128)}, u32[]{:S(2)}) copy-start(f32[1,32,16,128]{3,2,1,0:T(8,128)} %param.7) | copy-start | bytes 786436
  34.4 5.1 %copy-start.2 = (f32[1,32,16,128]{3,2,1,0:T(8,128)S(1)}, f32[1,32,16,128]{3,2,1,0:T(8,128)}, u32[]{:S(2)}) copy-start(f32[1,32,16,128]{3,2,1,0:T(8,128)} %param.6) | copy-start | bytes 786436
  34.4 5.1 %copy-start.5 = (s32[1,64,64,1]{2,3,1,0:T(1,128)S(1)}, s32[1,64,64,1]{2,3,1,0:T(1,128)}, u32[]{:S(2)}) copy-start(s32[1,64,64,1]{2,3,1,0:T(1,128)} %param.9) | copy-start | bytes 49156
  34.5 5.1 %copy-start.6 = (s32[1,64,64]{2,1,0:T(8,128)S(1)}, s32[1,64,64]{2,1,0:T(8,128)}, u32[]{:S(2)}) copy-start(s32[1,64,64]{2,1,0:T(8,128)} %param.10) | copy-start | bytes 49156
  34.5 5.1 %copy-start.7 = (f32[16,128]{1,0:T(8,128)S(1)}, f32[16,128]{1,0:T(8,128)}, u32[]{:S(2)}) copy-start(f32[16,128]{1,0:T(8,128)} %get-tuple-element.13.refs_0_) | copy-start | bytes 24580
  41.3 10.7 %collective-permute-start.2 = (f32[136,128]{1,0:T(8,128)S(1)}, f32[136,128]{1,0:T(8,128)S(1)}, u32[]{:S(2)}, u32[]{:S(2)}) collective-permute-start(f32[136,128]{1,0:T(8,128)S(1)} %get-tuple-element.19), channel_id=1, source_target_pairs={{4,8},{8,4},{12,16},{16,12},{20,24},{24,20},{28,32},{32,28},{36,40... | collective-permute-start | bytes 208904 | tf_op jit(solution)/shard_map/ppermute | solution.py:615
  44.2 7.8 %collective-permute-start.3 = (f32[2,512]{1,0:T(2,128)S(1)}, f32[2,512]{1,0:T(2,128)S(1)}, u32[]{:S(2)}, u32[]{:S(2)}) collective-permute-start(f32[2,512]{1,0:T(2,128)S(1)} %get-tuple-element.20), channel_id=1, source_target_pairs={{0,1},{1,0},{2,3},{3,2},{4,5},{5,4},{6,7},{7,6},{8,9},{9,8},{10,11... | collective-permute-start | bytes 12296 | tf_op jit(solution)/shard_map/ppermute | solution.py:616
  46.4 5.6 %collective-permute-start.4 = (f32[2,512]{1,0:T(2,128)S(1)}, f32[2,512]{1,0:T(2,128)S(1)}, u32[]{:S(2)}, u32[]{:S(2)}) collective-permute-start(f32[2,512]{1,0:T(2,128)S(1)} %get-tuple-element.21), channel_id=1, source_target_pairs={{1,2},{2,1},{5,6},{6,5},{9,10},{10,9},{13,14},{14,13},{17,18},{18,... | collective-permute-start | bytes 12296 | tf_op jit(solution)/shard_map/ppermute | solution.py:617

commit v5 on v4

--- a/solution.py
+++ b/solution.py
@@ -128,7 +128,8 @@
 
     def store(result, pair):
         for block in range(4):
-            out[:, block * 2 + pair, :] = result[block * count : (block + 1) * count]
+            at = (block & 1) * 2 + pair
+            out[1 - grp, :, block >> 1, at, :] = result[block * count : (block + 1) * count]
 
     for n in (0, 1, 3):
         copies[n].wait()
@@ -217,11 +218,6 @@
     row, lane = iota((8, CY), 0), iota((8, CY), 1)
     place = ones_where(((row == 0) & (lane == 0)) | ((row == 1) & (lane == CY - 1)))
     return pick_right(both, place, ((0,), (0,)))
-
-
-def near_row(inbox, chips, parity, part):
-    start = chips + part * PZ // 8
-    return inbox[1 - parity, pl.ds(start, PZ // 8)].reshape(PZ, CY)
 
 
 def beside(v, above, below, sides):
@@ -303,6 +299,7 @@
     owners,
     sources,
     inbox,
+    near,
     side_a,
     side_b,
     heat,
@@ -324,19 +321,10 @@
     grp, slab = ids[0], ids[1]
     parity = slab & 1
     far_top = parity == 0
-    chips = owners.shape[0] // 2
 
     def arrived(pair):
-        rows = []
-        for core in (0, 1):
-            for slot in (0, 1):
-                at = 2 * slot + pair
-                rows.append(
-                    jnp.where(
-                        parity == 0, inbox[core, :chips, at, :], inbox[core, :chips, 4 + at, :]
-                    )
-                )
-        return jnp.concatenate(rows, axis=0)
+        blocks = [(side, 2 * slot + pair) for side in (0, 1) for slot in (0, 1)]
+        return jnp.concatenate([inbox[1 - grp, :, side, at, :] for side, at in blocks], axis=0)
 
     lane = iota((CY, CY), 1)
 
@@ -360,7 +348,7 @@
         for part, (above, below, side) in enumerate(
             ((above_a, below_a, sides_a), (above_b, below_b, sides_b))
         ):
-            row = near_row(inbox, chips, parity, part)
+            row = near[1 - parity, part]
             above[...] = jnp.where(near_above, row, 0.0)
             below[...] = jnp.where(near_above, 0.0, row)
             side[...] = receive_sides(ids, side_a, side_b, part).reshape(PZ, CX, CY)
@@ -409,7 +397,7 @@
 def second_kernel(
     ids,
     deposit,
-    inbox,
+    near_k,
     side_a_k,
     side_b_k,
     near,
@@ -435,7 +423,6 @@
 ):
     grp, parity = ids[0], ids[1] & 1
     even = parity == 0
-    chips = inbox.shape[1] - 2 * PZ // 8
     parts = RESULT_PARTS
     size = PZ // parts
     halo_a = (above_a, below_a, sides_a)
@@ -464,7 +451,7 @@
             first[:, row, :] = first[:, row, :] + add
         copies.append(write(first, joined_out.at[0, 1], 1))
         place(above_a, below_a, near[1 - parity, 0], partial - scale_far * crossing)
-        place(above_b, below_b, near_row(inbox, chips, parity, 1), k_far)
+        place(above_b, below_b, near_k[1 - parity, 1], k_far)
         sides_a[...] = receive_sides(ids, side_a, side_b, 0).reshape(PZ, CX, CY)
         sides_b[...] = receive_sides(ids, side_a_k, side_b_k, 1).reshape(PZ, CX, CY)
         row = jnp.where(even, 0, CX - 1)
@@ -498,7 +485,7 @@
         copies = [write(warmth, result_out.at[0], 0)]
         for part, (above, below, side) in enumerate((halo_a, halo_b)):
             far_values = far[part * PZ : (part + 1) * PZ]
-            place(above, below, near_row(inbox, chips, parity, part), far_values)
+            place(above, below, near_k[1 - parity, part], far_values)
             side[...] = receive_sides(ids, side_a_k, side_b_k, part).reshape(PZ, CX, CY)
         for n in range(parts):
             begin, end = n * size, (n + 1) * size
@@ -571,7 +558,6 @@
         return call(located(kernel, slabs, cols), *specs, **options)
 
     near_pairs = [[2 * i, 2 * i + 1] for i in range(chips)]
-    same_core = [[2 * i + k for i in range(chips)] for k in range(2)]
     far_swap = swaps(range(1, slabs - 1, 2))
     side_a_swap, side_b_swap = swaps(range(0, cols - 1, 2)), swaps(range(1, cols - 1, 2))
     heat, conduct, orders = heat_field[0], coeff[0], order[0]
@@ -581,7 +567,7 @@
     outbox, deposit = place(
         pack_kernel,
         [SMEM] + [HBM] * 4,
-        [(chips, 8, CY), (CX, CY)],
+        [(2, chips, 2, 4, CY), (CX, CY)],
         [
             slab_table,
             slab_table,
@@ -591,27 +577,22 @@
         ],
         limit=60 << 20,
     )(number, owners, sources, heat.reshape(PZ // ZQ, ZQ, CX, CY), laser)
-    moved = lax.all_to_all(
-        outbox, "slab", split_axis=0, concat_axis=0, tiled=True, axis_index_groups=same_core
-    )
-    crossed = lax.all_gather(moved, "grp")
-    crossed = lax.dynamic_index_in_dim(crossed, 1 - grp, 0, keepdims=False)
-
+    inbox = lax.all_to_all(
+        outbox.reshape(-1, 4, CY), ("grp", "slab"), split_axis=0, concat_axis=0, tiled=True
+    ).reshape(outbox.shape)
     rows, column, field = (2, PZ, CY), (2, PZ * CX), (PZ, CX, CY)
     near, side_a, side_b = place(edges_kernel, [SMEM] + [VMEM] * 3, [rows, column, column])(
         number, heat, conduct, orders
     )
     side_a = lax.ppermute(side_a, "col", side_a_swap)
     side_b = lax.ppermute(side_b, "col", side_b_swap)
-    inbox = lax.all_gather(
-        jnp.concatenate([crossed, near.reshape(-1, 8, CY)]), "slab", axis_index_groups=near_pairs
-    )
+    near = lax.all_gather(near, "slab", axis_index_groups=near_pairs)
     joined, warmth, near_1, far_1, side_a_1, side_b_1 = place(
         first_kernel,
-        [SMEM] + [VMEM] * 9,
+        [SMEM] + [VMEM] * 10,
         [(2,) + field, field, (1, PZ, CY), (4 * PZ + 8, CY), column, column],
         halo_scratch(),
-    )(number, deposit, owners, sources, inbox, side_a, side_b, heat, conduct, orders)
+    )(number, deposit, owners, sources, inbox, near, side_a, side_b, heat, conduct, orders)
     far_1 = lax.ppermute(far_1, "slab", far_swap)
     side_a_1 = lax.ppermute(side_a_1, "col", side_a_swap)
     side_b_1 = lax.ppermute(side_b_1, "col", side_b_swap)
@@ -630,7 +611,7 @@
     )(
         number,
         deposit,
-        inbox,
+        near,
         side_a,
         side_b,
         near_1,

time: 54.5 us -> 50.8 us (0.932)
  the two profiles are of different devices: /device:TPU:3 before, /device:TPU:19 now
where the time goes in v5:
time: 50.8 us; the launch traced here: 50.4 us
  starting transfers between devices  32.4 us (64%)
  Pallas kernels  6.28 us (12%)
  blocking collectives  5.34 us (11%)
  waiting for transfers between devices  4.69 us (9%)
  local copies, waits for them, and re-layouts  0.98 us (2%)
  between operations  0.78 us (2%)
    all_to_all x1, starting transfers between devices, per_device(): lax.all_to_all(outbox.reshape(-1, 4, CY), ('grp', 'slab'), split_axis=0,...  17.7 us
    all_to_all x1, waiting for transfers between devices, per_device(): lax.all_to_all(outbox.reshape(-1, 4, CY), ('grp', 'slab'), split_axis=0,...  4.67 us
    ppermute x1, starting transfers between devices, per_device(): side_b = lax.ppermute(side_b, 'col', side_b_swap)  3.78 us
    ppermute x1, starting transfers between devices, per_device(): side_b_1 = lax.ppermute(side_b_1, 'col', side_b_swap)  3.78 us
    all_gather x1, blocking collectives, per_device(): near_1 = lax.all_gather(near_1, 'slab', axis_index_groups=near_pairs)  2.78 us
    ppermute x1, starting transfers between devices, per_device(): far_1 = lax.ppermute(far_1, 'slab', far_swap)  2.75 us
    all_gather x1, blocking collectives, per_device(): near = lax.all_gather(near, 'slab', axis_index_groups=near_pairs)  2.56 us
    ppermute x1, starting transfers between devices, per_device(): side_a = lax.ppermute(side_a, 'col', side_a_swap)  2.17 us
  transfers between devices with their start and end apart: 6, of which 1 were waited for; matrix products, arithmetic and copies ran while one was open for 0% of the time, Pallas kernels for 1%

profile of v5, /device:TPU:19, one launch (start us, length us, event | category | flops | bytes accessed | tf_op | source)
XLA Modules:
  0.0 50.4 jit_solution(6387626784158392138)
XLA Ops:
  0.6 0.0 copy-start
  0.6 2.1 %shard_map.77 = (f32[2,32,2,4,128]{4,3,2,1,0:T(4,128)}, f32[16,128]{1,0:T(8,128)}) custom-call(s32[1]{0:T(128)} %bitcast.number, s32[64,64]{1,0:T(8,128)} %bitcast.26, s32[64,64]{1,0:T(8,128)} %bitcast.28, f32[8,4,16,128]{3,2,1,0:T(8,128)} %bitcast.15, s32[1,32]{1,0:T(1,128)} %bitcast.31), custom_call_target="tpu_custom_call" | custom-call | tf_op jit(solution)/shard_map/pallas_call | solution.py:567
  2.8 0.0 copy-start.1
  2.8 17.7 %all-to-all-start = ((f32[128,4,128]{2,1,0:T(4,128)}), f32[128,4,128]{2,1,0:T(4,128)S(1)}, u32[]{:S(2)}, u32[]{:S(2)}) async-start(f32[128,4,128]{2,1,0:T(4,128)} %bitcast.30), calls=%async_computation | async-start | bytes 524288 | tf_op jit(solution)/shard_map/all_to_all | solution.py:580
  20.5 0.0 copy-done
  20.5 0.0 copy-done.1
  20.5 0.0 copy-start.2
  20.5 0.9 %copy-done.2 = f32[1,32,16,128]{3,2,1,0:T(8,128)S(1)} copy-done((f32[1,32,16,128]{3,2,1,0:T(8,128)S(1)}, f32[1,32,16,128]{3,2,1,0:T(8,128)}, u32[]{:S(2)}) %copy-start.2) | copy-done | bytes 262168
  21.5 0.0 copy-start.3
  21.5 0.3 shard_map.78
  21.7 2.2 %collective-permute-start = (f32[2,512]{1,0:T(2,128)S(1)}, f32[2,512]{1,0:T(2,128)S(1)}, u32[]{:S(2)}, u32[]{:S(2)}) collective-permute-start(f32[2,512]{1,0:T(2,128)S(1)} %get-tuple-element.15), channel_id=1, source_target_pairs={{0,1},{1,0},{2,3},{3,2},{4,5},{5,4},{6,7},{7,6},{8,9},{9,8},{10,11... | collective-permute-start | bytes 12296 | tf_op jit(solution)/shard_map/ppermute | solution.py:587
  23.9 3.8 %collective-permute-start.1 = (f32[2,512]{1,0:T(2,128)S(1)}, f32[2,512]{1,0:T(2,128)S(1)}, u32[]{:S(2)}, u32[]{:S(2)}) collective-permute-start(f32[2,512]{1,0:T(2,128)S(1)} %get-tuple-element.16), channel_id=1, source_target_pairs={{1,2},{2,1},{5,6},{6,5},{9,10},{10,9},{13,14},{14,13},{17,18},{18,... | collective-permute-start | bytes 12296 | tf_op jit(solution)/shard_map/ppermute | solution.py:588
  27.7 0.0 copy-start.4
  27.7 0.0 copy-start.5
  27.7 0.0 copy-start.6
  27.7 2.6 %all-gather = f32[4,32,128]{2,1,0:T(8,128)S(1)} all-gather(f32[2,32,128]{2,1,0:T(8,128)S(1)} %get-tuple-element.14), channel_id=2, replica_groups={{0,4},{8,12},{16,20},{24,28},{32,36},{40,44},{48,52},{56,60},{64,68},{7..., dimensions={0}, use_global_device_ids=true | all-gather | bytes 98304 | tf_op jit(solution)/shard_map/all_gather | solution.py:589
  30.3 0.0 collective-permute-done.refs_5_.refs_2_
  30.3 0.0 collective-permute-done.1.refs_6_.refs_3_
  30.3 4.7 %all-to-all-done = f32[128,4,128]{2,1,0:T(4,128)S(1)} async-done(((f32[128,4,128]{2,1,0:T(4,128)}), f32[128,4,128]{2,1,0:T(4,128)S(1)}, u32[]{:S(2)}, u32[]{:S(2)}) %all-to-all-start) | async-done | bytes 262176 | tf_op jit(solution)/shard_map/all_to_all | solution.py:580
  35.0 0.0 copy-done.3
  35.0 0.0 copy-done.4
  35.0 0.0 copy-done.5
  35.0 0.0 copy-done.6
  35.0 1.8 %shard_map.79 = (f32[2,32,16,128]{3,2,1,0:T(8,128)S(1)}, f32[32,16,128]{2,1,0:T(8,128)S(1)}, f32[1,32,128]{2,1,0:T(8,128)S(1)}, f32[136,128]{1,0:T(8,128)S(1)}, ...) custom-call(s32[1]{0:T(128)} %bitcast.number, f32[16,128]{1,0:T(8,128)S(1)} %copy-done.6, s32[64,64]{1,0:T(8,128)S(1)} %bitcast.27, ...), custom_call_target="tpu_custom_call" | custom-call | tf_op jit(solution)/shard_map/pallas_call | solution.py:590
  36.8 2.7 %collective-permute-start.2 = (f32[136,128]{1,0:T(8,128)S(1)}, f32[136,128]{1,0:T(8,128)S(1)}, u32[]{:S(2)}, u32[]{:S(2)}) collective-permute-start(f32[136,128]{1,0:T(8,128)S(1)} %get-tuple-element.19), channel_id=1, source_target_pairs={{4,8},{8,4},{12,16},{16,12},{20,24},{24,20},{28,32},{32,28},{36,40... | collective-permute-start | bytes 208904 | tf_op jit(solution)/shard_map/ppermute | solution.py:596
  39.6 2.2 %collective-permute-start.3 = (f32[2,512]{1,0:T(2,128)S(1)}, f32[2,512]{1,0:T(2,128)S(1)}, u32[]{:S(2)}, u32[]{:S(2)}) collective-permute-start(f32[2,512]{1,0:T(2,128)S(1)} %get-tuple-element.20), channel_id=1, source_target_pairs={{0,1},{1,0},{2,3},{3,2},{4,5},{5,4},{6,7},{7,6},{8,9},{9,8},{10,11... | collective-permute-start | bytes 12296 | tf_op jit(solution)/shard_map/ppermute | solution.py:597
  41.7 3.8 %collective-permute-start.4 = (f32[2,512]{1,0:T(2,128)S(1)}, f32[2,512]{1,0:T(2,128)S(1)}, u32[]{:S(2)}, u32[]{:S(2)}) collective-permute-start(f32[2,512]{1,0:T(2,128)S(1)} %get-tuple-element.21), channel_id=1, source_target_pairs={{1,2},{2,1},{5,6},{6,5},{9,10},{10,9},{13,14},{14,13},{17,18},{18,... | collective-permute-start | bytes 12296 | tf_op jit(solution)/shard_map/ppermute | solution.py:598
  45.5 2.8 %all-gather.1 = f32[2,32,128]{2,1,0:T(8,128)S(1)} all-gather(f32[1,32,128]{2,1,0:T(8,128)S(1)} %get-tuple-element.18), channel_id=3, replica_groups={{0,4},{8,12},{16,20},{24,28},{32,36},{40,44},{48,52},{56,60},{64,68},{7..., dimensions={0}, use_global_device_ids=true | all-gather | bytes 49152 | tf_op jit(solution)/shard_map/all_gather | solution.py:599
  48.3 0.0 collective-permute-done.3.refs_6_
  48.3 0.0 collective-permute-done.4.refs_7_
  48.3 0.0 collective-permute-done.2.refs_5_
  48.3 2.1 %shard_map.80 = (f32[1,32,16,128]{3,2,1,0:T(8,128)}, f32[1,2,32,16,128]{4,3,2,1,0:T(8,128)}) custom-call(s32[1]{0:T(128)} %bitcast.number, f32[16,128]{1,0:T(8,128)S(1)} %copy-done.6, f32[2,2,32,128]{3,2,1,0:T(8,128)S(1)} %bitcast.24, f32[2,512]{1,0:T(2,128)S(1)} %collective-permute-done.refs_5_.refs_2_, ...), custom_call_target="tpu_custom_call" | custom-call | tf_op jit(solution)/shard_map/pallas_call | solution.py:600
Async XLA Ops:
  0.6 19.9 %copy-start = (f32[1,2,32,16,128]{4,3,2,1,0:T(8,128)S(1)}, f32[1,2,32,16,128]{4,3,2,1,0:T(8,128)}, u32[]{:S(2)}) copy-start(f32[1,2,32,16,128]{4,3,2,1,0:T(8,128)} %param.8) | copy-start | bytes 1572868
  2.8 17.7 %copy-start.1 = (f32[1,32,16,128]{3,2,1,0:T(8,128)S(1)}, f32[1,32,16,128]{3,2,1,0:T(8,128)}, u32[]{:S(2)}) copy-start(f32[1,32,16,128]{3,2,1,0:T(8,128)} %param.6) | copy-start | bytes 786436
  2.8 32.2 %all-to-all-start = ((f32[128,4,128]{2,1,0:T(4,128)}), f32[128,4,128]{2,1,0:T(4,128)S(1)}, u32[]{:S(2)}, u32[]{:S(2)}) async-start(f32[128,4,128]{2,1,0:T(4,128)} %bitcast.30), calls=%async_computation | async-start | bytes 524288 | tf_op jit(solution)/shard_map/all_to_all | solution.py:580
  20.5 1.0 %copy-start.2 = (f32[1,32,16,128]{3,2,1,0:T(8,128)S(1)}, f32[1,32,16,128]{3,2,1,0:T(8,128)}, u32[]{:S(2)}) copy-start(f32[1,32,16,128]{3,2,1,0:T(8,128)} %param.7) | copy-start | bytes 786436
  21.5 13.5 %copy-start.3 = (f32[1,32,16,128]{3,2,1,0:T(8,128)S(1)}, f32[1,32,16,128]{3,2,1,0:T(8,128)}, u32[]{:S(2)}) copy-start(f32[1,32,16,128]{3,2,1,0:T(8,128)} %param.7) | copy-start | bytes 786436
  21.7 8.6 %collective-permute-start = (f32[2,512]{1,0:T(2,128)S(1)}, f32[2,512]{1,0:T(2,128)S(1)}, u32[]{:S(2)}, u32[]{:S(2)}) collective-permute-start(f32[2,512]{1,0:T(2,128)S(1)} %get-tuple-element.15), channel_id=1, source_target_pairs={{0,1},{1,0},{2,3},{3,2},{4,5},{5,4},{6,7},{7,6},{8,9},{9,8},{10,11... | collective-permute-start | bytes 12296 | tf_op jit(solution)/shard_map/ppermute | solution.py:587
  23.9 6.4 %collective-permute-start.1 = (f32[2,512]{1,0:T(2,128)S(1)}, f32[2,512]{1,0:T(2,128)S(1)}, u32[]{:S(2)}, u32[]{:S(2)}) collective-permute-start(f32[2,512]{1,0:T(2,128)S(1)} %get-tuple-element.16), channel_id=1, source_target_pairs={{1,2},{2,1},{5,6},{6,5},{9,10},{10,9},{13,14},{14,13},{17,18},{18,... | collective-permute-start | bytes 12296 | tf_op jit(solution)/shard_map/ppermute | solution.py:588
  27.7 7.3 %copy-start.4 = (s32[1,64,64,1]{2,3,1,0:T(1,128)S(1)}, s32[1,64,64,1]{2,3,1,0:T(1,128)}, u32[]{:S(2)}) copy-start(s32[1,64,64,1]{2,3,1,0:T(1,128)} %param.9) | copy-start | bytes 49156
  27.7 7.3 %copy-start.5 = (s32[1,64,64]{2,1,0:T(8,128)S(1)}, s32[1,64,64]{2,1,0:T(8,128)}, u32[]{:S(2)}) copy-start(s32[1,64,64]{2,1,0:T(8,128)} %param.10) | copy-start | bytes 49156
  27.7 7.3 %copy-start.6 = (f32[16,128]{1,0:T(8,128)S(1)}, f32[16,128]{1,0:T(8,128)}, u32[]{:S(2)}) copy-start(f32[16,128]{1,0:T(8,128)} %get-tuple-element.13.refs_0_) | copy-start | bytes 24580
  36.8 11.5 %collective-permute-start.2 = (f32[136,128]{1,0:T(8,128)S(1)}, f32[136,128]{1,0:T(8,128)S(1)}, u32[]{:S(2)}, u32[]{:S(2)}) collective-permute-start(f32[136,128]{1,0:T(8,128)S(1)} %get-tuple-element.19), channel_id=1, source_target_pairs={{4,8},{8,4},{12,16},{16,12},{20,24},{24,20},{28,32},{32,28},{36,40... | collective-permute-start | bytes 208904 | tf_op jit(solution)/shard_map/ppermute | solution.py:596
  39.6 8.7 %collective-permute-start.3 = (f32[2,512]{1,0:T(2,128)S(1)}, f32[2,512]{1,0:T(2,128)S(1)}, u32[]{:S(2)}, u32[]{:S(2)}) collective-permute-start(f32[2,512]{1,0:T(2,128)S(1)} %get-tuple-element.20), channel_id=1, source_target_pairs={{0,1},{1,0},{2,3},{3,2},{4,5},{5,4},{6,7},{7,6},{8,9},{9,8},{10,11... | collective-permute-start | bytes 12296 | tf_op jit(solution)/shard_map/ppermute | solution.py:597
  41.7 6.6 %collective-permute-start.4 = (f32[2,512]{1,0:T(2,128)S(1)}, f32[2,512]{1,0:T(2,128)S(1)}, u32[]{:S(2)}, u32[]{:S(2)}) collective-permute-start(f32[2,512]{1,0:T(2,128)S(1)} %get-tuple-element.21), channel_id=1, source_target_pairs={{1,2},{2,1},{5,6},{6,5},{9,10},{10,9},{13,14},{14,13},{17,18},{18,... | collective-permute-start | bytes 12296 | tf_op jit(solution)/shard_map/ppermute | solution.py:598

commit v6 on v5

--- a/solution.py
+++ b/solution.py
@@ -234,7 +234,7 @@
 
 
 def heat_planes(
-    temp, cond, order, source, result, temp_halo, cond_halo, begin=0, end=PZ
+    temp, cond, order, source, result, temp_halo, cond_halo, begin=0, end=PZ, scales=None
 ):
     temp_above, temp_below, temp_sides = temp_halo
     cond_above, cond_below, cond_sides = cond_halo
@@ -250,6 +250,8 @@
         for v_next, k_next in zip(vs, ks):
             total = total + harmonic(k, k_next) * (v_next - v)
         result[z] = v + heat_dt * ((total + source(z)) / order[0, z] - order[1, z] * v)
+        if scales is not None:
+            scales[z] = heat_dt / order[0, z]
         return to_below
 
     if begin == 0:
@@ -293,13 +295,59 @@
     lax.fori_loop(begin, end, plane, 0, unroll=4)
 
 
-def first_kernel(
+def base_kernel(
     ids,
     deposit,
     owners,
     sources,
+    near,
+    side_a,
+    side_b,
+    heat,
+    coeff,
+    order,
+    table,
+    base,
+    scales,
+    above_a,
+    below_a,
+    sides_a,
+    above_b,
+    below_b,
+    sides_b,
+):
+    grp, slab = ids[0], ids[1]
+    near_above = slab & 1 == 1
+
+    @pl.when(grp == 0)
+    def _():
+        table[...] = plate_table(owners, sources, slab).astype(F32)
+        for part, (above, below, side) in enumerate(
+            ((above_a, below_a, sides_a), (above_b, below_b, sides_b))
+        ):
+            row = near[1 - (slab & 1), part]
+            above[...] = jnp.where(near_above, row, 0.0)
+            below[...] = jnp.where(near_above, 0.0, row)
+            side[...] = receive_sides(ids, side_a, side_b, part).reshape(PZ, CX, CY)
+
+        def source(z):
+            return jnp.where(z == 0, deposit[...], 0.0)
+
+        halo_a = (above_a, below_a, sides_a)
+        halo_b = (above_b, below_b, sides_b)
+        heat_planes(heat, coeff, order, source, base, halo_a, halo_b, scales=scales)
+
+    @pl.when(grp == 1)
+    def _():
+        table[:, :CY] = window_table(owners, slab).astype(F32)
+
+
+def first_kernel(
+    ids,
     inbox,
-    near,
+    table,
+    base,
+    scales,
     side_a,
     side_b,
     heat,
@@ -311,15 +359,8 @@
     far_out,
     side_a_out,
     side_b_out,
-    above_a,
-    below_a,
-    sides_a,
-    above_b,
-    below_b,
-    sides_b,
 ):
-    grp, slab = ids[0], ids[1]
-    parity = slab & 1
+    grp, parity = ids[0], ids[1] & 1
     far_top = parity == 0
 
     def arrived(pair):
@@ -330,34 +371,21 @@
 
     @pl.when(grp == 0)
     def _():
-        table = plate_table(owners, sources, slab)
+        picks = table[...].astype(BF16)
+        first = joined.at[1]
         for pair in (0, 1):
-            units = pick_left(table, arrived(pair), ((0,), (0,)))
+            units = pick_left(picks, arrived(pair), ((0,), (0,)))
             left, right = units[:CY], units[CY:]
             even = jnp.where(lane < HALF, left, pltpu.roll(right, HALF, 1))
             odd = jnp.where(lane < HALF, pltpu.roll(left, HALF, 1), right)
             for i, layer in ((2 * pair, even), (2 * pair + 1, odd)):
                 layer = layer.reshape(PZ // ZQ, CX, CY)
                 for q in range(PZ // ZQ):
-                    joined[0, ZQ * q + i] = layer[q]
-
-        def source(z):
-            return joined[0, z] + jnp.where(z == 0, deposit[...], 0.0)
-
-        near_above = parity == 1
-        for part, (above, below, side) in enumerate(
-            ((above_a, below_a, sides_a), (above_b, below_b, sides_b))
-        ):
-            row = near[1 - parity, part]
-            above[...] = jnp.where(near_above, row, 0.0)
-            below[...] = jnp.where(near_above, 0.0, row)
-            side[...] = receive_sides(ids, side_a, side_b, part).reshape(PZ, CX, CY)
-        halo_a = (above_a, below_a, sides_a)
-        halo_b = (above_b, below_b, sides_b)
-        first = joined.at[1]
-        heat_planes(heat, coeff, order, source, first, halo_a, halo_b)
-        near_out[0] = edge_row(first, near_above)
-        scale = heat_dt / edge_row(order.at[0], far_top)
+                    z = ZQ * q + i
+                    joined[0, z] = layer[q]
+                    first[z] = base[z] + scales[z] * layer[q]
+        near_out[0] = edge_row(first, jnp.logical_not(far_top))
+        scale = edge_row(scales, far_top)
         for part, x in enumerate((heat, coeff, first)):
             far_out[part * PZ : (part + 1) * PZ] = edge_row(x, far_top)
         far_out[3 * PZ : 4 * PZ] = scale
@@ -373,7 +401,7 @@
 
     @pl.when(grp == 1)
     def _():
-        table = window_table(owners, slab)
+        picks = table[:, :CY].astype(BF16)
         row = iota((CY, 2 * CY), 0)
         col = iota((CY, 2 * CY), 1)
         target = col & (CY - 1)
@@ -385,7 +413,7 @@
         )
         for pair in (0, 1):
             refined = pick_right(arrived(pair), fine)
-            placed = pick_left(table, refined, ((0,), (0,)))
+            placed = pick_left(picks, refined, ((0,), (0,)))
             for i in (0, 1):
                 layer = placed[:, i * CY : (i + 1) * CY].reshape(PZ // ZQ, CX, CY)
                 for q in range(PZ // ZQ):
@@ -587,12 +615,14 @@
     side_a = lax.ppermute(side_a, "col", side_a_swap)
     side_b = lax.ppermute(side_b, "col", side_b_swap)
     near = lax.all_gather(near, "slab", axis_index_groups=near_pairs)
+    table, base, scales = place(
+        base_kernel, [SMEM] + [VMEM] * 9, [(2 * slabs, 256), field, field], halo_scratch()
+    )(number, deposit, owners, sources, near, side_a, side_b, heat, conduct, orders)
     joined, warmth, near_1, far_1, side_a_1, side_b_1 = place(
         first_kernel,
-        [SMEM] + [VMEM] * 10,
+        [SMEM] + [VMEM] * 9,
         [(2,) + field, field, (1, PZ, CY), (4 * PZ + 8, CY), column, column],
-        halo_scratch(),
-    )(number, deposit, owners, sources, inbox, near, side_a, side_b, heat, conduct, orders)
+    )(number, inbox, table, base, scales, side_a, side_b, heat, conduct, orders)
     far_1 = lax.ppermute(far_1, "slab", far_swap)
     side_a_1 = lax.ppermute(side_a_1, "col", side_a_swap)
     side_b_1 = lax.ppermute(side_b_1, "col", side_b_swap)

time: 50.8 us -> 49.6 us (0.976)
  waiting for transfers between devices: 4.69 us -> 3.37 us
    all_to_all x1, waiting for transfers between devices: 4.67 us -> 3.35 us  [per_device(): lax.all_to_all(outbox.reshape(-1, 4, CY), ('grp', 'slab'), split_axis=0,...]
    pallas_call x1 -> x2, Pallas kernels: 1.81 us -> 1.89 us  [the longest x1 1.28 us: per_device(): place(base_kernel, [SMEM] + [VMEM] * 9, [(2 * slabs, 256), field, field],...]
  transfers between devices with their start and end apart: 6 -> 6, of which waited for: 1 -> 1; matrix products, arithmetic and copies ran while one was open for 0% -> 0% of each run, Pallas kernels for 1% -> 3%
where the time goes in v6:
time: 49.6 us; the launch traced here: 49.2 us
  starting transfers between devices  32.4 us (65%)
  Pallas kernels  6.36 us (13%)
  blocking collectives  5.33 us (11%)
  waiting for transfers between devices  3.37 us (7%)
  local copies, waits for them, and re-layouts  0.98 us (2%)
  between operations  0.81 us (2%)
    all_to_all x1, starting transfers between devices, per_device(): lax.all_to_all(outbox.reshape(-1, 4, CY), ('grp', 'slab'), split_axis=0,...  17.7 us
    ppermute x1, starting transfers between devices, per_device(): side_b = lax.ppermute(side_b, 'col', side_b_swap)  3.78 us
    ppermute x1, starting transfers between devices, per_device(): side_b_1 = lax.ppermute(side_b_1, 'col', side_b_swap)  3.78 us
    all_to_all x1, waiting for transfers between devices, per_device(): lax.all_to_all(outbox.reshape(-1, 4, CY), ('grp', 'slab'), split_axis=0,...  3.35 us
    all_gather x1, blocking collectives, per_device(): near_1 = lax.all_gather(near_1, 'slab', axis_index_groups=near_pairs)  2.77 us
    ppermute x1, starting transfers between devices, per_device(): far_1 = lax.ppermute(far_1, 'slab', far_swap)  2.75 us
    all_gather x1, blocking collectives, per_device(): near = lax.all_gather(near, 'slab', axis_index_groups=near_pairs)  2.56 us
    ppermute x1, starting transfers between devices, per_device(): side_a = lax.ppermute(side_a, 'col', side_a_swap)  2.17 us
  transfers between devices with their start and end apart: 6, of which 1 were waited for; matrix products, arithmetic and copies ran while one was open for 0% of the time, Pallas kernels for 3%

profile of v6, /device:TPU:19, one launch (start us, length us, event | category | flops | bytes accessed | tf_op | source)
XLA Modules:
  0.0 49.2 jit_solution(15717282079590541767)
XLA Ops:
  0.6 0.0 copy-start
  0.6 2.1 %shard_map.77 = (f32[2,32,2,4,128]{4,3,2,1,0:T(4,128)}, f32[16,128]{1,0:T(8,128)}) custom-call(s32[1]{0:T(128)} %bitcast.number, s32[64,64]{1,0:T(8,128)} %bitcast.29, s32[64,64]{1,0:T(8,128)} %bitcast.31, f32[8,4,16,128]{3,2,1,0:T(8,128)} %bitcast.16, s32[1,32]{1,0:T(1,128)} %bitcast.34), custom_call_target="tpu_custom_call" | custom-call | tf_op jit(solution)/shard_map/pallas_call | solution.py:595
  2.8 0.0 copy-start.1
  2.8 17.7 %all-to-all-start = ((f32[128,4,128]{2,1,0:T(4,128)}), f32[128,4,128]{2,1,0:T(4,128)S(1)}, u32[]{:S(2)}, u32[]{:S(2)}) async-start(f32[128,4,128]{2,1,0:T(4,128)} %bitcast.33), calls=%async_computation | async-start | bytes 524288 | tf_op jit(solution)/shard_map/all_to_all | solution.py:608
  20.5 0.0 copy-done
  20.5 0.0 copy-done.1
  20.5 0.0 copy-start.2
  20.5 0.9 %copy-done.2 = f32[1,32,16,128]{3,2,1,0:T(8,128)S(1)} copy-done((f32[1,32,16,128]{3,2,1,0:T(8,128)S(1)}, f32[1,32,16,128]{3,2,1,0:T(8,128)}, u32[]{:S(2)}) %copy-start.2) | copy-done | bytes 262168
  21.5 0.0 copy-start.3
  21.5 0.3 shard_map.78
  21.7 2.2 %collective-permute-start = (f32[2,512]{1,0:T(2,128)S(1)}, f32[2,512]{1,0:T(2,128)S(1)}, u32[]{:S(2)}, u32[]{:S(2)}) collective-permute-start(f32[2,512]{1,0:T(2,128)S(1)} %get-tuple-element.18), channel_id=1, source_target_pairs={{0,1},{1,0},{2,3},{3,2},{4,5},{5,4},{6,7},{7,6},{8,9},{9,8},{10,11... | collective-permute-start | bytes 12296 | tf_op jit(solution)/shard_map/ppermute | solution.py:615
  23.9 3.8 %collective-permute-start.1 = (f32[2,512]{1,0:T(2,128)S(1)}, f32[2,512]{1,0:T(2,128)S(1)}, u32[]{:S(2)}, u32[]{:S(2)}) collective-permute-start(f32[2,512]{1,0:T(2,128)S(1)} %get-tuple-element.19), channel_id=1, source_target_pairs={{1,2},{2,1},{5,6},{6,5},{9,10},{10,9},{13,14},{14,13},{17,18},{18,... | collective-permute-start | bytes 12296 | tf_op jit(solution)/shard_map/ppermute | solution.py:616
  27.7 0.0 copy-start.4
  27.7 0.0 copy-start.5
  27.7 0.0 copy-start.6
  27.7 2.6 %all-gather = f32[4,32,128]{2,1,0:T(8,128)S(1)} all-gather(f32[2,32,128]{2,1,0:T(8,128)S(1)} %get-tuple-element.17), channel_id=2, replica_groups={{0,4},{8,12},{16,20},{24,28},{32,36},{40,44},{48,52},{56,60},{64,68},{7..., dimensions={0}, use_global_device_ids=true | all-gather | bytes 98304 | tf_op jit(solution)/shard_map/all_gather | solution.py:617
  30.3 0.0 collective-permute-done.refs_4_.refs_2_
  30.3 0.0 collective-permute-done.1.refs_5_.refs_3_
  30.3 0.0 copy-done.3
  30.3 0.0 copy-done.4
  30.3 0.0 copy-done.5
  30.3 0.0 copy-done.6
  30.3 1.3 %shard_map.79 = (f32[128,256]{1,0:T(8,128)S(1)}, f32[32,16,128]{2,1,0:T(8,128)S(1)}, f32[32,16,128]{2,1,0:T(8,128)S(1)}) custom-call(s32[1]{0:T(128)} %bitcast.number, f32[16,128]{1,0:T(8,128)S(1)} %copy-done.6, s32[64,64]{1,0:T(8,128)S(1)} %bitcast.30, s32[64,64]{1,0:T(8,128)S(1)} %bitcast.32, f32[2,2,32,128]{3,2,1,0:T(8,128)S(1)} %bitcast.26, ...), custom_call_target="tpu_custom_call" | custom-call | tf_op jit(solution)/shard_map/pallas_call | solution.py:618
  31.6 3.4 %all-to-all-done = f32[128,4,128]{2,1,0:T(4,128)S(1)} async-done(((f32[128,4,128]{2,1,0:T(4,128)}), f32[128,4,128]{2,1,0:T(4,128)S(1)}, u32[]{:S(2)}, u32[]{:S(2)}) %all-to-all-start) | async-done | bytes 262176 | tf_op jit(solution)/shard_map/all_to_all | solution.py:608
  35.0 0.6 %shard_map.80 = (f32[2,32,16,128]{3,2,1,0:T(8,128)S(1)}, f32[32,16,128]{2,1,0:T(8,128)S(1)}, f32[1,32,128]{2,1,0:T(8,128)S(1)}, f32[136,128]{1,0:T(8,128)S(1)}, ...) custom-call(s32[1]{0:T(128)} %bitcast.number, f32[2,32,2,4,128]{4,3,2,1,0:T(4,128)S(1)} %bitcast.25, ...), custom_call_target="tpu_custom_call" | custom-call | tf_op jit(solution)/shard_map/pallas_call | solution.py:621
  35.6 2.8 %collective-permute-start.2 = (f32[136,128]{1,0:T(8,128)S(1)}, f32[136,128]{1,0:T(8,128)S(1)}, u32[]{:S(2)}, u32[]{:S(2)}) collective-permute-start(f32[136,128]{1,0:T(8,128)S(1)} %get-tuple-element.25), channel_id=1, source_target_pairs={{4,8},{8,4},{12,16},{16,12},{20,24},{24,20},{28,32},{32,28},{36,40... | collective-permute-start | bytes 208904 | tf_op jit(solution)/shard_map/ppermute | solution.py:626
  38.4 2.2 %collective-permute-start.3 = (f32[2,512]{1,0:T(2,128)S(1)}, f32[2,512]{1,0:T(2,128)S(1)}, u32[]{:S(2)}, u32[]{:S(2)}) collective-permute-start(f32[2,512]{1,0:T(2,128)S(1)} %get-tuple-element.26), channel_id=1, source_target_pairs={{0,1},{1,0},{2,3},{3,2},{4,5},{5,4},{6,7},{7,6},{8,9},{9,8},{10,11... | collective-permute-start | bytes 12296 | tf_op jit(solution)/shard_map/ppermute | solution.py:627
  40.5 3.8 %collective-permute-start.4 = (f32[2,512]{1,0:T(2,128)S(1)}, f32[2,512]{1,0:T(2,128)S(1)}, u32[]{:S(2)}, u32[]{:S(2)}) collective-permute-start(f32[2,512]{1,0:T(2,128)S(1)} %get-tuple-element.27), channel_id=1, source_target_pairs={{1,2},{2,1},{5,6},{6,5},{9,10},{10,9},{13,14},{14,13},{17,18},{18,... | collective-permute-start | bytes 12296 | tf_op jit(solution)/shard_map/ppermute | solution.py:628
  44.3 2.8 %all-gather.1 = f32[2,32,128]{2,1,0:T(8,128)S(1)} all-gather(f32[1,32,128]{2,1,0:T(8,128)S(1)} %get-tuple-element.24), channel_id=3, replica_groups={{0,4},{8,12},{16,20},{24,28},{32,36},{40,44},{48,52},{56,60},{64,68},{7..., dimensions={0}, use_global_device_ids=true | all-gather | bytes 49152 | tf_op jit(solution)/shard_map/all_gather | solution.py:629
  47.1 0.0 collective-permute-done.3.refs_6_
  47.1 0.0 collective-permute-done.4.refs_7_
  47.1 0.0 collective-permute-done.2.refs_5_
  47.1 2.1 %shard_map.81 = (f32[1,32,16,128]{3,2,1,0:T(8,128)}, f32[1,2,32,16,128]{4,3,2,1,0:T(8,128)}) custom-call(s32[1]{0:T(128)} %bitcast.number, f32[16,128]{1,0:T(8,128)S(1)} %copy-done.6, f32[2,2,32,128]{3,2,1,0:T(8,128)S(1)} %bitcast.27, f32[2,512]{1,0:T(2,128)S(1)} %collective-permute-done.refs_4_.refs_2_, ...), custom_call_target="tpu_custom_call" | custom-call | tf_op jit(solution)/shard_map/pallas_call | solution.py:630
Async XLA Ops:
  0.6 19.9 %copy-start = (f32[1,2,32,16,128]{4,3,2,1,0:T(8,128)S(1)}, f32[1,2,32,16,128]{4,3,2,1,0:T(8,128)}, u32[]{:S(2)}) copy-start(f32[1,2,32,16,128]{4,3,2,1,0:T(8,128)} %param.8) | copy-start | bytes 1572868
  2.8 17.7 %copy-start.1 = (f32[1,32,16,128]{3,2,1,0:T(8,128)S(1)}, f32[1,32,16,128]{3,2,1,0:T(8,128)}, u32[]{:S(2)}) copy-start(f32[1,32,16,128]{3,2,1,0:T(8,128)} %param.6) | copy-start | bytes 786436
  2.8 32.2 %all-to-all-start = ((f32[128,4,128]{2,1,0:T(4,128)}), f32[128,4,128]{2,1,0:T(4,128)S(1)}, u32[]{:S(2)}, u32[]{:S(2)}) async-start(f32[128,4,128]{2,1,0:T(4,128)} %bitcast.33), calls=%async_computation | async-start | bytes 524288 | tf_op jit(solution)/shard_map/all_to_all | solution.py:608
  20.5 1.0 %copy-start.2 = (f32[1,32,16,128]{3,2,1,0:T(8,128)S(1)}, f32[1,32,16,128]{3,2,1,0:T(8,128)}, u32[]{:S(2)}) copy-start(f32[1,32,16,128]{3,2,1,0:T(8,128)} %param.7) | copy-start | bytes 786436
  21.5 8.8 %copy-start.3 = (f32[1,32,16,128]{3,2,1,0:T(8,128)S(1)}, f32[1,32,16,128]{3,2,1,0:T(8,128)}, u32[]{:S(2)}) copy-start(f32[1,32,16,128]{3,2,1,0:T(8,128)} %param.7) | copy-start | bytes 786436
  21.7 8.6 %collective-permute-start = (f32[2,512]{1,0:T(2,128)S(1)}, f32[2,512]{1,0:T(2,128)S(1)}, u32[]{:S(2)}, u32[]{:S(2)}) collective-permute-start(f32[2,512]{1,0:T(2,128)S(1)} %get-tuple-element.18), channel_id=1, source_target_pairs={{0,1},{1,0},{2,3},{3,2},{4,5},{5,4},{6,7},{7,6},{8,9},{9,8},{10,11... | collective-permute-start | bytes 12296 | tf_op jit(solution)/shard_map/ppermute | solution.py:615
  23.9 6.4 %collective-permute-start.1 = (f32[2,512]{1,0:T(2,128)S(1)}, f32[2,512]{1,0:T(2,128)S(1)}, u32[]{:S(2)}, u32[]{:S(2)}) collective-permute-start(f32[2,512]{1,0:T(2,128)S(1)} %get-tuple-element.19), channel_id=1, source_target_pairs={{1,2},{2,1},{5,6},{6,5},{9,10},{10,9},{13,14},{14,13},{17,18},{18,... | collective-permute-start | bytes 12296 | tf_op jit(solution)/shard_map/ppermute | solution.py:616
  27.7 2.6 %copy-start.4 = (s32[1,64,64,1]{2,3,1,0:T(1,128)S(1)}, s32[1,64,64,1]{2,3,1,0:T(1,128)}, u32[]{:S(2)}) copy-start(s32[1,64,64,1]{2,3,1,0:T(1,128)} %param.9) | copy-start | bytes 49156
  27.7 2.6 %copy-start.5 = (s32[1,64,64]{2,1,0:T(8,128)S(1)}, s32[1,64,64]{2,1,0:T(8,128)}, u32[]{:S(2)}) copy-start(s32[1,64,64]{2,1,0:T(8,128)} %param.10) | copy-start | bytes 49156
  27.7 2.6 %copy-start.6 = (f32[16,128]{1,0:T(8,128)S(1)}, f32[16,128]{1,0:T(8,128)}, u32[]{:S(2)}) copy-start(f32[16,128]{1,0:T(8,128)} %get-tuple-element.16.refs_0_) | copy-start | bytes 24580
  35.6 11.5 %collective-permute-start.2 = (f32[136,128]{1,0:T(8,128)S(1)}, f32[136,128]{1,0:T(8,128)S(1)}, u32[]{:S(2)}, u32[]{:S(2)}) collective-permute-start(f32[136,128]{1,0:T(8,128)S(1)} %get-tuple-element.25), channel_id=1, source_target_pairs={{4,8},{8,4},{12,16},{16,12},{20,24},{24,20},{28,32},{32,28},{36,40... | collective-permute-start | bytes 208904 | tf_op jit(solution)/shard_map/ppermute | solution.py:626
  38.4 8.7 %collective-permute-start.3 = (f32[2,512]{1,0:T(2,128)S(1)}, f32[2,512]{1,0:T(2,128)S(1)}, u32[]{:S(2)}, u32[]{:S(2)}) collective-permute-start(f32[2,512]{1,0:T(2,128)S(1)} %get-tuple-element.26), channel_id=1, source_target_pairs={{0,1},{1,0},{2,3},{3,2},{4,5},{5,4},{6,7},{7,6},{8,9},{9,8},{10,11... | collective-permute-start | bytes 12296 | tf_op jit(solution)/shard_map/ppermute | solution.py:627
  40.5 6.6 %collective-permute-start.4 = (f32[2,512]{1,0:T(2,128)S(1)}, f32[2,512]{1,0:T(2,128)S(1)}, u32[]{:S(2)}, u32[]{:S(2)}) collective-permute-start(f32[2,512]{1,0:T(2,128)S(1)} %get-tuple-element.27), channel_id=1, source_target_pairs={{1,2},{2,1},{5,6},{6,5},{9,10},{10,9},{13,14},{14,13},{17,18},{18,... | collective-permute-start | bytes 12296 | tf_op jit(solution)/shard_map/ppermute | solution.py:628

commit v7 on v6

--- a/solution.py
+++ b/solution.py
@@ -233,9 +233,7 @@
     return 2.0 * center * beside_it / (center + beside_it)
 
 
-def heat_planes(
-    temp, cond, order, source, result, temp_halo, cond_halo, begin=0, end=PZ, scales=None
-):
+def base_planes(temp, cond, order, deposit, base, scales, shares, top, temp_halo, cond_halo):
     temp_above, temp_below, temp_sides = temp_halo
     cond_above, cond_below, cond_sides = cond_halo
 
@@ -245,20 +243,53 @@
         vs = beside(v, temp_above[one, :], temp_below[one, :], temp_sides[z])
         ks = beside(k, cond_above[one, :], cond_below[one, :], cond_sides[z])
         later = jnp.minimum(z + 1, PZ - 1)
-        to_below = harmonic(k, cond[later]) * (temp[later] - v)
+        shared = harmonic(k, cond[later])
+        shares[0, z] = shared
+        to_below = shared * (temp[later] - v)
         total = to_below - from_above
-        for v_next, k_next in zip(vs, ks):
-            total = total + harmonic(k, k_next) * (v_next - v)
-        result[z] = v + heat_dt * ((total + source(z)) / order[0, z] - order[1, z] * v)
-        if scales is not None:
-            scales[z] = heat_dt / order[0, z]
+        for n, (v_next, k_next) in enumerate(zip(vs, ks)):
+            shared = harmonic(k, k_next)
+            if n == 0:
+                top[one, :] = shared[:1]
+            else:
+                shares[n, z] = shared
+            total = total + shared * (v_next - v)
+        total = total + jnp.where(z == 0, deposit[...], 0.0)
+        base[z] = v + heat_dt * (total / order[0, z] - order[1, z] * v)
+        scales[z] = heat_dt / order[0, z]
+        return to_below
+
+    lax.fori_loop(0, PZ, plane, jnp.zeros((CX, CY), F32), unroll=4)
+
+
+def second_planes(
+    v, order, latent, deposit, shares, top, halo, far_row, far_flux, result, begin, end
+):
+    above, below, sides = halo
+    row = iota((CX, CY), 0)
+
+    def spread(line):
+        return jnp.broadcast_to(line, (CX, CY))
+
+    def plane(z, from_above):
+        center = v[z]
+        one = pl.ds(z, 1)
+        vs = beside(center, above[one, :], below[one, :], sides[z])
+        down = shares[1, z]
+        up = jnp.where(row == 0, spread(top[one, :]), pltpu.roll(down, 1, 0))
+        to_below = shares[0, z] * (v[jnp.minimum(z + 1, PZ - 1)] - center)
+        total = to_below - from_above
+        for shared, v_next in zip((up, down, shares[2, z], shares[3, z]), vs):
+            total = total + shared * (v_next - center)
+        total = total + jnp.where(row == far_row, spread(far_flux[one, :]), 0.0)
+        source = latent[z] + jnp.where(z == 0, deposit[...], 0.0)
+        result[z] = center + heat_dt * ((total + source) / order[0, z] - order[1, z] * center)
         return to_below
 
     if begin == 0:
         carry = jnp.zeros((CX, CY), F32)
     else:
-        before = begin - 1
-        carry = harmonic(cond[before], cond[begin]) * (temp[begin] - temp[before])
+        carry = shares[0, begin - 1] * (v[begin] - v[begin - 1])
     lax.fori_loop(begin, end, plane, carry, unroll=4)
 
 
@@ -309,6 +340,8 @@
     table,
     base,
     scales,
+    shares,
+    top,
     above_a,
     below_a,
     sides_a,
@@ -330,12 +363,11 @@
             below[...] = jnp.where(near_above, 0.0, row)
             side[...] = receive_sides(ids, side_a, side_b, part).reshape(PZ, CX, CY)
 
-        def source(z):
-            return jnp.where(z == 0, deposit[...], 0.0)
-
         halo_a = (above_a, below_a, sides_a)
         halo_b = (above_b, below_b, sides_b)
-        heat_planes(heat, coeff, order, source, base, halo_a, halo_b, scales=scales)
+        base_planes(
+            heat, coeff, order, deposit, base, scales, shares, top, halo_a, halo_b
+        )
 
     @pl.when(grp == 1)
     def _():
@@ -432,7 +464,9 @@
     far,
     side_a,
     side_b,
-    heat,
+    far_sent,
+    shares,
+    top,
     coeff,
     order,
     joined,
@@ -447,6 +481,7 @@
     sides_b,
     result,
     both,
+    far_flux,
     sems,
 ):
     grp, parity = ids[0], ids[1] & 1
@@ -469,19 +504,20 @@
     def _():
         copies = [write(joined.at[0], joined_out.at[0, 0], 0)]
         t_far, k_far, partial, scale_far = [far[n * PZ : (n + 1) * PZ] for n in range(4)]
-        t_here, k_here = edge_row(heat, even), edge_row(coeff, even)
-        scale = heat_dt / edge_row(order.at[0], even)
-        crossing = harmonic(k_here, k_far) * (t_far - t_here)
+        t_here, k_here = far_sent[:PZ], far_sent[PZ : 2 * PZ]
+        scale = far_sent[3 * PZ : 4 * PZ]
+        shared_far = harmonic(k_here, k_far)
+        crossing = shared_far * (t_far - t_here)
         first = both.at[0]
         first[...] = joined[1]
-        for top, row in ((True, 0), (False, CX - 1)):
-            add = jnp.where(even == top, scale * crossing, 0.0)
+        for at_top, row in ((True, 0), (False, CX - 1)):
+            add = jnp.where(even == at_top, scale * crossing, 0.0)
             first[:, row, :] = first[:, row, :] + add
         copies.append(write(first, joined_out.at[0, 1], 1))
-        place(above_a, below_a, near[1 - parity, 0], partial - scale_far * crossing)
-        place(above_b, below_b, near_k[1 - parity, 1], k_far)
+        far_first = partial - scale_far * crossing
+        far_flux[...] = shared_far * (far_first - edge_row(first, even))
+        place(above_a, below_a, near[1 - parity, 0], far_first)
         sides_a[...] = receive_sides(ids, side_a, side_b, 0).reshape(PZ, CX, CY)
-        sides_b[...] = receive_sides(ids, side_a_k, side_b_k, 1).reshape(PZ, CX, CY)
         row = jnp.where(even, 0, CX - 1)
         lane = iota((PZ, CY), 1)
         add = jnp.zeros((PZ, CY), F32)
@@ -494,15 +530,24 @@
             shared = 2.0 * k * k_next / jnp.maximum(k + k_next, 1e-6)
             change = down(scales[n][:, :CY]) * shared * (t_next - t)
             add = add + jnp.where(lane == end, change, 0.0)
-        for top, row in ((True, 0), (False, CX - 1)):
-            sides_a[:, row, :] = sides_a[:, row, :] + jnp.where(even == top, add, 0.0)
-
-        def source(z):
-            return joined[0, z] + jnp.where(z == 0, deposit[...], 0.0)
-
+        for at_top, edge in ((True, 0), (False, CX - 1)):
+            sides_a[:, edge, :] = sides_a[:, edge, :] + jnp.where(even == at_top, add, 0.0)
         for n in range(parts):
             begin, end = n * size, (n + 1) * size
-            heat_planes(first, coeff, order, source, result, halo_a, halo_b, begin, end)
+            second_planes(
+                first,
+                order,
+                joined.at[0],
+                deposit,
+                shares,
+                top,
+                halo_a,
+                row,
+                far_flux,
+                result,
+                begin,
+                end,
+            )
             planes = pl.ds(begin, size)
             copies.append(write(result.at[planes], result_out.at[0, planes], 2 + n))
         for copy in copies:
@@ -615,26 +660,31 @@
     side_a = lax.ppermute(side_a, "col", side_a_swap)
     side_b = lax.ppermute(side_b, "col", side_b_swap)
     near = lax.all_gather(near, "slab", axis_index_groups=near_pairs)
-    table, base, scales = place(
-        base_kernel, [SMEM] + [VMEM] * 9, [(2 * slabs, 256), field, field], halo_scratch()
+    table, base, scales, shares, top = place(
+        base_kernel,
+        [SMEM] + [VMEM] * 9,
+        [(2 * slabs, 256), field, field, (4,) + field, (PZ, CY)],
+        halo_scratch(),
     )(number, deposit, owners, sources, near, side_a, side_b, heat, conduct, orders)
     joined, warmth, near_1, far_1, side_a_1, side_b_1 = place(
         first_kernel,
         [SMEM] + [VMEM] * 9,
         [(2,) + field, field, (1, PZ, CY), (4 * PZ + 8, CY), column, column],
     )(number, inbox, table, base, scales, side_a, side_b, heat, conduct, orders)
+    far_sent = far_1
     far_1 = lax.ppermute(far_1, "slab", far_swap)
     side_a_1 = lax.ppermute(side_a_1, "col", side_a_swap)
     side_b_1 = lax.ppermute(side_b_1, "col", side_b_swap)
     near_1 = lax.all_gather(near_1, "slab", axis_index_groups=near_pairs)
     return place(
         second_kernel,
-        [SMEM] + [VMEM] * 13,
+        [SMEM] + [VMEM] * 15,
         [(1,) + field, (1, 2) + field],
         halo_scratch()
         + [
             pltpu.VMEM(field, F32),
             pltpu.VMEM((2,) + field, F32),
+            pltpu.VMEM((PZ, CY), F32),
             pltpu.SemaphoreType.DMA((2 + RESULT_PARTS,)),
         ],
         HBM,
@@ -648,7 +698,9 @@
         far_1,
         side_a_1,
         side_b_1,
-        heat,
+        far_sent,
+        shares,
+        top,
         conduct,
         orders,
         joined,

time: 49.6 us -> 49.3 us (level)
  the two profiles are of different devices: /device:TPU:19 before, /device:TPU:27 now
where the time goes in v7:
time: 49.3 us; the launch traced here: 48.9 us
  starting transfers between devices  32.2 us (65%)
  blocking collectives  6.49 us (13%)
  Pallas kernels  5.25 us (11%)
  waiting for transfers between devices  3.17 us (6%)
  local copies, waits for them, and re-layouts  0.98 us (2%)
  between operations  0.8 us (2%)
    all_to_all x1, starting transfers between devices, per_device(): lax.all_to_all(outbox.reshape(-1, 4, CY), ('grp', 'slab'), split_axis=0,...  17.8 us
    all_gather x1, blocking collectives, per_device(): near_1 = lax.all_gather(near_1, 'slab', axis_index_groups=near_pairs)  3.93 us
    ppermute x1, starting transfers between devices, per_device(): side_b_1 = lax.ppermute(side_b_1, 'col', side_b_swap)  3.78 us
    ppermute x1, starting transfers between devices, per_device(): side_b = lax.ppermute(side_b, 'col', side_b_swap)  3.78 us
    all_to_all x1, waiting for transfers between devices, per_device(): lax.all_to_all(outbox.reshape(-1, 4, CY), ('grp', 'slab'), split_axis=0,...  3.15 us
    all_gather x1, blocking collectives, per_device(): near = lax.all_gather(near, 'slab', axis_index_groups=near_pairs)  2.56 us
    ppermute x1, starting transfers between devices, per_device(): far_1 = lax.ppermute(far_1, 'slab', far_swap)  2.51 us
    pallas_call x1, Pallas kernels, per_device(): place(pack_kernel, [SMEM] + [HBM] * 4, [(2, chips, 2, 4, CY), (CX, CY)],...  2.32 us
  transfers between devices with their start and end apart: 6, of which 1 were waited for; matrix products, arithmetic and copies ran while one was open for 0% of the time, Pallas kernels for 1%

profile of v7, /device:TPU:27, one launch (start us, length us, event | category | flops | bytes accessed | tf_op | source)
XLA Modules:
  0.0 48.9 jit_solution(3784987944597485745)
XLA Ops:
  0.6 0.0 copy-start
  0.6 2.3 %shard_map.77 = (f32[2,32,2,4,128]{4,3,2,1,0:T(4,128)}, f32[16,128]{1,0:T(8,128)}) custom-call(s32[1]{0:T(128)} %bitcast.number, s32[64,64]{1,0:T(8,128)} %bitcast.28, s32[64,64]{1,0:T(8,128)} %bitcast.30, f32[8,4,16,128]{3,2,1,0:T(8,128)} %bitcast.16, s32[1,32]{1,0:T(1,128)} %bitcast.33), custom_call_target="tpu_custom_call" | custom-call | tf_op jit(solution)/shard_map/pallas_call | solution.py:640
  3.0 0.0 copy-start.1
  3.0 17.8 %all-to-all-start = ((f32[128,4,128]{2,1,0:T(4,128)}), f32[128,4,128]{2,1,0:T(4,128)S(1)}, u32[]{:S(2)}, u32[]{:S(2)}) async-start(f32[128,4,128]{2,1,0:T(4,128)} %bitcast.32), calls=%async_computation | async-start | bytes 524288 | tf_op jit(solution)/shard_map/all_to_all | solution.py:653
  20.8 0.0 copy-done
  20.8 0.0 copy-done.1
  20.8 0.0 copy-start.2
  20.8 0.9 %copy-done.2 = f32[1,32,16,128]{3,2,1,0:T(8,128)S(1)} copy-done((f32[1,32,16,128]{3,2,1,0:T(8,128)S(1)}, f32[1,32,16,128]{3,2,1,0:T(8,128)}, u32[]{:S(2)}) %copy-start.2) | copy-done | bytes 262168
  21.8 0.0 copy-start.3
  21.8 0.3 shard_map.78
  22.0 2.2 %collective-permute-start = (f32[2,512]{1,0:T(2,128)S(1)}, f32[2,512]{1,0:T(2,128)S(1)}, u32[]{:S(2)}, u32[]{:S(2)}) collective-permute-start(f32[2,512]{1,0:T(2,128)S(1)} %get-tuple-element.20), channel_id=1, source_target_pairs={{0,1},{1,0},{2,3},{3,2},{4,5},{5,4},{6,7},{7,6},{8,9},{9,8},{10,11... | collective-permute-start | bytes 12296 | tf_op jit(solution)/shard_map/ppermute | solution.py:660
  24.2 3.8 %collective-permute-start.1 = (f32[2,512]{1,0:T(2,128)S(1)}, f32[2,512]{1,0:T(2,128)S(1)}, u32[]{:S(2)}, u32[]{:S(2)}) collective-permute-start(f32[2,512]{1,0:T(2,128)S(1)} %get-tuple-element.21), channel_id=1, source_target_pairs={{1,2},{2,1},{5,6},{6,5},{9,10},{10,9},{13,14},{14,13},{17,18},{18,... | collective-permute-start | bytes 12296 | tf_op jit(solution)/shard_map/ppermute | solution.py:661
  28.0 0.0 copy-start.4
  28.0 0.0 copy-start.5
  28.0 0.0 copy-start.6
  28.0 2.6 %all-gather = f32[4,32,128]{2,1,0:T(8,128)S(1)} all-gather(f32[2,32,128]{2,1,0:T(8,128)S(1)} %get-tuple-element.19), channel_id=2, replica_groups={{0,4},{8,12},{16,20},{24,28},{32,36},{40,44},{48,52},{56,60},{64,68},{7..., dimensions={0}, use_global_device_ids=true | all-gather | bytes 98304 | tf_op jit(solution)/shard_map/all_gather | solution.py:662
  30.6 0.0 collective-permute-done.refs_4_.refs_2_
  30.6 0.0 collective-permute-done.1.refs_5_.refs_3_
  30.6 0.0 copy-done.3
  30.6 0.0 copy-done.4
  30.6 0.0 copy-done.5
  30.6 0.0 copy-done.6
  30.6 0.2 shard_map.79
  30.9 3.2 %all-to-all-done = f32[128,4,128]{2,1,0:T(4,128)S(1)} async-done(((f32[128,4,128]{2,1,0:T(4,128)}), f32[128,4,128]{2,1,0:T(4,128)S(1)}, u32[]{:S(2)}, u32[]{:S(2)}) %all-to-all-start) | async-done | bytes 262176 | tf_op jit(solution)/shard_map/all_to_all | solution.py:653
  34.0 0.5 shard_map.80
  34.5 2.5 %collective-permute-start.2 = (f32[136,128]{1,0:T(8,128)S(1)}, f32[136,128]{1,0:T(8,128)S(1)}, u32[]{:S(2)}, u32[]{:S(2)}) collective-permute-start(f32[136,128]{1,0:T(8,128)S(1)} %get-tuple-element.27.refs_8_), channel_id=1, source_target_pairs={{4,8},{8,4},{12,16},{16,12},{20,24},{24,20},{28,32},{32,28},{36,40... | collective-permute-start | bytes 208904 | tf_op jit(solution)/shard_map/ppermute | solution.py:675
  37.0 2.2 %collective-permute-start.3 = (f32[2,512]{1,0:T(2,128)S(1)}, f32[2,512]{1,0:T(2,128)S(1)}, u32[]{:S(2)}, u32[]{:S(2)}) collective-permute-start(f32[2,512]{1,0:T(2,128)S(1)} %get-tuple-element.28), channel_id=1, source_target_pairs={{0,1},{1,0},{2,3},{3,2},{4,5},{5,4},{6,7},{7,6},{8,9},{9,8},{10,11... | collective-permute-start | bytes 12296 | tf_op jit(solution)/shard_map/ppermute | solution.py:676
  39.2 3.8 %collective-permute-start.4 = (f32[2,512]{1,0:T(2,128)S(1)}, f32[2,512]{1,0:T(2,128)S(1)}, u32[]{:S(2)}, u32[]{:S(2)}) collective-permute-start(f32[2,512]{1,0:T(2,128)S(1)} %get-tuple-element.29), channel_id=1, source_target_pairs={{1,2},{2,1},{5,6},{6,5},{9,10},{10,9},{13,14},{14,13},{17,18},{18,... | collective-permute-start | bytes 12296 | tf_op jit(solution)/shard_map/ppermute | solution.py:677
  43.0 3.9 %all-gather.1 = f32[2,32,128]{2,1,0:T(8,128)S(1)} all-gather(f32[1,32,128]{2,1,0:T(8,128)S(1)} %get-tuple-element.26), channel_id=3, replica_groups={{0,4},{8,12},{16,20},{24,28},{32,36},{40,44},{48,52},{56,60},{64,68},{7..., dimensions={0}, use_global_device_ids=true | all-gather | bytes 49152 | tf_op jit(solution)/shard_map/all_gather | solution.py:678
  46.9 0.0 collective-permute-done.3.refs_6_
  46.9 0.0 collective-permute-done.4.refs_7_
  46.9 0.0 collective-permute-done.2.refs_5_
  46.9 2.0 %shard_map.81 = (f32[1,32,16,128]{3,2,1,0:T(8,128)}, f32[1,2,32,16,128]{4,3,2,1,0:T(8,128)}) custom-call(s32[1]{0:T(128)} %bitcast.number, f32[16,128]{1,0:T(8,128)S(1)} %copy-done.6, f32[2,2,32,128]{3,2,1,0:T(8,128)S(1)} %bitcast.26, f32[2,512]{1,0:T(2,128)S(1)} %collective-permute-done.refs_4_.refs_2_, ...), custom_call_target="tpu_custom_call" | custom-call | tf_op jit(solution)/shard_map/pallas_call | solution.py:679
Async XLA Ops:
  0.6 20.2 %copy-start = (f32[1,2,32,16,128]{4,3,2,1,0:T(8,128)S(1)}, f32[1,2,32,16,128]{4,3,2,1,0:T(8,128)}, u32[]{:S(2)}) copy-start(f32[1,2,32,16,128]{4,3,2,1,0:T(8,128)} %param.8) | copy-start | bytes 1572868
  3.0 17.8 %copy-start.1 = (f32[1,32,16,128]{3,2,1,0:T(8,128)S(1)}, f32[1,32,16,128]{3,2,1,0:T(8,128)}, u32[]{:S(2)}) copy-start(f32[1,32,16,128]{3,2,1,0:T(8,128)} %param.6) | copy-start | bytes 786436
  3.0 31.0 %all-to-all-start = ((f32[128,4,128]{2,1,0:T(4,128)}), f32[128,4,128]{2,1,0:T(4,128)S(1)}, u32[]{:S(2)}, u32[]{:S(2)}) async-start(f32[128,4,128]{2,1,0:T(4,128)} %bitcast.32), calls=%async_computation | async-start | bytes 524288 | tf_op jit(solution)/shard_map/all_to_all | solution.py:653
  20.8 1.0 %copy-start.2 = (f32[1,32,16,128]{3,2,1,0:T(8,128)S(1)}, f32[1,32,16,128]{3,2,1,0:T(8,128)}, u32[]{:S(2)}) copy-start(f32[1,32,16,128]{3,2,1,0:T(8,128)} %param.7) | copy-start | bytes 786436
  21.8 8.8 %copy-start.3 = (f32[1,32,16,128]{3,2,1,0:T(8,128)S(1)}, f32[1,32,16,128]{3,2,1,0:T(8,128)}, u32[]{:S(2)}) copy-start(f32[1,32,16,128]{3,2,1,0:T(8,128)} %param.7) | copy-start | bytes 786436
  22.0 8.6 %collective-permute-start = (f32[2,512]{1,0:T(2,128)S(1)}, f32[2,512]{1,0:T(2,128)S(1)}, u32[]{:S(2)}, u32[]{:S(2)}) collective-permute-start(f32[2,512]{1,0:T(2,128)S(1)} %get-tuple-element.20), channel_id=1, source_target_pairs={{0,1},{1,0},{2,3},{3,2},{4,5},{5,4},{6,7},{7,6},{8,9},{9,8},{10,11... | collective-permute-start | bytes 12296 | tf_op jit(solution)/shard_map/ppermute | solution.py:660
  24.2 6.4 %collective-permute-start.1 = (f32[2,512]{1,0:T(2,128)S(1)}, f32[2,512]{1,0:T(2,128)S(1)}, u32[]{:S(2)}, u32[]{:S(2)}) collective-permute-start(f32[2,512]{1,0:T(2,128)S(1)} %get-tuple-element.21), channel_id=1, source_target_pairs={{1,2},{2,1},{5,6},{6,5},{9,10},{10,9},{13,14},{14,13},{17,18},{18,... | collective-permute-start | bytes 12296 | tf_op jit(solution)/shard_map/ppermute | solution.py:661
  28.0 2.6 %copy-start.4 = (s32[1,64,64,1]{2,3,1,0:T(1,128)S(1)}, s32[1,64,64,1]{2,3,1,0:T(1,128)}, u32[]{:S(2)}) copy-start(s32[1,64,64,1]{2,3,1,0:T(1,128)} %param.9) | copy-start | bytes 49156
  28.0 2.6 %copy-start.5 = (s32[1,64,64]{2,1,0:T(8,128)S(1)}, s32[1,64,64]{2,1,0:T(8,128)}, u32[]{:S(2)}) copy-start(s32[1,64,64]{2,1,0:T(8,128)} %param.10) | copy-start | bytes 49156
  28.0 2.6 %copy-start.6 = (f32[16,128]{1,0:T(8,128)S(1)}, f32[16,128]{1,0:T(8,128)}, u32[]{:S(2)}) copy-start(f32[16,128]{1,0:T(8,128)} %get-tuple-element.18.refs_0_) | copy-start | bytes 24580
  34.5 12.4 %collective-permute-start.2 = (f32[136,128]{1,0:T(8,128)S(1)}, f32[136,128]{1,0:T(8,128)S(1)}, u32[]{:S(2)}, u32[]{:S(2)}) collective-permute-start(f32[136,128]{1,0:T(8,128)S(1)} %get-tuple-element.27.refs_8_), channel_id=1, source_target_pairs={{4,8},{8,4},{12,16},{16,12},{20,24},{24,20},{28,32},{32,28},{36,40... | collective-permute-start | bytes 208904 | tf_op jit(solution)/shard_map/ppermute | solution.py:675
  37.0 9.9 %collective-permute-start.3 = (f32[2,512]{1,0:T(2,128)S(1)}, f32[2,512]{1,0:T(2,128)S(1)}, u32[]{:S(2)}, u32[]{:S(2)}) collective-permute-start(f32[2,512]{1,0:T(2,128)S(1)} %get-tuple-element.28), channel_id=1, source_target_pairs={{0,1},{1,0},{2,3},{3,2},{4,5},{5,4},{6,7},{7,6},{8,9},{9,8},{10,11... | collective-permute-start | bytes 12296 | tf_op jit(solution)/shard_map/ppermute | solution.py:676
  39.2 7.7 %collective-permute-start.4 = (f32[2,512]{1,0:T(2,128)S(1)}, f32[2,512]{1,0:T(2,128)S(1)}, u32[]{:S(2)}, u32[]{:S(2)}) collective-permute-start(f32[2,512]{1,0:T(2,128)S(1)} %get-tuple-element.29), channel_id=1, source_target_pairs={{1,2},{2,1},{5,6},{6,5},{9,10},{10,9},{13,14},{14,13},{17,18},{18,... | collective-permute-start | bytes 12296 | tf_op jit(solution)/shard_map/ppermute | solution.py:677

commit v8 on v7

--- a/solution.py
+++ b/solution.py
@@ -259,7 +259,7 @@
         scales[z] = heat_dt / order[0, z]
         return to_below
 
-    lax.fori_loop(0, PZ, plane, jnp.zeros((CX, CY), F32), unroll=4)
+    lax.fori_loop(0, PZ, plane, jnp.zeros((CX, CY), F32), unroll=8)
 
 
 def second_planes(
@@ -290,7 +290,7 @@
         carry = jnp.zeros((CX, CY), F32)
     else:
         carry = shares[0, begin - 1] * (v[begin] - v[begin - 1])
-    lax.fori_loop(begin, end, plane, carry, unroll=4)
+    lax.fori_loop(begin, end, plane, carry, unroll=8)
 
 
 def phase_planes(
@@ -323,7 +323,7 @@
         new_sol[z] = s + phase_dt * spread_s - solute_reject * (p_new - p) * s
         return carry
 
-    lax.fori_loop(begin, end, plane, 0, unroll=4)
+    lax.fori_loop(begin, end, plane, 0, unroll=8)
 
 
 def base_kernel(

time: 49.3 us -> 48.8 us (0.990)
  the two profiles are of different devices: /device:TPU:27 before, /device:TPU:19 now
where the time goes in v8:
time: 48.8 us; the launch traced here: 48.4 us
  starting transfers between devices  32.4 us (66%)
  blocking collectives  5.33 us (11%)
  Pallas kernels  5.3 us (11%)
  waiting for transfers between devices  3.65 us (7%)
  local copies, waits for them, and re-layouts  0.98 us (2%)
  between operations  0.81 us (2%)
    all_to_all x1, starting transfers between devices, per_device(): lax.all_to_all(outbox.reshape(-1, 4, CY), ('grp', 'slab'), split_axis=0,...  17.7 us
    ppermute x1, starting transfers between devices, per_device(): side_b = lax.ppermute(side_b, 'col', side_b_swap)  3.78 us
    ppermute x1, starting transfers between devices, per_device(): side_b_1 = lax.ppermute(side_b_1, 'col', side_b_swap)  3.78 us
    all_to_all x1, waiting for transfers between devices, per_device(): lax.all_to_all(outbox.reshape(-1, 4, CY), ('grp', 'slab'), split_axis=0,...  3.64 us
    all_gather x1, blocking collectives, per_device(): near_1 = lax.all_gather(near_1, 'slab', axis_index_groups=near_pairs)  2.77 us
    ppermute x1, starting transfers between devices, per_device(): far_1 = lax.ppermute(far_1, 'slab', far_swap)  2.75 us
    all_gather x1, blocking collectives, per_device(): near = lax.all_gather(near, 'slab', axis_index_groups=near_pairs)  2.56 us
    ppermute x1, starting transfers between devices, per_device(): side_a = lax.ppermute(side_a, 'col', side_a_swap)  2.17 us
  transfers between devices with their start and end apart: 6, of which 1 were waited for; matrix products, arithmetic and copies ran while one was open for 0% of the time, Pallas kernels for 3%

profile of v8, /device:TPU:19, one launch (start us, length us, event | category | flops | bytes accessed | tf_op | source)
XLA Modules:
  0.0 48.4 jit_solution(17233285862946454537)
XLA Ops:
  0.6 0.0 copy-start
  0.6 2.1 %shard_map.77 = (f32[2,32,2,4,128]{4,3,2,1,0:T(4,128)}, f32[16,128]{1,0:T(8,128)}) custom-call(s32[1]{0:T(128)} %bitcast.number, s32[64,64]{1,0:T(8,128)} %bitcast.28, s32[64,64]{1,0:T(8,128)} %bitcast.30, f32[8,4,16,128]{3,2,1,0:T(8,128)} %bitcast.16, s32[1,32]{1,0:T(1,128)} %bitcast.33), custom_call_target="tpu_custom_call" | custom-call | tf_op jit(solution)/shard_map/pallas_call | solution.py:640
  2.8 0.0 copy-start.1
  2.8 17.7 %all-to-all-start = ((f32[128,4,128]{2,1,0:T(4,128)}), f32[128,4,128]{2,1,0:T(4,128)S(1)}, u32[]{:S(2)}, u32[]{:S(2)}) async-start(f32[128,4,128]{2,1,0:T(4,128)} %bitcast.32), calls=%async_computation | async-start | bytes 524288 | tf_op jit(solution)/shard_map/all_to_all | solution.py:653
  20.5 0.0 copy-done
  20.5 0.0 copy-done.1
  20.5 0.0 copy-start.2
  20.5 0.9 %copy-done.2 = f32[1,32,16,128]{3,2,1,0:T(8,128)S(1)} copy-done((f32[1,32,16,128]{3,2,1,0:T(8,128)S(1)}, f32[1,32,16,128]{3,2,1,0:T(8,128)}, u32[]{:S(2)}) %copy-start.2) | copy-done | bytes 262168
  21.5 0.0 copy-start.3
  21.5 0.3 shard_map.78
  21.7 2.2 %collective-permute-start = (f32[2,512]{1,0:T(2,128)S(1)}, f32[2,512]{1,0:T(2,128)S(1)}, u32[]{:S(2)}, u32[]{:S(2)}) collective-permute-start(f32[2,512]{1,0:T(2,128)S(1)} %get-tuple-element.20), channel_id=1, source_target_pairs={{0,1},{1,0},{2,3},{3,2},{4,5},{5,4},{6,7},{7,6},{8,9},{9,8},{10,11... | collective-permute-start | bytes 12296 | tf_op jit(solution)/shard_map/ppermute | solution.py:660
  23.9 3.8 %collective-permute-start.1 = (f32[2,512]{1,0:T(2,128)S(1)}, f32[2,512]{1,0:T(2,128)S(1)}, u32[]{:S(2)}, u32[]{:S(2)}) collective-permute-start(f32[2,512]{1,0:T(2,128)S(1)} %get-tuple-element.21), channel_id=1, source_target_pairs={{1,2},{2,1},{5,6},{6,5},{9,10},{10,9},{13,14},{14,13},{17,18},{18,... | collective-permute-start | bytes 12296 | tf_op jit(solution)/shard_map/ppermute | solution.py:661
  27.7 0.0 copy-start.4
  27.7 0.0 copy-start.5
  27.7 0.0 copy-start.6
  27.7 2.6 %all-gather = f32[4,32,128]{2,1,0:T(8,128)S(1)} all-gather(f32[2,32,128]{2,1,0:T(8,128)S(1)} %get-tuple-element.19), channel_id=2, replica_groups={{0,4},{8,12},{16,20},{24,28},{32,36},{40,44},{48,52},{56,60},{64,68},{7..., dimensions={0}, use_global_device_ids=true | all-gather | bytes 98304 | tf_op jit(solution)/shard_map/all_gather | solution.py:662
  30.3 0.0 collective-permute-done.refs_4_.refs_2_
  30.3 0.0 collective-permute-done.1.refs_5_.refs_3_
  30.3 0.0 copy-done.3
  30.3 0.0 copy-done.4
  30.3 0.0 copy-done.5
  30.3 0.0 copy-done.6
  30.3 1.0 %shard_map.79 = (f32[128,256]{1,0:T(8,128)S(1)}, f32[32,16,128]{2,1,0:T(8,128)S(1)}, f32[32,16,128]{2,1,0:T(8,128)S(1)}, f32[4,32,16,128]{3,2,1,0:T(8,128)S(1)}, f32[32,128]{1,0:T(8,128)S(1)}) custom-call(s32[1]{0:T(128)} %bitcast.number, f32[16,128]{1,0:T(8,128)S(1)} %copy-done.6, s32[64,64]{1,0:T(8,128)S(1)} %bitcast.29, s32[64,64]{1,0:T(8,128)S(1)} %bitcast.31, ...), custom_call_target="tpu_custom_call" | custom-call | tf_op jit(solution)/shard_map/pallas_call | solution.py:663
  31.3 3.6 %all-to-all-done = f32[128,4,128]{2,1,0:T(4,128)S(1)} async-done(((f32[128,4,128]{2,1,0:T(4,128)}), f32[128,4,128]{2,1,0:T(4,128)S(1)}, u32[]{:S(2)}, u32[]{:S(2)}) %all-to-all-start) | async-done | bytes 262176 | tf_op jit(solution)/shard_map/all_to_all | solution.py:653
  35.0 0.6 %shard_map.80 = (f32[2,32,16,128]{3,2,1,0:T(8,128)S(1)}, f32[32,16,128]{2,1,0:T(8,128)S(1)}, f32[1,32,128]{2,1,0:T(8,128)S(1)}, f32[136,128]{1,0:T(8,128)S(1)}, ...) custom-call(s32[1]{0:T(128)} %bitcast.number, f32[2,32,2,4,128]{4,3,2,1,0:T(4,128)S(1)} %bitcast.24, ...), custom_call_target="tpu_custom_call" | custom-call | tf_op jit(solution)/shard_map/pallas_call | solution.py:669
  35.6 2.8 %collective-permute-start.2 = (f32[136,128]{1,0:T(8,128)S(1)}, f32[136,128]{1,0:T(8,128)S(1)}, u32[]{:S(2)}, u32[]{:S(2)}) collective-permute-start(f32[136,128]{1,0:T(8,128)S(1)} %get-tuple-element.27.refs_8_), channel_id=1, source_target_pairs={{4,8},{8,4},{12,16},{16,12},{20,24},{24,20},{28,32},{32,28},{36,40... | collective-permute-start | bytes 208904 | tf_op jit(solution)/shard_map/ppermute | solution.py:675
  38.4 2.2 %collective-permute-start.3 = (f32[2,512]{1,0:T(2,128)S(1)}, f32[2,512]{1,0:T(2,128)S(1)}, u32[]{:S(2)}, u32[]{:S(2)}) collective-permute-start(f32[2,512]{1,0:T(2,128)S(1)} %get-tuple-element.28), channel_id=1, source_target_pairs={{0,1},{1,0},{2,3},{3,2},{4,5},{5,4},{6,7},{7,6},{8,9},{9,8},{10,11... | collective-permute-start | bytes 12296 | tf_op jit(solution)/shard_map/ppermute | solution.py:676
  40.5 3.8 %collective-permute-start.4 = (f32[2,512]{1,0:T(2,128)S(1)}, f32[2,512]{1,0:T(2,128)S(1)}, u32[]{:S(2)}, u32[]{:S(2)}) collective-permute-start(f32[2,512]{1,0:T(2,128)S(1)} %get-tuple-element.29), channel_id=1, source_target_pairs={{1,2},{2,1},{5,6},{6,5},{9,10},{10,9},{13,14},{14,13},{17,18},{18,... | collective-permute-start | bytes 12296 | tf_op jit(solution)/shard_map/ppermute | solution.py:677
  44.3 2.8 %all-gather.1 = f32[2,32,128]{2,1,0:T(8,128)S(1)} all-gather(f32[1,32,128]{2,1,0:T(8,128)S(1)} %get-tuple-element.26), channel_id=3, replica_groups={{0,4},{8,12},{16,20},{24,28},{32,36},{40,44},{48,52},{56,60},{64,68},{7..., dimensions={0}, use_global_device_ids=true | all-gather | bytes 49152 | tf_op jit(solution)/shard_map/all_gather | solution.py:678
  47.1 0.0 collective-permute-done.3.refs_6_
  47.1 0.0 collective-permute-done.4.refs_7_
  47.1 0.0 collective-permute-done.2.refs_5_
  47.1 1.3 %shard_map.81 = (f32[1,32,16,128]{3,2,1,0:T(8,128)}, f32[1,2,32,16,128]{4,3,2,1,0:T(8,128)}) custom-call(s32[1]{0:T(128)} %bitcast.number, f32[16,128]{1,0:T(8,128)S(1)} %copy-done.6, f32[2,2,32,128]{3,2,1,0:T(8,128)S(1)} %bitcast.26, f32[2,512]{1,0:T(2,128)S(1)} %collective-permute-done.refs_4_.refs_2_, ...), custom_call_target="tpu_custom_call" | custom-call | tf_op jit(solution)/shard_map/pallas_call | solution.py:679
Async XLA Ops:
  0.6 19.9 %copy-start = (f32[1,2,32,16,128]{4,3,2,1,0:T(8,128)S(1)}, f32[1,2,32,16,128]{4,3,2,1,0:T(8,128)}, u32[]{:S(2)}) copy-start(f32[1,2,32,16,128]{4,3,2,1,0:T(8,128)} %param.8) | copy-start | bytes 1572868
  2.8 17.7 %copy-start.1 = (f32[1,32,16,128]{3,2,1,0:T(8,128)S(1)}, f32[1,32,16,128]{3,2,1,0:T(8,128)}, u32[]{:S(2)}) copy-start(f32[1,32,16,128]{3,2,1,0:T(8,128)} %param.6) | copy-start | bytes 786436
  2.8 32.2 %all-to-all-start = ((f32[128,4,128]{2,1,0:T(4,128)}), f32[128,4,128]{2,1,0:T(4,128)S(1)}, u32[]{:S(2)}, u32[]{:S(2)}) async-start(f32[128,4,128]{2,1,0:T(4,128)} %bitcast.32), calls=%async_computation | async-start | bytes 524288 | tf_op jit(solution)/shard_map/all_to_all | solution.py:653
  20.5 1.0 %copy-start.2 = (f32[1,32,16,128]{3,2,1,0:T(8,128)S(1)}, f32[1,32,16,128]{3,2,1,0:T(8,128)}, u32[]{:S(2)}) copy-start(f32[1,32,16,128]{3,2,1,0:T(8,128)} %param.7) | copy-start | bytes 786436
  21.5 8.8 %copy-start.3 = (f32[1,32,16,128]{3,2,1,0:T(8,128)S(1)}, f32[1,32,16,128]{3,2,1,0:T(8,128)}, u32[]{:S(2)}) copy-start(f32[1,32,16,128]{3,2,1,0:T(8,128)} %param.7) | copy-start | bytes 786436
  21.7 8.6 %collective-permute-start = (f32[2,512]{1,0:T(2,128)S(1)}, f32[2,512]{1,0:T(2,128)S(1)}, u32[]{:S(2)}, u32[]{:S(2)}) collective-permute-start(f32[2,512]{1,0:T(2,128)S(1)} %get-tuple-element.20), channel_id=1, source_target_pairs={{0,1},{1,0},{2,3},{3,2},{4,5},{5,4},{6,7},{7,6},{8,9},{9,8},{10,11... | collective-permute-start | bytes 12296 | tf_op jit(solution)/shard_map/ppermute | solution.py:660
  23.9 6.4 %collective-permute-start.1 = (f32[2,512]{1,0:T(2,128)S(1)}, f32[2,512]{1,0:T(2,128)S(1)}, u32[]{:S(2)}, u32[]{:S(2)}) collective-permute-start(f32[2,512]{1,0:T(2,128)S(1)} %get-tuple-element.21), channel_id=1, source_target_pairs={{1,2},{2,1},{5,6},{6,5},{9,10},{10,9},{13,14},{14,13},{17,18},{18,... | collective-permute-start | bytes 12296 | tf_op jit(solution)/shard_map/ppermute | solution.py:661
  27.7 2.6 %copy-start.4 = (s32[1,64,64,1]{2,3,1,0:T(1,128)S(1)}, s32[1,64,64,1]{2,3,1,0:T(1,128)}, u32[]{:S(2)}) copy-start(s32[1,64,64,1]{2,3,1,0:T(1,128)} %param.9) | copy-start | bytes 49156
  27.7 2.6 %copy-start.5 = (s32[1,64,64]{2,1,0:T(8,128)S(1)}, s32[1,64,64]{2,1,0:T(8,128)}, u32[]{:S(2)}) copy-start(s32[1,64,64]{2,1,0:T(8,128)} %param.10) | copy-start | bytes 49156
  27.7 2.6 %copy-start.6 = (f32[16,128]{1,0:T(8,128)S(1)}, f32[16,128]{1,0:T(8,128)}, u32[]{:S(2)}) copy-start(f32[16,128]{1,0:T(8,128)} %get-tuple-element.18.refs_0_) | copy-start | bytes 24580
  35.6 11.5 %collective-permute-start.2 = (f32[136,128]{1,0:T(8,128)S(1)}, f32[136,128]{1,0:T(8,128)S(1)}, u32[]{:S(2)}, u32[]{:S(2)}) collective-permute-start(f32[136,128]{1,0:T(8,128)S(1)} %get-tuple-element.27.refs_8_), channel_id=1, source_target_pairs={{4,8},{8,4},{12,16},{16,12},{20,24},{24,20},{28,32},{32,28},{36,40... | collective-permute-start | bytes 208904 | tf_op jit(solution)/shard_map/ppermute | solution.py:675
  38.4 8.7 %collective-permute-start.3 = (f32[2,512]{1,0:T(2,128)S(1)}, f32[2,512]{1,0:T(2,128)S(1)}, u32[]{:S(2)}, u32[]{:S(2)}) collective-permute-start(f32[2,512]{1,0:T(2,128)S(1)} %get-tuple-element.28), channel_id=1, source_target_pairs={{0,1},{1,0},{2,3},{3,2},{4,5},{5,4},{6,7},{7,6},{8,9},{9,8},{10,11... | collective-permute-start | bytes 12296 | tf_op jit(solution)/shard_map/ppermute | solution.py:676
  40.5 6.6 %collective-permute-start.4 = (f32[2,512]{1,0:T(2,128)S(1)}, f32[2,512]{1,0:T(2,128)S(1)}, u32[]{:S(2)}, u32[]{:S(2)}) collective-permute-start(f32[2,512]{1,0:T(2,128)S(1)} %get-tuple-element.29), channel_id=1, source_target_pairs={{1,2},{2,1},{5,6},{6,5},{9,10},{10,9},{13,14},{14,13},{17,18},{18,... | collective-permute-start | bytes 12296 | tf_op jit(solution)/shard_map/ppermute | solution.py:677
